TPU v7x, 32 devices: a whole 2x2x4 slice. The times are simulated.
32 devices in a mesh: exp: 8 (over y, x, core), head: 4 (over z).
Axes of the slice: x: 2, y: 2, z: 4, core: 2. Of those that a mesh axis runs over, the one named last changes fastest.
Arguments:
- tokens: bfloat16 [13824, 768], P('exp'), may hold values from -6 to 6
- segments: int32 [24, 576], P('exp'), may hold values from 0 to 3, never falling along the last dimension, each value on 1 to 288 neighbouring positions
- live_mask: int32 [24, 576], P('exp'), may hold values 0 or 1
- routes: int32 [13824, 2], P('exp'), may hold values from 0 to 7, all different within a row
- priority: int32 [8, 1728], P('exp'), may hold values from 0 to 1727, each once within a row
- norm1_gain: bfloat16 [768], replicated, may hold values from 0.5 to 1.5
- norm1_bias: bfloat16 [768], replicated, may hold values from -1.1953125 to 1.1953125
- qkv_weight: bfloat16 [768, 3, 768], P(None, None, 'head'), may hold values from -0.21875 to 0.21875
- qv_bias: bfloat16 [2, 768], P(None, 'head'), may hold values from -1.796875 to 1.796875
- out_weight: bfloat16 [768, 768], P('head'), may hold values from -1 to 1
- out_bias: bfloat16 [768], replicated, may hold values from -1.1953125 to 1.1953125
- norm2_gain: bfloat16 [768], replicated, may hold values from 0.5 to 1.5
- norm2_bias: bfloat16 [768], replicated, may hold values from -1.1953125 to 1.1953125
- router: bfloat16 [768, 8], replicated, may hold values from -0.15625 to 0.15625
- up_weight: bfloat16 [8, 768, 3072], P('exp', None, 'head'), may hold values from -0.21875 to 0.21875
- up_bias: bfloat16 [8, 3072], P('exp', 'head'), may hold values from -1.796875 to 1.796875
- down_weight: bfloat16 [8, 3072, 768], P('exp', 'head'), may hold values from -1.75 to 1.75
- down_bias: bfloat16 [8, 768], P('exp', 'head'), may hold values from -6 to 6
- cotangent: bfloat16 [13824, 768], P('exp', 'head'), may hold values from -6 to 6
Outputs:
- block_out: bfloat16 [13824, 768], P('exp', 'head')
- grad_tokens: float32 [13824, 768], P('exp')
- grad_norm1_gain: float32 [768], replicated
- grad_norm1_bias: float32 [768], replicated
- grad_qkv_weight: float32 [768, 3, 768], P(None, None, 'head')
- grad_qv_bias: float32 [2, 768], P(None, 'head')
- grad_out_weight: float32 [768, 768], P('head')
- grad_out_bias: float32 [768], replicated
- grad_norm2_gain: float32 [768], replicated
- grad_norm2_bias: float32 [768], replicated
- grad_router: float32 [768, 8], replicated
- grad_up_weight: float32 [8, 768, 3072], P('exp', None, 'head')
- grad_up_bias: float32 [8, 3072], P('exp', 'head')
- grad_down_weight: float32 [8, 3072, 768], P('exp', 'head')
- grad_down_bias: float32 [8, 768], P('exp', 'head')
Inputs may be any that keep to these rules, and one draw needn't show every extreme that they name: `segments`: segment numbers never fall along a sequence; each segment has at most 288 patches. `routes`: the two experts of a patch differ. `priority`: each row is a permutation.
All inputs are finite; a program needn't handle non-finite values. No bound on the sum of `live_mask` on one device may be relied on, other than what follows from the above.
Results may differ from a plain program's by a relative error of at most 0.015.
Values may be sent and summed in bfloat16 or wider, within the bound.
A program may use at most 192 MiB of HBM per device.

v0:
```python
from functools import partial
import math

import jax
import jax.numpy as jnp
from jax import lax
from jax.sharding import PartitionSpec as P

HEAD_DIM = 64


EPSILON = 1e-06
NEGATIVE = -1e30
CONTRACT_FIRST = (((0,), (0,)), ((), ()))
CONTRACT_LAST = (((1,), (1,)), ((), ()))


def norm_rows(values, gain_row, shift_row):
    row_mean = jnp.mean(values, axis=-1, keepdims=True)
    centred = values - row_mean
    spread = jnp.mean(centred * centred, axis=-1, keepdims=True)
    return centred * lax.rsqrt(spread + EPSILON) * gain_row + shift_row


def masked_scores(query_rows, key_rows, seg_row, live_row, factor):
    scores = (
        jnp.einsum("qhd,khd->hqk", query_rows, key_rows, preferred_element_type=jnp.float32)
        * factor
    )
    same_segment = seg_row[:, None] == seg_row[None, :]
    diagonal = jnp.eye(seg_row.shape[0], dtype=bool)
    allowed = same_segment & ((live_row[None, :] > 0) | diagonal)
    return jnp.where(allowed[None], scores, NEGATIVE)


def attend_sequence(block_item, factor):
    query_rows, key_rows, value_rows, seg_row, live_row = block_item
    masked = masked_scores(query_rows, key_rows, seg_row, live_row, factor)
    largest = jnp.max(masked, axis=-1, keepdims=True)
    weights = jnp.exp(masked - largest)
    totals = jnp.sum(weights, axis=-1, keepdims=True)
    context = jnp.einsum(
        "hqk,khd->qhd",
        (weights / totals).astype(jnp.bfloat16),
        value_rows,
        preferred_element_type=jnp.float32,
    )
    return (context.astype(jnp.bfloat16), largest + jnp.log(totals))


def attend_backward(block_item, factor):
    query_rows, key_rows, value_rows, seg_row, live_row, context_grad, log_total = block_item
    masked = masked_scores(query_rows, key_rows, seg_row, live_row, factor)
    weights = jnp.exp(masked - log_total)
    value_grad = jnp.einsum(
        "hqk,qhd->khd",
        weights.astype(jnp.bfloat16),
        context_grad,
        preferred_element_type=jnp.float32,
    )
    weight_grad = jnp.einsum(
        "qhd,khd->hqk", context_grad, value_rows, preferred_element_type=jnp.float32
    )
    score_grad = (
        weights * (weight_grad - jnp.sum(weights * weight_grad, axis=-1, keepdims=True))
    ).astype(jnp.bfloat16)
    query_grad = (
        jnp.einsum("hqk,khd->qhd", score_grad, key_rows, preferred_element_type=jnp.float32)
        * factor
    )
    key_grad = (
        jnp.einsum("hqk,qhd->khd", score_grad, query_rows, preferred_element_type=jnp.float32)
        * factor
    )
    return (
        query_grad.astype(jnp.bfloat16),
        key_grad.astype(jnp.bfloat16),
        value_grad.astype(jnp.bfloat16),
    )


def slot_tables(routes, live_mask, priority, seqlen, experts, capacity):
    tok_count = routes.shape[0]
    expert_ids = jnp.arange(experts, dtype=jnp.int32)
    live_column = live_mask.reshape(tok_count, 1) > 0
    first_hot = ((routes[:, 0:1] == expert_ids[None, :]) & live_column).astype(jnp.bfloat16)
    second_hot = ((routes[:, 1:2] == expert_ids[None, :]) & live_column).astype(jnp.bfloat16)
    both_hot = jnp.concatenate([first_hot, second_hot], axis=1)
    rank_all = priority.reshape(tok_count)

    def count_block(rank_block):
        earlier = (rank_all[None, :] < rank_block[:, None]).astype(jnp.bfloat16)
        return jnp.dot(earlier, both_hot, preferred_element_type=jnp.float32)

    counts = lax.map(count_block, rank_all.reshape(-1, seqlen)).reshape(tok_count, 2 * experts)
    first_float = first_hot.astype(jnp.float32)
    second_float = second_hot.astype(jnp.float32)
    pos_first = jnp.sum(counts[:, :experts] * first_float, axis=1)
    pos_second = jnp.sum(counts[:, experts:] * second_float, axis=1) + jnp.sum(
        second_float * jnp.sum(first_float, axis=0)[None, :], axis=1
    )
    positions = jnp.stack([pos_first, pos_second], axis=1).astype(jnp.int32)
    kept_pairs = (positions < capacity) & live_column
    return (routes * capacity + positions, kept_pairs)


def slot_onehot(slot_ids, kept_rows, slot_count):
    return (
        (slot_ids[:, None] == jnp.arange(slot_count, dtype=jnp.int32)[None, :]) & kept_rows[:, None]
    ).astype(jnp.bfloat16)


def dispatch_rows(slot_ids, kept_pairs, rows, slot_count, seqlen):
    blocks = rows.shape[0] // seqlen

    def dispatch_add_block(running, block_item):
        ids_block, kept_block, rows_block = block_item
        onehot = slot_onehot(ids_block[:, 0], kept_block[:, 0], slot_count) + slot_onehot(
            ids_block[:, 1], kept_block[:, 1], slot_count
        )
        return (
            running
            + lax.dot_general(
                onehot, rows_block, CONTRACT_FIRST, preferred_element_type=jnp.float32
            ),
            None,
        )

    zeros_start = jnp.zeros((slot_count, rows.shape[1]), jnp.float32)
    running, ignored = lax.scan(
        dispatch_add_block,
        zeros_start,
        (
            slot_ids.reshape(blocks, seqlen, 2),
            kept_pairs.reshape(blocks, seqlen, 2),
            rows.reshape(blocks, seqlen, rows.shape[1]),
        ),
    )
    return running


def scatter_pairs(slot_ids, kept_pairs, pair_rows, slot_count, seqlen):
    blocks = pair_rows.shape[0] // seqlen

    def scatter_add_block(running, block_item):
        ids_block, kept_block, rows_block = block_item
        for route_pick in range(2):
            onehot = slot_onehot(ids_block[:, route_pick], kept_block[:, route_pick], slot_count)
            running = running + lax.dot_general(
                onehot,
                rows_block[:, route_pick],
                CONTRACT_FIRST,
                preferred_element_type=jnp.float32,
            )
        return (running, None)

    zeros_start = jnp.zeros((slot_count, pair_rows.shape[2]), jnp.float32)
    running, ignored = lax.scan(
        scatter_add_block,
        zeros_start,
        (
            slot_ids.reshape(blocks, seqlen, 2),
            kept_pairs.reshape(blocks, seqlen, 2),
            pair_rows.reshape(blocks, seqlen, 2, pair_rows.shape[2]),
        ),
    )
    return running


def select_rows(slot_ids, kept_pairs, buffer, seqlen):
    blocks = slot_ids.shape[0] // seqlen

    def pick_block(block_item):
        ids_block, kept_block = block_item
        first_rows = jnp.dot(
            slot_onehot(ids_block[:, 0], kept_block[:, 0], buffer.shape[0]),
            buffer,
            preferred_element_type=jnp.float32,
        )
        second_rows = jnp.dot(
            slot_onehot(ids_block[:, 1], kept_block[:, 1], buffer.shape[0]),
            buffer,
            preferred_element_type=jnp.float32,
        )
        return jnp.stack([first_rows, second_rows], axis=1)

    picked = lax.map(
        pick_block, (slot_ids.reshape(blocks, seqlen, 2), kept_pairs.reshape(blocks, seqlen, 2))
    )
    return picked.reshape(slot_ids.shape[0], 2, buffer.shape[1])


def body(
    tokens,
    segments,
    live_mask,
    routes,
    priority,
    norm1_gain,
    norm1_bias,
    qkv_weight,
    qv_bias,
    out_weight,
    out_bias,
    norm2_gain,
    norm2_bias,
    router,
    up_weight,
    up_bias,
    down_weight,
    down_bias,
    cotangent,
):
    tok_count, model_width = tokens.shape
    seq_count, seqlen = segments.shape
    experts = lax.axis_size("exp")
    head_parts = lax.axis_size("head")
    head_index = lax.axis_index("head")
    quarter = model_width // head_parts
    col_start = head_index * quarter
    capacity = (21 * tok_count + 10 * experts - 1) // (10 * experts)
    slot_count = experts * capacity
    local_width = qkv_weight.shape[2]
    head_count = local_width // HEAD_DIM
    factor = 1.0 / math.sqrt(HEAD_DIM)
    inputs = tokens.astype(jnp.float32)
    normed_one, norm_one_back = jax.vjp(
        norm_rows, inputs, norm1_gain.astype(jnp.float32), norm1_bias.astype(jnp.float32)
    )
    first_in = normed_one.astype(jnp.bfloat16)
    flat_qkv = qkv_weight.reshape(model_width, 3 * local_width)
    projected = jnp.dot(first_in, flat_qkv, preferred_element_type=jnp.float32).reshape(
        tok_count, 3, local_width
    )
    bias_rows = qv_bias.astype(jnp.float32)
    shape_four = (seq_count, seqlen, head_count, HEAD_DIM)
    query_rows = (projected[:, 0] + bias_rows[0]).astype(jnp.bfloat16).reshape(shape_four)
    key_rows = projected[:, 1].astype(jnp.bfloat16).reshape(shape_four)
    value_rows = (projected[:, 2] + bias_rows[1]).astype(jnp.bfloat16).reshape(shape_four)
    context, log_total = lax.map(
        partial(attend_sequence, factor=factor),
        (query_rows, key_rows, value_rows, segments, live_mask),
    )
    context_flat = context.reshape(tok_count, local_width)
    partial_out = jnp.dot(context_flat, out_weight, preferred_element_type=jnp.float32)
    residual = inputs + lax.psum(partial_out, "head") + out_bias.astype(jnp.float32)
    normed_two, norm_two_back = jax.vjp(
        norm_rows, residual, norm2_gain.astype(jnp.float32), norm2_bias.astype(jnp.float32)
    )
    second_in = normed_two.astype(jnp.bfloat16)
    logits = jnp.dot(second_in, router, preferred_element_type=jnp.float32)
    chances = jax.nn.softmax(logits, axis=-1)
    slot_ids, kept_pairs = slot_tables(routes, live_mask, priority, seqlen, experts, capacity)
    kept_float = kept_pairs.astype(jnp.float32)
    expert_ids = jnp.arange(experts, dtype=jnp.int32)
    chosen = (routes[:, :, None] == expert_ids[None, None, :]).astype(jnp.float32)
    gate_values = jnp.sum(chosen * chances[:, None, :], axis=2) * kept_float
    packed = dispatch_rows(slot_ids, kept_pairs, second_in, slot_count, seqlen).astype(jnp.bfloat16)
    arrived = lax.all_to_all(
        packed.reshape(experts, capacity, model_width),
        "exp",
        split_axis=0,
        concat_axis=0,
        tiled=True,
    )
    expert_rows = arrived.reshape(slot_count, model_width)
    pre_act = jnp.dot(expert_rows, up_weight[0], preferred_element_type=jnp.float32) + up_bias[
        0
    ].astype(jnp.float32)
    gelu_value, gelu_back = jax.vjp(jax.nn.gelu, pre_act)
    hidden = gelu_value.astype(jnp.bfloat16)
    partial_expert = jnp.dot(hidden, down_weight[0], preferred_element_type=jnp.float32)
    expert_cols = lax.psum_scatter(partial_expert, "head", scatter_dimension=1, tiled=True)
    expert_half = (expert_cols + down_bias[0].astype(jnp.float32)).astype(jnp.bfloat16)
    returned = lax.all_to_all(
        expert_half.reshape(experts, capacity, quarter),
        "exp",
        split_axis=0,
        concat_axis=0,
        tiled=True,
    )
    picked = select_rows(slot_ids, kept_pairs, returned.reshape(slot_count, quarter), seqlen)
    moe_cols = jnp.sum(gate_values[:, :, None] * picked, axis=1)
    block_out = (lax.dynamic_slice_in_dim(residual, col_start, quarter, 1) + moe_cols).astype(
        jnp.bfloat16
    )
    out_grad = cotangent.astype(jnp.float32)
    pair_grad = (gate_values[:, :, None] * out_grad[:, None, :]).astype(jnp.bfloat16)
    slot_grad = scatter_pairs(slot_ids, kept_pairs, pair_grad, slot_count, seqlen).astype(
        jnp.bfloat16
    )
    grad_rows = lax.all_to_all(
        slot_grad.reshape(experts, capacity, quarter),
        "exp",
        split_axis=0,
        concat_axis=0,
        tiled=True,
    ).reshape(slot_count, quarter)
    grad_down_bias = jnp.sum(grad_rows, axis=0, dtype=jnp.float32)[None]
    grad_full = lax.all_gather(grad_rows, "head", axis=1, tiled=True)
    grad_down_weight = lax.dot_general(
        hidden, grad_full, CONTRACT_FIRST, preferred_element_type=jnp.float32
    )[None]
    hidden_grad = lax.dot_general(
        grad_full, down_weight[0], CONTRACT_LAST, preferred_element_type=jnp.float32
    )
    pre_grad = gelu_back(hidden_grad)[0].astype(jnp.bfloat16)
    grad_up_weight = lax.dot_general(
        expert_rows, pre_grad, CONTRACT_FIRST, preferred_element_type=jnp.float32
    )[None]
    grad_up_bias = jnp.sum(pre_grad, axis=0, dtype=jnp.float32)[None]
    rows_grad = lax.dot_general(
        pre_grad, up_weight[0], CONTRACT_LAST, preferred_element_type=jnp.float32
    )
    rows_columns = lax.psum_scatter(rows_grad, "head", scatter_dimension=1, tiled=True).astype(
        jnp.bfloat16
    )
    home_grad = lax.all_to_all(
        rows_columns.reshape(experts, capacity, quarter),
        "exp",
        split_axis=0,
        concat_axis=0,
        tiled=True,
    )
    back_pair = select_rows(
        slot_ids, kept_pairs, home_grad.reshape(slot_count, quarter), seqlen
    ).astype(jnp.bfloat16)
    picked_half = picked.astype(jnp.bfloat16)
    first_back, second_back, first_out, second_out, out_full = (
        lax.all_gather(back_pair[:, 0], "head", axis=1, tiled=True),
        lax.all_gather(back_pair[:, 1], "head", axis=1, tiled=True),
        lax.all_gather(picked_half[:, 0], "head", axis=1, tiled=True),
        lax.all_gather(picked_half[:, 1], "head", axis=1, tiled=True),
        lax.all_gather(cotangent, "head", axis=1, tiled=True),
    )
    out_full_float = out_full.astype(jnp.float32)
    gate_grad = jnp.stack(
        [
            jnp.sum(first_out.astype(jnp.float32) * out_full_float, axis=1),
            jnp.sum(second_out.astype(jnp.float32) * out_full_float, axis=1),
        ],
        axis=1,
    )
    route_grad = jnp.sum(chosen * (gate_grad * kept_float)[:, :, None], axis=1)
    logit_grad = (
        chances * (route_grad - jnp.sum(chances * route_grad, axis=1, keepdims=True))
    ).astype(jnp.bfloat16)
    grad_router = lax.dot_general(
        second_in, logit_grad, CONTRACT_FIRST, preferred_element_type=jnp.float32
    )
    normed_two_grad = (
        first_back.astype(jnp.float32)
        + second_back.astype(jnp.float32)
        + lax.dot_general(logit_grad, router, CONTRACT_LAST, preferred_element_type=jnp.float32)
    )
    residual_norm, grad_norm2_gain, grad_norm2_bias = norm_two_back(normed_two_grad)
    residual_grad = out_full_float + residual_norm
    grad_out_bias = jnp.sum(residual_grad, axis=0)
    residual_half = residual_grad.astype(jnp.bfloat16)
    grad_out_weight = lax.dot_general(
        context_flat, residual_half, CONTRACT_FIRST, preferred_element_type=jnp.float32
    )
    context_grad = (
        lax.dot_general(
            residual_half, out_weight, CONTRACT_LAST, preferred_element_type=jnp.float32
        )
        .astype(jnp.bfloat16)
        .reshape(shape_four)
    )
    query_grad, key_grad, value_grad = lax.map(
        partial(attend_backward, factor=factor),
        (query_rows, key_rows, value_rows, segments, live_mask, context_grad, log_total),
    )
    query_flat = query_grad.reshape(tok_count, local_width)
    value_flat = value_grad.reshape(tok_count, local_width)
    qkv_grad = jnp.stack(
        [query_flat, key_grad.reshape(tok_count, local_width), value_flat], axis=1
    ).reshape(tok_count, 3 * local_width)
    grad_qkv_weight = lax.dot_general(
        first_in, qkv_grad, CONTRACT_FIRST, preferred_element_type=jnp.float32
    ).reshape(model_width, 3, local_width)
    grad_qv_bias = jnp.stack(
        [
            jnp.sum(query_flat, axis=0, dtype=jnp.float32),
            jnp.sum(value_flat, axis=0, dtype=jnp.float32),
        ],
        axis=0,
    )
    normed_one_grad = lax.psum(
        lax.dot_general(qkv_grad, flat_qkv, CONTRACT_LAST, preferred_element_type=jnp.float32),
        "head",
    )
    inputs_norm, grad_norm1_gain, grad_norm1_bias = norm_one_back(normed_one_grad)
    grad_tokens = residual_grad + inputs_norm
    summed = lax.psum(
        (
            grad_norm1_gain,
            grad_norm1_bias,
            grad_qkv_weight,
            grad_qv_bias,
            grad_out_weight,
            grad_out_bias,
            grad_norm2_gain,
            grad_norm2_bias,
            grad_router,
        ),
        "exp",
    )
    return (
        block_out,
        grad_tokens,
        summed[0],
        summed[1],
        summed[2],
        summed[3],
        summed[4],
        summed[5],
        summed[6],
        summed[7],
        summed[8],
        grad_up_weight,
        grad_up_bias,
        grad_down_weight,
        grad_down_bias,
    )


def solution(mesh):
    in_specs = (
        P("exp", None),
        P("exp", None),
        P("exp", None),
        P("exp", None),
        P("exp", None),
        P(),
        P(),
        P(None, None, "head"),
        P(None, "head"),
        P("head", None),
        P(),
        P(),
        P(),
        P(),
        P("exp", None, "head"),
        P("exp", "head"),
        P("exp", "head", None),
        P("exp", "head"),
        P("exp", "head"),
    )
    out_specs = (
        P("exp", "head"),
        P("exp", None),
        P(),
        P(),
        P(None, None, "head"),
        P(None, "head"),
        P("head", None),
        P(),
        P(),
        P(),
        P(),
        P("exp", None, "head"),
        P("exp", "head"),
        P("exp", "head", None),
        P("exp", "head"),
    )
    return jax.shard_map(body, mesh=mesh, in_specs=in_specs, out_specs=out_specs, check_vma=False)
```

profile of v0, /device:TPU:0, one launch (start us, length us, event | category | flops | bytes accessed | tf_op | source)
XLA Modules:
  0.0 1701.9 jit_solution(8506605268477176976)
XLA Ops:
  28.6 18.8 %while.85 = (s32[]{:T(128)}, bf16[3,576,3,64]{1,3,2,0:T(8,128)(2,1)S(1)}, f32[3,3,576,1]{2,1,3,0:T(4,128)}, bf16[3,576,3,64]{1,3,2,0:T(8,128)(2,1)}, s32[3,576]{...) while((s32[]{:T(128)}, ...), condition=%wide.region_5.6_spmd.clone, body=%wide.region_2.5_spmd.sunk.clone | while | flops 268184448 | bytes 14848477 | solution.py:240
  63.9 186.1 %all-reduce.6.cloned.1.call-done = f32[1728,768]{1,0:T(8,128)} async-done(((f32[1728,768]{1,0:T(8,128)}), f32[1728,768]{1,0:T(8,128)}) %all-reduce.6.cloned.1.call-update) | async-done | bytes 5308432 | tf_op jit(solution)/shard_map/psum | solution.py:246
  257.4 42.5 %while.90 = (s32[]{:T(128)}, f32[3632,768]{1,0:T(8,128)}, s32[3,576,2]{1,2,0:T(2,128)S(1)}, pred[3,576,2]{1,2,0:T(4,128)(4,1)S(1)}, bf16[3,576,768]{2,1,0:T(8,128)(2,1)}) while((s32[]{:T(128)}, f32[3632,768]{1,0:T(8,128)}, s32[3,576,2]{1,2,0:T(2,128)S(1)}, pred[3,576,2]{1,2,0:T(4,128)(4,1)S(1)}, ...), condition=%wide.region_19.20_spmd.clone.clone, body=%wide.region_18.19_spmd.clone.sunk.clone | while | flops 3239860224 | bytes 23229132 | solution.py:130
  269.4 15.2 select_add_fusion.3
  284.7 15.2 select_add_fusion.3
  316.8 64.1 %all-to-all-done = bf16[8,454,768]{2,1,0:T(8,128)(2,1)} async-done(((bf16[8,454,768]{2,1,0:T(8,128)(2,1)}), bf16[8,454,768]{2,1,0:T(8,128)(2,1)}, u32[]{:S(2)}, u32[]{:S(2)}) %all-to-all-start) | async-done | bytes 5578784 | tf_op jit(solution)/shard_map/all_to_all | solution.py:259
  406.1 189.5 %reduce-scatter.3.cloned.1.call-done = f32[3632,192]{0,1:T(8,128)} async-done(((f32[3632,768]{0,1:T(8,128)}), f32[3632,192]{0,1:T(8,128)}) %reduce-scatter.3.cloned.1.call-update) | async-done | bytes 2789392 | tf_op jit(solution)/shard_map/reduce_scatter | solution.py:273
  610.2 20.2 %all-to-all-done.1 = bf16[8,454,192]{1,2,0:T(8,128)(2,1)} async-done(((bf16[8,454,192]{1,2,0:T(8,128)(2,1)}), bf16[8,454,192]{1,2,0:T(8,128)(2,1)}, u32[]{:S(2)}, u32[]{:S(2)}) %all-to-all-start.1) | async-done | bytes 1394720 | tf_op jit(solution)/shard_map/all_to_all | solution.py:275
  635.8 23.1 %while.87 = (s32[]{:T(128)}, f32[3,576,2,192]{1,3,2,0:T(8,128)}, s32[3,576,2]{1,2,0:T(2,128)S(1)}, pred[3,576,2]{1,2,0:T(4,128)(4,1)S(1)}, bf16[3632,192]{1,0:T(8,128)(2,1)}) while((s32[]{:T(128)}, f32[3,576,2,192]{1,3,2,0:T(8,128)}, s32[3,576,2]{1,2,0:T(2,128)S(1)}, pred[3,576,2]{1,2,0:T(4,128)(4,1)S(1)}, ...), condition=%wide.region_22.23_spmd.clone, body=%wide.region_21.22_spmd.sunk.clone | while | flops 1615269888 | bytes 11150049 | solution.py:187
  681.4 46.7 %all-gather.19.cloned.1.call-done = bf16[1728,1,768]{0,2,1:T(8,128)(2,1)} async-done(((bf16[1728,1,192]{0,2,1:T(8,128)(2,1)}), bf16[1728,1,768]{0,2,1:T(8,128)(2,1)}) %all-gather.19.cloned.1.call-update) | async-done | bytes 2654224 | tf_op jit(solution)/shard_map/all_gather | solution.py:332
  732.7 53.1 %all-gather.21.cloned.1.call-done = bf16[1728,1,768]{0,2,1:T(8,128)(2,1)} async-done(((bf16[1728,1,192]{0,2,1:T(8,128)(2,1)}), bf16[1728,1,768]{0,2,1:T(8,128)(2,1)}) %all-gather.21.cloned.1.call-update) | async-done | bytes 2654224 | tf_op jit(solution)/shard_map/all_gather | solution.py:333
  799.8 23.9 %while.91 = (s32[]{:T(128)}, f32[3632,192]{0,1:T(8,128)}, s32[3,576,2]{1,2,0:T(2,128)S(1)}, pred[3,576,2]{1,2,0:T(4,128)(4,1)S(1)}, bf16[3,576,2,192]{1,3,2,0:T(8,128)(2,1)S(1)}) while((s32[]{:T(128)}, f32[3632,192]{0,1:T(8,128)}, s32[3,576,2]{1,2,0:T(2,128)S(1)}, pred[3,576,2]{1,2,0:T(4,128)(4,1)S(1)}, ...), condition=%wide.region_25.26_spmd.clone.clone, body=%wide.region_24.25_spmd.clone.sunk.clone | while | flops 1617140736 | bytes 12628563 | solution.py:158
  832.0 24.8 %all_to_all.20 = bf16[8,454,192]{1,2,0:T(8,128)(2,1)S(1)} all-to-all(bf16[8,454,192]{1,2,0:T(8,128)(2,1)S(1)} %copy.280), channel_id=1, replica_groups=mesh['exp'=8,'head'=4] {'exp'}, dimensions={0} | all-to-all | bytes 2789376 | tf_op jit(solution)/shard_map/all_to_all | solution.py:292
  862.2 102.6 %all-gather.13.cloned.1.call-done = bf16[3632,768]{0,1:T(8,128)(2,1)} async-done(((bf16[3632,192]{0,1:T(8,128)(2,1)}), bf16[3632,768]{0,1:T(8,128)(2,1)}) %all-gather.13.cloned.1.call-update) | async-done | bytes 5578768 | tf_op jit(solution)/shard_map/all_gather | solution.py:300
  989.8 191.3 %reduce-scatter.5.cloned.1.call-done = f32[3632,192]{0,1:T(8,128)} async-done(((f32[3632,768]{0,1:T(8,128)}), f32[3632,192]{0,1:T(8,128)}) %reduce-scatter.5.cloned.1.call-update) | async-done | bytes 2789392 | tf_op jit(solution)/shard_map/reduce_scatter | solution.py:315
  1196.1 19.7 %all-to-all-done.3 = bf16[8,454,192]{1,2,0:T(8,128)(2,1)} async-done(((bf16[8,454,192]{1,2,0:T(8,128)(2,1)}), bf16[8,454,192]{1,2,0:T(8,128)(2,1)}, u32[]{:S(2)}, u32[]{:S(2)}) %all-to-all-start.3) | async-done | bytes 1394720 | tf_op jit(solution)/shard_map/all_to_all | solution.py:318
  1221.0 22.5 %while.88 = (s32[]{:T(128)}, bf16[3,576,2,192]{1,3,2,0:T(8,128)(2,1)}, s32[3,576,2]{1,2,0:T(2,128)S(1)}, pred[3,576,2]{1,2,0:T(4,128)(4,1)S(1)}, bf16[3632,192]{1,0:T(8,128)(2,1)}) while((s32[]{:T(128)}, bf16[3,576,2,192]{1,3,2,0:T(8,128)(2,1)}, s32[3,576,2]{1,2,0:T(2,128)S(1)}, pred[3,576,2]{1,2,0:T(4,128)(4,1)S(1)}, ...), condition=%wide.region_28.29_spmd.clone, body=%wide.region_27.28_spmd.sunk.clone | while | flops 1615933440 | bytes 9773793 | solution.py:187
  1258.8 46.9 %all-gather.15.cloned.1.call-done = bf16[1728,1,768]{0,2,1:T(8,128)(2,1)} async-done(((bf16[1728,1,192]{0,2,1:T(8,128)(2,1)}), bf16[1728,1,768]{0,2,1:T(8,128)(2,1)}) %all-gather.15.cloned.1.call-update) | async-done | bytes 2654224 | tf_op jit(solution)/shard_map/all_gather | solution.py:330
  1310.3 53.4 %all-gather.17.cloned.1.call-done = bf16[1728,1,768]{0,2,1:T(8,128)(2,1)} async-done(((bf16[1728,1,192]{0,2,1:T(8,128)(2,1)}), bf16[1728,1,768]{0,2,1:T(8,128)(2,1)}) %all-gather.17.cloned.1.call-update) | async-done | bytes 2654224 | tf_op jit(solution)/shard_map/all_gather | solution.py:331
  1385.6 31.7 %while.89 = (s32[]{:T(128)}, bf16[3,576,3,64]{1,3,2,0:T(8,128)(2,1)S(1)}, bf16[3,576,3,64]{1,3,2,0:T(8,128)(2,1)}, bf16[3,576,3,64]{1,3,2,0:T(8,128)(2,1)S(1)}, ...) while((s32[]{:T(128)}, ...), condition=%wide.region_37.38_spmd.clone, body=%wide.region_35.37_spmd.sunk.clone | while | flops 653818752 | bytes 37770260 | solution.py:370
  1448.5 15.4 convolution_bitcast_fusion.1
  1473.2 150.9 %all-reduce.8.cloned.1.call-done = f32[1728,768]{1,0:T(8,128)} async-done(((f32[1728,768]{1,0:T(8,128)}), f32[1728,768]{1,0:T(8,128)}) %all-reduce.8.cloned.1.call-update) | async-done | bytes 5308432 | tf_op jit(solution)/shard_map/psum | solution.py:389
  1638.6 25.4 %all-reduce = (f32[768]{0:T(1024)}, f32[768]{0:T(1024)}, f32[2,192]{1,0:T(2,128)}, f32[768]{0:T(1024)}, f32[768]{0:T(1024)}, /*index=5*/f32[768]{0:T(1024)}, f32[768,8]{0,1:T(8,128)}) all-reduce(f32[768]{0:T(1024)S(1)} %get-tuple-element.674, f32[768]{0:T(1024)S(1)} %get-tuple-element.677, ...), channel_id=1, replica_groups=mesh['exp'=8,'head'=4] {'exp'}, use_global_device_ids=true, to_apply=%region_42.43 | all-reduce | flops 10368 | bytes 82944 | tf_op jit(solution)/shard_map/psum | solution.py:395
  1664.0 26.4 %all-reduce.10.cloned.1.call-done = (f32[768,3,192]{0,2,1:T(8,128)}, f32[192,768]{1,0:T(8,128)}) async-done(((f32[768,3,192]{0,2,1:T(8,128)}, f32[192,768]{1,0:T(8,128)}), (f32[768,3,192]{0,2,1:T(8,128)}, f32[192,768]{1,0:T(8,128)})) %all-reduce.10.cloned.1.call-update) | async-done | bytes 2359312 | tf_op jit(solution)/shard_map/psum | solution.py:395
  (492 shorter events, 444.2 us)
Async XLA Ops:
  7.2 389.6 %copy-start = (bf16[1,768,768]{2,1,0:T(8,128)(2,1)S(1)}, bf16[1,768,768]{2,1,0:T(8,128)(2,1)}, u32[]{:S(2)}) copy-start(bf16[1,768,768]{2,1,0:T(8,128)(2,1)} %param.49) | copy-start | bytes 3538948
  7.2 242.7 %all-reduce.6.cloned.1.call-start = ((), (), s32[]{:S(2)}) async-start(), calls=%async_computation.6 | async-start | bytes 10616832 | tf_op jit(solution)/shard_map/psum | solution.py:246
  56.1 198.0 %copy-start.57 = (pred[3,576]{1,0:T(4,128)(4,1)}, pred[3,576]{1,0:T(4,128)(4,1)S(1)}, u32[]{:S(2)}) copy-start(pred[3,576]{1,0:T(4,128)(4,1)S(1)} %broadcast_compare_fusion) | copy-start | bytes 5188
  56.7 197.4 %copy-start.54 = (pred[1728]{0:T(1024)(128)(4,1)}, pred[1728]{0:T(1024)(128)(4,1)S(1)}, u32[]{:S(2)}) copy-start(pred[1728]{0:T(1024)(128)(4,1)S(1)} %gt.28) | copy-start | bytes 5188
  63.5 190.6 %copy-start.36 = (f32[3,576,1]{1,0,2:T(4,128)}, f32[3,576,1]{1,0,2:T(4,128)S(1)}, u32[]{:S(2)}) copy-start(f32[3,576,1]{1,0,2:T(4,128)S(1)} %add.235) | copy-start | bytes 20740
  63.5 190.6 %copy-start.50 = (f32[1728,1]{0,1:T(1,128)}, f32[1728,1]{0,1:T(1,128)S(1)}, u32[]{:S(2)}) copy-start(f32[1728,1]{0,1:T(1,128)S(1)} %add.239) | copy-start | bytes 20740
  63.6 190.5 %copy-start.38 = (f32[3,576,1]{1,0,2:T(4,128)}, f32[3,576,1]{1,0,2:T(4,128)S(1)}, u32[]{:S(2)}) copy-start(f32[3,576,1]{1,0,2:T(4,128)S(1)} %stack.50) | copy-start | bytes 20740
  63.6 190.5 %copy-start.52 = (f32[1728,1]{0,1:T(1,128)}, f32[1728,1]{0,1:T(1,128)S(1)}, u32[]{:S(2)}) copy-start(f32[1728,1]{0,1:T(1,128)S(1)} %stack.52) | copy-start | bytes 20740
  63.7 191.3 %copy-start.48 = (f32[768]{0:T(1024)}, f32[768]{0:T(1024)S(1)}, u32[]{:S(2)}) copy-start(f32[768]{0:T(1024)S(1)} %convert_element_type.208) | copy-start | bytes 9220
  311.9 69.0 %all-to-all-start = ((bf16[8,454,768]{2,1,0:T(8,128)(2,1)}), bf16[8,454,768]{2,1,0:T(8,128)(2,1)}, u32[]{:S(2)}, u32[]{:S(2)}) async-start(bf16[8,454,768]{2,1,0:T(8,128)(2,1)} %reshape.463), calls=%async_computation | async-start | bytes 11206656 | tf_op jit(solution)/shard_map/all_to_all | solution.py:259
  316.7 278.9 %reduce-scatter.3.cloned.1.call-start = ((), (), s32[]{:S(2)}) async-start(), calls=%async_computation.7 | async-start | bytes 14254080 | tf_op jit(solution)/shard_map/reduce_scatter | solution.py:273
  605.1 25.3 %all-to-all-start.1 = ((bf16[8,454,192]{1,2,0:T(8,128)(2,1)}), bf16[8,454,192]{1,2,0:T(8,128)(2,1)}, u32[]{:S(2)}, u32[]{:S(2)}) async-start(bf16[8,454,192]{1,2,0:T(8,128)(2,1)} %copy.269), calls=%async_computation.2 | async-start | bytes 3145728 | tf_op jit(solution)/shard_map/all_to_all | solution.py:275
  609.4 64.6 %all-gather.11.cloned.1.call-start = ((), (), s32[]{:S(2)}) async-start(), calls=%async_computation.8 | async-start | bytes 3440640 | tf_op jit(solution)/shard_map/all_gather | solution.py:334
  610.2 117.9 %all-gather.19.cloned.1.call-start = ((), (), s32[]{:S(2)}) async-start(), calls=%async_computation.14 | async-start | bytes 3440640 | tf_op jit(solution)/shard_map/all_gather | solution.py:332
  668.2 117.6 %all-gather.21.cloned.1.call-start = ((), (), s32[]{:S(2)}) async-start(), calls=%async_computation.15 | async-start | bytes 3440640 | tf_op jit(solution)/shard_map/all_gather | solution.py:333
  670.6 294.2 %all-gather.13.cloned.1.call-start = ((), (), s32[]{:S(2)}) async-start(), calls=%async_computation.9 | async-start | bytes 7127040 | tf_op jit(solution)/shard_map/all_gather | solution.py:300
  862.2 120.1 %copy-start.70 = (bf16[1,768,768]{2,1,0:T(8,128)(2,1)S(1)}, bf16[1,768,768]{2,1,0:T(8,128)(2,1)}, u32[]{:S(2)}) copy-start(bf16[1,768,768]{2,1,0:T(8,128)(2,1)} %param.47) | copy-start | bytes 3538948
  862.2 318.9 %reduce-scatter.5.cloned.1.call-start = ((), (), s32[]{:S(2)}) async-start(), calls=%async_computation.10 | async-start | bytes 14254080 | tf_op jit(solution)/shard_map/reduce_scatter | solution.py:315
  1190.5 25.3 %all-to-all-start.3 = ((bf16[8,454,192]{1,2,0:T(8,128)(2,1)}), bf16[8,454,192]{1,2,0:T(8,128)(2,1)}, u32[]{:S(2)}, u32[]{:S(2)}) async-start(bf16[8,454,192]{1,2,0:T(8,128)(2,1)} %copy.282), calls=%async_computation.5 | async-start | bytes 3145728 | tf_op jit(solution)/shard_map/all_to_all | solution.py:318
  1194.8 111.0 %all-gather.15.cloned.1.call-start = ((), (), s32[]{:S(2)}) async-start(), calls=%async_computation.12 | async-start | bytes 3440640 | tf_op jit(solution)/shard_map/all_gather | solution.py:330
  1249.4 114.4 %all-gather.17.cloned.1.call-start = ((), (), s32[]{:S(2)}) async-start(), calls=%async_computation.13 | async-start | bytes 3440640 | tf_op jit(solution)/shard_map/all_gather | solution.py:331
  1250.6 373.5 %all-reduce.8.cloned.1.call-start = ((), (), s32[]{:S(2)}) async-start(), calls=%async_computation.11 | async-start | bytes 10616832 | tf_op jit(solution)/shard_map/psum | solution.py:389
  1434.2 256.2 %all-reduce.10.cloned.1.call-start = ((), (), s32[]{:S(2)}) async-start(), calls=%async_computation.16 | async-start | bytes 4718592 | tf_op jit(solution)/shard_map/psum | solution.py:395
  1473.2 155.8 %copy-start.43 = (f32[1728]{0:T(1024)S(1)}, f32[1728]{0:T(1024)}, u32[]{:S(2)}) copy-start(f32[1728]{0:T(1024)} %copy-done.42) | copy-start | bytes 20740
  (74 other events, 797.6 us)
Sparse Core Ops, SparseCore 0:
  56.1 193.7 all-reduce.5
  405.6 189.9 reduce-scatter.2
  611.8 58.4 all-gather.10
  672.3 55.7 all-gather.18
  730.1 55.7 all-gather.20
  862.3 102.5 all-gather.12
  989.9 191.1 reduce-scatter.4
  1249.5 56.2 all-gather.14
  1308.0 55.7 all-gather.16
  1434.3 189.7 all-reduce.7
  1628.0 62.3 all-reduce.9
where the time goes:
time: 1710 us; the launch traced here: 1700 us
  waiting for transfers between devices  1150 us (67%)
  matrix products  236 us (14%)
  local copies, waits for them, and re-layouts  152 us (9%)
  other arithmetic  80.8 us (5%)
  blocking collectives  50.2 us (3%)
    reduce_scatter x1, waiting for transfers between devices, body(): lax.psum_scatter(rows_grad, 'head', scatter_dimension=1, tiled=True)  191 us
    reduce_scatter x1, waiting for transfers between devices, body(): lax.psum_scatter(partial_expert, 'head', scatter_dimension=1, tiled=True)  190 us
    psum x1, waiting for transfers between devices, body(): lax.psum(partial_out, 'head')  186 us
    psum x1, waiting for transfers between devices, body(): lax.psum(lax.dot_general(qkv_grad, flat_qkv, CONTRACT_LAST, preferred_ele...  151 us
    all_gather x1, waiting for transfers between devices, body(): grad_full = lax.all_gather(grad_rows, 'head', axis=1, tiled=True)  103 us
    all_to_all x1, waiting for transfers between devices, body(): lax.all_to_all(packed.reshape(experts, capacity, model_width), 'exp', spl...  64.1 us
    all_gather x1, waiting for transfers between devices, body(): lax.all_gather(back_pair[:, 1], 'head', axis=1, tiled=True)  53.4 us
    all_gather x1, waiting for transfers between devices, body(): lax.all_gather(picked_half[:, 1], 'head', axis=1, tiled=True)  53.1 us
  transfers between devices with their start and end apart: 14, of which 13 were waited for; matrix products, arithmetic and copies ran while one was open for 8% of the time, Pallas kernels for 0%

commit v1 on v0

v1 whole, which is shorter than its diff:
```python
from functools import partial
import math

import jax
import jax.numpy as jnp
from jax import lax
from jax.sharding import PartitionSpec as P

HEAD_DIM = 64


EPSILON = 1e-06
NEGATIVE = -1e30
CONTRACT_FIRST = (((0,), (0,)), ((), ()))
CONTRACT_LAST = (((1,), (1,)), ((), ()))


def norm_rows(values, gain_row, shift_row):
    row_mean = jnp.mean(values, axis=-1, keepdims=True)
    centred = values - row_mean
    spread = jnp.mean(centred * centred, axis=-1, keepdims=True)
    return centred * lax.rsqrt(spread + EPSILON) * gain_row + shift_row


def masked_scores(query_rows, key_rows, seg_row, live_row, factor):
    scores = (
        jnp.einsum("qhd,khd->hqk", query_rows, key_rows, preferred_element_type=jnp.float32)
        * factor
    )
    same_segment = seg_row[:, None] == seg_row[None, :]
    diagonal = jnp.eye(seg_row.shape[0], dtype=bool)
    allowed = same_segment & ((live_row[None, :] > 0) | diagonal)
    return jnp.where(allowed[None], scores, NEGATIVE)


def attend_sequence(block_item, factor):
    query_rows, key_rows, value_rows, seg_row, live_row = block_item
    masked = masked_scores(query_rows, key_rows, seg_row, live_row, factor)
    largest = jnp.max(masked, axis=-1, keepdims=True)
    weights = jnp.exp(masked - largest)
    totals = jnp.sum(weights, axis=-1, keepdims=True)
    context = jnp.einsum(
        "hqk,khd->qhd",
        (weights / totals).astype(jnp.bfloat16),
        value_rows,
        preferred_element_type=jnp.float32,
    )
    return (context.astype(jnp.bfloat16), largest + jnp.log(totals))


def attend_backward(block_item, factor):
    query_rows, key_rows, value_rows, seg_row, live_row, context_grad, log_total = block_item
    masked = masked_scores(query_rows, key_rows, seg_row, live_row, factor)
    weights = jnp.exp(masked - log_total)
    value_grad = jnp.einsum(
        "hqk,qhd->khd",
        weights.astype(jnp.bfloat16),
        context_grad,
        preferred_element_type=jnp.float32,
    )
    weight_grad = jnp.einsum(
        "qhd,khd->hqk", context_grad, value_rows, preferred_element_type=jnp.float32
    )
    score_grad = (
        weights * (weight_grad - jnp.sum(weights * weight_grad, axis=-1, keepdims=True))
    ).astype(jnp.bfloat16)
    query_grad = (
        jnp.einsum("hqk,khd->qhd", score_grad, key_rows, preferred_element_type=jnp.float32)
        * factor
    )
    key_grad = (
        jnp.einsum("hqk,qhd->khd", score_grad, query_rows, preferred_element_type=jnp.float32)
        * factor
    )
    return (
        query_grad.astype(jnp.bfloat16),
        key_grad.astype(jnp.bfloat16),
        value_grad.astype(jnp.bfloat16),
    )


def slot_tables(routes, live_mask, priority, seqlen, experts, capacity, stride):
    tok_count = routes.shape[0]
    expert_ids = jnp.arange(experts, dtype=jnp.int32)
    live_column = live_mask.reshape(tok_count, 1) > 0
    first_hot = ((routes[:, 0:1] == expert_ids[None, :]) & live_column).astype(jnp.bfloat16)
    second_hot = ((routes[:, 1:2] == expert_ids[None, :]) & live_column).astype(jnp.bfloat16)
    both_hot = jnp.concatenate([first_hot, second_hot], axis=1)
    rank_all = priority.reshape(tok_count)

    def count_block(rank_block):
        earlier = (rank_all[None, :] < rank_block[:, None]).astype(jnp.bfloat16)
        return jnp.dot(earlier, both_hot, preferred_element_type=jnp.float32)

    counts = lax.map(count_block, rank_all.reshape(-1, seqlen)).reshape(tok_count, 2 * experts)
    first_float = first_hot.astype(jnp.float32)
    second_float = second_hot.astype(jnp.float32)
    pos_first = jnp.sum(counts[:, :experts] * first_float, axis=1)
    pos_second = jnp.sum(counts[:, experts:] * second_float, axis=1) + jnp.sum(
        second_float * jnp.sum(first_float, axis=0)[None, :], axis=1
    )
    positions = jnp.stack([pos_first, pos_second], axis=1).astype(jnp.int32)
    kept_pairs = (positions < capacity) & live_column
    return (jnp.where(kept_pairs, routes * stride + positions, -1), kept_pairs)


def round_up(number, step):
    return (number + step - 1) // step * step


def exchange(slot_rows, experts):
    blocks = slot_rows.reshape(experts, slot_rows.shape[0] // experts, *slot_rows.shape[1:])
    moved = lax.all_to_all(blocks, "exp", split_axis=0, concat_axis=0, tiled=True)
    return moved.reshape(slot_rows.shape)


def to_slots(slot_ids, rows, slot_count):
    numbers = jnp.arange(slot_count, dtype=jnp.int32)[:, None]
    onehot = (slot_ids[None, :, 0] == numbers) | (slot_ids[None, :, 1] == numbers)
    return jnp.dot(onehot.astype(jnp.bfloat16), rows, preferred_element_type=jnp.float32).astype(
        jnp.bfloat16
    )


def body(
    tokens,
    segments,
    live_mask,
    routes,
    priority,
    norm1_gain,
    norm1_bias,
    qkv_weight,
    qv_bias,
    out_weight,
    out_bias,
    norm2_gain,
    norm2_bias,
    router,
    up_weight,
    up_bias,
    down_weight,
    down_bias,
    cotangent,
):
    tok_count, model_width = tokens.shape
    seq_count, seqlen = segments.shape
    experts = lax.axis_size("exp")
    head_parts = lax.axis_size("head")
    head_index = lax.axis_index("head")
    quarter = model_width // head_parts
    tok_part = tok_count // head_parts
    capacity = (21 * tok_count + 10 * experts - 1) // (10 * experts)
    stride = round_up(capacity, 16)
    slot_count = experts * stride
    local_width = qkv_weight.shape[2]
    head_count = local_width // HEAD_DIM
    factor = 1.0 / math.sqrt(HEAD_DIM)
    f32 = jnp.float32
    bf16 = jnp.bfloat16

    def my_rows(rows):
        return lax.dynamic_slice_in_dim(rows, head_index * tok_part, tok_part, 0)

    out_full_weight = lax.all_gather(out_weight, "head", axis=0, tiled=True)
    slot_ids, kept_pairs = slot_tables(
        routes, live_mask, priority, seqlen, experts, capacity, stride
    )
    kept_float = kept_pairs.astype(f32)
    out_slots = to_slots(slot_ids, cotangent, slot_count)
    out_rows = lax.all_gather(exchange(out_slots, experts), "head", axis=1, tiled=True)

    inputs = tokens.astype(f32)
    gain_one, bias_one = norm1_gain.astype(f32), norm1_bias.astype(f32)
    gain_two, bias_two = norm2_gain.astype(f32), norm2_bias.astype(f32)
    first_in = norm_rows(inputs, gain_one, bias_one).astype(bf16)
    flat_qkv = qkv_weight.reshape(model_width, 3 * local_width)
    projected = jnp.dot(first_in, flat_qkv, preferred_element_type=f32).reshape(
        tok_count, 3, local_width
    )
    bias_rows = qv_bias.astype(f32)
    shape_four = (seq_count, seqlen, head_count, HEAD_DIM)
    query_rows = (projected[:, 0] + bias_rows[0]).astype(bf16).reshape(shape_four)
    key_rows = projected[:, 1].astype(bf16).reshape(shape_four)
    value_rows = (projected[:, 2] + bias_rows[1]).astype(bf16).reshape(shape_four)
    context, log_total = lax.map(
        partial(attend_sequence, factor=factor),
        (query_rows, key_rows, value_rows, segments, live_mask),
    )
    context_flat = context.reshape(tok_count, local_width)
    context_full = lax.all_gather(context_flat, "head", axis=1, tiled=True)
    residual = (
        inputs
        + jnp.dot(context_full, out_full_weight, preferred_element_type=f32)
        + out_bias.astype(f32)
    )
    second_in = norm_rows(residual, gain_two, bias_two).astype(bf16)
    logits = jnp.dot(second_in, router, preferred_element_type=f32)
    chances = jax.nn.softmax(logits, axis=-1)
    expert_ids = jnp.arange(experts, dtype=jnp.int32)
    chosen = (routes[:, :, None] == expert_ids[None, None, :]).astype(f32)
    gate_values = jnp.sum(chosen * chances[:, None, :], axis=2) * kept_float
    numbers = jnp.arange(slot_count, dtype=jnp.int32)[:, None]
    gate_slots = jnp.sum(
        jnp.where(slot_ids[None, :, 0] == numbers, gate_values[None, :, 0], 0.0)
        + jnp.where(slot_ids[None, :, 1] == numbers, gate_values[None, :, 1], 0.0),
        axis=1,
    )
    expert_rows = exchange(to_slots(slot_ids, second_in, slot_count), experts)
    gate_rows = exchange(gate_slots, experts)

    pre_act = jnp.dot(expert_rows, up_weight[0], preferred_element_type=f32) + up_bias[0].astype(
        f32
    )
    filled = lax.rem(jnp.arange(slot_count, dtype=jnp.int32), stride) < capacity
    gelu_value, gelu_back = jax.vjp(jax.nn.gelu, pre_act)
    hidden = gelu_value.astype(bf16)
    bias_full = lax.dynamic_update_slice_in_dim(
        jnp.zeros((model_width,), f32), down_bias[0].astype(f32), head_index * quarter, 0
    )
    partial_expert = jnp.dot(hidden, down_weight[0], preferred_element_type=f32) + bias_full
    gate_grad_rows = jnp.sum(partial_expert * out_rows.astype(f32), axis=1)
    grad_full = (gate_rows[:, None] * out_rows.astype(f32)).astype(bf16)
    hidden_grad = lax.dot_general(
        grad_full, down_weight[0], CONTRACT_LAST, preferred_element_type=f32
    )
    pre_grad = gelu_back(hidden_grad)[0].astype(bf16)
    rows_grad = lax.dot_general(
        pre_grad, up_weight[0], CONTRACT_LAST, preferred_element_type=f32
    ).astype(bf16)
    home_grad = exchange(rows_grad, experts)
    home_gate = exchange(lax.psum(gate_grad_rows, "head"), experts)
    home_out = exchange(partial_expert.astype(bf16), experts)
    grad_down_bias = jnp.sum(
        lax.dynamic_slice_in_dim(grad_full, head_index * quarter, quarter, 1), axis=0, dtype=f32
    )[None]
    grad_down_weight = lax.dot_general(
        hidden, grad_full, CONTRACT_FIRST, preferred_element_type=f32
    )[None]
    grad_up_weight = lax.dot_general(
        expert_rows, pre_grad, CONTRACT_FIRST, preferred_element_type=f32
    )[None]
    grad_up_bias = jnp.sum(pre_grad, axis=0, dtype=f32)[None]

    first_hit = slot_ids[:, 0:1] == numbers.T
    second_hit = slot_ids[:, 1:2] == numbers.T
    back_sum = jnp.dot(
        (first_hit | second_hit).astype(bf16), home_grad, preferred_element_type=f32
    ).astype(bf16)
    back_rows = lax.psum_scatter(back_sum, "head", scatter_dimension=0, tiled=True)
    my_ids = my_rows(slot_ids)
    gate_grad = jnp.stack(
        [
            jnp.sum(jnp.where(my_ids[:, 0:1] == numbers.T, home_gate[None, :], 0.0), axis=1),
            jnp.sum(jnp.where(my_ids[:, 1:2] == numbers.T, home_gate[None, :], 0.0), axis=1),
        ],
        axis=1,
    )
    my_chances = my_rows(chances)
    my_second = my_rows(second_in)
    route_grad = jnp.sum(my_rows(chosen) * gate_grad[:, :, None], axis=1)
    logit_grad = (
        my_chances * (route_grad - jnp.sum(my_chances * route_grad, axis=1, keepdims=True))
    ).astype(bf16)
    grad_router = lax.dot_general(
        my_second, logit_grad, CONTRACT_FIRST, preferred_element_type=f32
    )
    normed_two_grad = back_rows.astype(f32) + lax.dot_general(
        logit_grad, router, CONTRACT_LAST, preferred_element_type=f32
    )
    ignored, norm_two_back = jax.vjp(norm_rows, my_rows(residual), gain_two, bias_two)
    residual_norm, grad_norm2_gain, grad_norm2_bias = norm_two_back(normed_two_grad)
    cotangent_rows = lax.all_to_all(
        cotangent, "head", split_axis=0, concat_axis=1, tiled=True
    )
    residual_grad = cotangent_rows.astype(f32) + residual_norm
    grad_out_bias = jnp.sum(residual_grad, axis=0)
    residual_half = lax.all_gather(residual_grad.astype(bf16), "head", axis=0, tiled=True)

    moe_sum = jnp.dot(
        jnp.where(first_hit, gate_values[:, 0:1], jnp.where(second_hit, gate_values[:, 1:2], 0.0)).astype(bf16),
        home_out,
        preferred_element_type=f32,
    ).astype(bf16)
    moe_cols = lax.psum_scatter(moe_sum, "head", scatter_dimension=1, tiled=True)
    block_out = (
        lax.dynamic_slice_in_dim(residual, head_index * quarter, quarter, 1) + moe_cols.astype(f32)
    ).astype(bf16)

    grad_out_weight = lax.dot_general(
        context_flat, residual_half, CONTRACT_FIRST, preferred_element_type=f32
    )
    context_grad = (
        lax.dot_general(residual_half, out_weight, CONTRACT_LAST, preferred_element_type=f32)
        .astype(bf16)
        .reshape(shape_four)
    )
    query_grad, key_grad, value_grad = lax.map(
        partial(attend_backward, factor=factor),
        (query_rows, key_rows, value_rows, segments, live_mask, context_grad, log_total),
    )
    query_flat = query_grad.reshape(tok_count, local_width)
    value_flat = value_grad.reshape(tok_count, local_width)
    qkv_grad = jnp.stack(
        [query_flat, key_grad.reshape(tok_count, local_width), value_flat], axis=1
    ).reshape(tok_count, 3 * local_width)
    normed_one_grad = lax.psum_scatter(
        lax.dot_general(qkv_grad, flat_qkv, CONTRACT_LAST, preferred_element_type=f32).astype(bf16),
        "head",
        scatter_dimension=0,
        tiled=True,
    ).astype(f32)
    grad_qkv_weight = lax.dot_general(
        first_in, qkv_grad, CONTRACT_FIRST, preferred_element_type=f32
    ).reshape(model_width, 3, local_width)
    grad_qv_bias = jnp.stack(
        [jnp.sum(query_flat, axis=0, dtype=f32), jnp.sum(value_flat, axis=0, dtype=f32)], axis=0
    )
    ignored, norm_one_back = jax.vjp(norm_rows, my_rows(inputs), gain_one, bias_one)
    inputs_norm, grad_norm1_gain, grad_norm1_bias = norm_one_back(normed_one_grad)
    grad_tokens = lax.all_gather(
        (residual_grad + inputs_norm).astype(bf16), "head", axis=0, tiled=True
    ).astype(f32)
    sums_all = lax.psum(
        (
            grad_norm1_gain,
            grad_norm1_bias,
            grad_out_bias,
            grad_norm2_gain,
            grad_norm2_bias,
            grad_router,
        ),
        ("exp", "head"),
    )
    grad_out_weight = lax.psum(grad_out_weight, "exp")
    grad_qkv_weight, grad_qv_bias = lax.psum((grad_qkv_weight, grad_qv_bias), "exp")
    return (
        block_out,
        grad_tokens,
        sums_all[0],
        sums_all[1],
        grad_qkv_weight,
        grad_qv_bias,
        grad_out_weight,
        sums_all[2],
        sums_all[3],
        sums_all[4],
        sums_all[5],
        grad_up_weight,
        grad_up_bias,
        grad_down_weight,
        grad_down_bias,
    )


def solution(mesh):
    in_specs = (
        P("exp", None),
        P("exp", None),
        P("exp", None),
        P("exp", None),
        P("exp", None),
        P(),
        P(),
        P(None, None, "head"),
        P(None, "head"),
        P("head", None),
        P(),
        P(),
        P(),
        P(),
        P("exp", None, "head"),
        P("exp", "head"),
        P("exp", "head", None),
        P("exp", "head"),
        P("exp", "head"),
    )
    out_specs = (
        P("exp", "head"),
        P("exp", None),
        P(),
        P(),
        P(None, None, "head"),
        P(None, "head"),
        P("head", None),
        P(),
        P(),
        P(),
        P(),
        P("exp", None, "head"),
        P("exp", "head"),
        P("exp", "head", None),
        P("exp", "head"),
    )
    return jax.shard_map(body, mesh=mesh, in_specs=in_specs, out_specs=out_specs, check_vma=False)
```

time: 1710 us -> 829 us (0.48)
  waiting for transfers between devices: 1150 us -> 274 us
  blocking collectives: 50.2 us -> 144 us
  local copies, waits for them, and re-layouts: 152 us -> 103 us
  matrix products: 236 us -> 195 us
  other arithmetic: 80.8 us -> 63 us
    reduce_scatter x2, waiting for transfers between devices: 381 us -> 29 us  [the longest x1 29 us: body(): lax.psum_scatter(lax.dot_general(qkv_grad, flat_qkv, CONTRACT_LAST, prefe...]
    psum x3 -> x1, waiting for transfers between devices: 363 us -> 53.6 us  [body(): lax.psum((grad_qkv_weight, grad_qv_bias), 'exp')]
    all_gather x6 -> x5, waiting for transfers between devices: 303 us -> 46.5 us  [the longest x1 46.5 us: body(): lax.all_gather(residual_grad.astype(bf16), 'head', axis=0, tiled=True)]
    psum x1 -> x3, blocking collectives: 25.4 us -> 76.4 us  [the longest x1 43 us: body(): lax.psum((grad_norm1_gain, grad_norm1_bias, grad_out_bias, grad_norm2_gai...]
    all_to_all x1, blocking collectives: 24.8 us -> 67.7 us  [exchange(): lax.all_to_all(blocks, 'exp', split_axis=0, concat_axis=0, tiled=True)]
    dot_general x27 -> x10, matrix products: 132 us -> 92.5 us  [the longest x2 26 us: to_slots(): jnp.dot(onehot.astype(jnp.bfloat16), rows, preferred_element_type=jnp.flo...]
    all_to_all x3 -> x6, waiting for transfers between devices: 104 us -> 132 us  [the longest x5 89.9 us: exchange(): lax.all_to_all(blocks, 'exp', split_axis=0, concat_axis=0, tiled=True)]
  transfers between devices with their start and end apart: 14 -> 15, of which waited for: 13 -> 8; matrix products, arithmetic and copies ran while one was open for 8% -> 34% of each run, Pallas kernels for 0% -> 0%
where the time goes in v1:
time: 829 us; the launch traced here: 823 us
  waiting for transfers between devices  274 us (33%)
  matrix products  195 us (24%)
  blocking collectives  144 us (17%)
  local copies, waits for them, and re-layouts  103 us (12%)
  other arithmetic  63 us (8%)
  starting transfers between devices  27.3 us (3%)
  between operations  15.4 us (2%)
    all_to_all x5, waiting for transfers between devices, exchange(): lax.all_to_all(blocks, 'exp', split_axis=0, concat_axis=0, tiled=True)  89.9 us
    all_to_all x1, blocking collectives, exchange(): lax.all_to_all(blocks, 'exp', split_axis=0, concat_axis=0, tiled=True)  67.7 us
    psum x1, waiting for transfers between devices, body(): lax.psum((grad_qkv_weight, grad_qv_bias), 'exp')  53.6 us
    all_gather x1, waiting for transfers between devices, body(): lax.all_gather(residual_grad.astype(bf16), 'head', axis=0, tiled=True)  46.5 us
    psum x1, blocking collectives, body(): lax.psum((grad_norm1_gain, grad_norm1_bias, grad_out_bias, grad_norm2_gai...  43 us
    all_to_all x1, waiting for transfers between devices, body(): lax.all_to_all(cotangent, 'head', split_axis=0, concat_axis=1, tiled=True)  41.8 us
    reduce_scatter x1, waiting for transfers between devices, body(): lax.psum_scatter(lax.dot_general(qkv_grad, flat_qkv, CONTRACT_LAST, prefe...  29 us
    dot_general x2, matrix products, to_slots(): jnp.dot(onehot.astype(jnp.bfloat16), rows, preferred_element_type=jnp.flo...  26 us
  transfers between devices with their start and end apart: 15, of which 8 were waited for; matrix products, arithmetic and copies ran while one was open for 34% of the time, Pallas kernels for 0%

profile of v1, /device:TPU:0, one launch (start us, length us, event | category | flops | bytes accessed | tf_op | source)
XLA Modules:
  0.0 822.9 jit_solution(4650629003328193193)
XLA Ops:
  29.8 18.8 %while.36 = (s32[]{:T(128)}, bf16[3,576,3,64]{1,3,2,0:T(8,128)(2,1)S(1)}, f32[3,3,576,1]{2,1,3,0:T(4,128)}, bf16[3,576,3,64]{1,3,2,0:T(8,128)(2,1)}, s32[3,576]{...) while((s32[]{:T(128)}, ...), condition=%wide.region_5.6_spmd, body=%wide.region_2.0_spmd.sunk | while | flops 268184448 | bytes 14847985 | solution.py:186
  53.7 9.0 %while.37 = (s32[]{:T(128)}, f32[3,576,16]{1,0,2:T(4,128)}, s32[1,1728]{1,0:T(1,128)S(1)}, s32[3,576]{1,0:T(4,128)S(1)}, bf16[1728,16]{0,1:T(8,128)(2,1)S(1)}, /*index=5*/s32[]{:T(128)}, s32[]{:T(128)}) while((s32[]{:T(128)}, f32[3,576,16]{1,0,2:T(4,128)}, s32[1,1728]{1,0:T(1,128)S(1)}, s32[3,576]{1,0:T(4,128)S(1)}, ...), condition=%wide.region_7.8_spmd, body=%wide.region_6.7_spmd.sunk | while | flops 32845824 | bytes 267361 | solution.py:95
  84.3 20.9 %all-to-all-done.4 = bf16[8,464,192]{1,2,0:T(8,128)(2,1)S(1)} async-done(((bf16[8,464,192]{1,2,0:T(8,128)(2,1)}), bf16[8,464,192]{1,2,0:T(8,128)(2,1)S(1)}, u32[]{:S(2)}, u32[]{:S(2)}) %all-to-all-start.4) | async-done | bytes 1425440 | tf_op jit(solution)/shard_map/all_to_all | solution.py:113
  107.2 13.3 %reshape.386 = bf16[3712,192]{0,1:T(8,128)(2,1)} reshape(bf16[8,464,192]{1,0,2:T(8,128)(2,1)} %copy.139) | data formatting | bytes 2850816 | tf_op jit(solution)/shard_map/reshape | solution.py:114
  130.4 10.5 %add_reduce_fusion = f32[3712]{0:T(1024)S(1)} fusion(f32[1728]{0:T(1024)S(1)} %get-tuple-element.333, f32[1728]{0:T(1024)S(1)} %get-tuple-element.332, s32[1728]{0:T(1024)S(1)} %copy-done.36, s32[1728]{0:T(1024)S(1)} %copy-done.33), kind=kLoop, calls=%fused_computation.78 | loop fusion | flops 38482304 | bytes 42496 | tf_op jit(solution)/shard_map/reduce_sum | solution.py:204
  145.0 17.6 %fusion.99 = bf16[3712,768]{1,0:T(8,128)(2,1)} fusion(bf16[1728,768]{1,0:T(8,128)(2,1)} %copy-done.10, s32[1728]{0:T(1024)S(1)} %copy-done.36, s32[1728]{0:T(1024)S(1)} %copy-done.33), kind=kOutput, calls=%fused_computation.117 | convolution fusion | flops 9874513920 | bytes 8369664 | tf_op jit(solution)/shard_map/dot_general | solution.py:120
  168.4 64.4 %all-to-all-done = bf16[8,464,768]{2,1,0:T(8,128)(2,1)} async-done(((bf16[8,464,768]{2,1,0:T(8,128)(2,1)}), bf16[8,464,768]{2,1,0:T(8,128)(2,1)}, u32[]{:S(2)}, u32[]{:S(2)}) %all-to-all-start) | async-done | bytes 5701664 | tf_op jit(solution)/shard_map/all_to_all | solution.py:113
  232.7 9.8 %fusion.124 = f32[3712,768]{1,0:T(8,128)} fusion(bf16[3712,768]{1,0:T(8,128)(2,1)} %bitcast.23, bf16[1,768,768]{2,1,0:T(8,128)(2,1)S(1)} %copy-done.54), kind=kOutput, calls=%fused_computation.172 | convolution fusion | flops 4378853376 | bytes 18284544 | tf_op jit(solution)/shard_map/dot_general | solution.py:212
  250.9 15.0 %fusion.91 = (f32[3712]{0:T(1024)S(1)}, bf16[3712,768]{1,0:T(8,128)(2,1)}, bf16[3712,768]{1,0:T(8,128)(2,1)S(1)}) fusion(bf16[3712,768]{1,0:T(8,128)(2,1)} %copy.140, f32[768]{0:T(1024)S(1)} %dynamic_update_slice.26, f32[3712]{0:T(1024)S(1)} %mul.291, bf16[1,768,768]{2,1,0:T(8,128)(2,1)S(1)} %copy-done, f32[3712,768]{1,0:T(8,128)} %fusion.124, ...), kind=kOutput, calls=%fused_computation.106 | convolution fusion | flops 4427313664 | bytes 29723648 | tf_op jit(solution)/shard_map/dot_general | solution.py:221
  265.9 17.2 %convert_reduce_fusion = (f32[768]{0:T(1024)}, bf16[3712,768]{1,0:T(8,128)(2,1)}) fusion(f32[3712,768]{1,0:T(8,128)} %fusion.124, f32[768]{0:T(1024)S(1)} %convert_reduce_fusion.7, bf16[3712,768]{1,0:T(8,128)(2,1)S(1)} %get-tuple-element.407, bf16[1,768,768]{2,1,0:T(8,128)(2,1)S(1)} %copy-done), kind=kOutput, calls=%fused_computation.114 | convolution fusion | flops 4444421120 | bytes 23992320 | tf_op jit(solution)/shard_map/dot_general | solution.py:224
  291.0 67.7 %all_to_all.51 = bf16[8,464,768]{2,1,0:T(8,128)(2,1)S(1)} all-to-all(bf16[8,464,768]{2,1,0:T(8,128)(2,1)S(1)} %bitcast.217), channel_id=1, replica_groups=mesh['exp'=8,'head'=4] {'exp'}, dimensions={0} | all-to-all | bytes 11403264 | tf_op jit(solution)/shard_map/all_to_all | solution.py:113
  358.7 14.5 %fusion.106 = bf16[1728,768]{1,0:T(8,128)(2,1)} fusion(bf16[3712,768]{1,0:T(8,128)(2,1)S(1)} %bitcast.216, s32[1728]{0:T(1024)S(1)} %copy-done.36, s32[1728]{0:T(1024)S(1)} %copy-done.33), kind=kOutput, calls=%fused_computation.133 | convolution fusion | flops 9872990208 | bytes 8369664 | tf_op jit(solution)/shard_map/dot_general | solution.py:247
  380.4 41.8 %all-to-all-done.2 = bf16[4,432,192]{1,2,0:T(8,128)(2,1)S(1)} async-done(((bf16[4,432,192]{1,2,0:T(8,128)(2,1)}), bf16[4,432,192]{1,2,0:T(8,128)(2,1)S(1)}, u32[]{:S(2)}, u32[]{:S(2)}) %all-to-all-start.2) | async-done | bytes 663584 | tf_op jit(solution)/shard_map/all_to_all | solution.py:273
  427.1 19.0 %psum.70 = f32[8,1,464]{2,1,0:T(1,128)} all-reduce(f32[8,1,464]{2,1,0:T(1,128)S(1)} %all_to_all.42), channel_id=1, replica_groups=mesh['exp'=8,'head'=4] {'head'}, use_global_device_ids=true, to_apply=%region_21.22 | all-reduce | flops 3712 | bytes 29696 | tf_op jit(solution)/shard_map/psum | solution.py:232
  468.4 46.5 %all-gather.12.cloned.1.call-done = bf16[1728,768]{1,0:T(8,128)(2,1)} async-done(((bf16[432,768]{1,0:T(8,128)(2,1)}), bf16[1728,768]{1,0:T(8,128)(2,1)}) %all-gather.12.cloned.1.call-update) | async-done | bytes 2654224 | tf_op jit(solution)/shard_map/all_gather | solution.py:278
  526.7 35.1 %while.38 = (s32[]{:T(128)}, bf16[3,576,3,64]{1,3,2,0:T(8,128)(2,1)}, bf16[3,576,3,64]{1,3,2,0:T(8,128)(2,1)}, bf16[3,576,3,64]{1,3,2,0:T(8,128)(2,1)}, bf16[3,5...) while((s32[]{:T(128)}, ...), condition=%wide.region_32.33_spmd, body=%wide.region_30.32_spmd.sunk | while | flops 653818752 | bytes 37770276 | solution.py:298
  580.4 17.5 %fusion.109 = bf16[768,1728]{1,0:T(8,128)(2,1)} fusion(bf16[3712,768]{1,0:T(8,128)(2,1)} %bitcast.28, f32[1728]{0:T(1024)S(1)} %copy-done.41, s32[1728]{0:T(1024)S(1)} %copy-done.37, f32[1728]{0:T(1024)S(1)} %copy-done.39, s32[1728]{0:T(1024)S(1)} %copy-done.34), kind=kOutput, calls=%fused_computation.134 | convolution fusion | flops 9879404544 | bytes 8383488 | tf_op jit(solution)/shard_map/dot_general | solution.py:280
  602.6 29.0 %reduce-scatter.8.cloned.1.call-done = bf16[432,768]{1,0:T(8,128)(2,1)} async-done(((bf16[1728,768]{1,0:T(8,128)(2,1)}), bf16[432,768]{1,0:T(8,128)(2,1)}) %reduce-scatter.8.cloned.1.call-update) | async-done | bytes 663568 | tf_op jit(solution)/shard_map/reduce_scatter | solution.py:307
  638.8 14.0 %convolution_bitcast_fusion = f32[1,768,768]{2,1,0:T(8,128)} fusion(bf16[3712,768]{1,0:T(8,128)(2,1)} %copy-done.17, f32[3712,768]{1,0:T(8,128)} %fusion.124, f32[768]{0:T(1024)S(1)} %copy-done.44), kind=kOutput, calls=%fused_computation.147 | convolution fusion | flops 4407361536 | bytes 19467264 | tf_op jit(solution)/shard_map/dot_general | solution.py:237
  658.9 10.8 %convolution_bitcast_fusion.1 = f32[1,768,768]{2,1,0:T(8,128)} fusion(bf16[3712,768]{1,0:T(8,128)(2,1)} %bitcast.23, bf16[3712,768]{1,0:T(8,128)(2,1)} %get-tuple-element.422), kind=kOutput, calls=%fused_computation.148 | convolution fusion | flops 4378853376 | bytes 13762560 | tf_op jit(solution)/shard_map/dot_general | solution.py:240
  675.2 12.6 %reduce-scatter.10.cloned.1.call-done = bf16[192,1728]{1,0:T(8,128)(2,1)} async-done(((bf16[768,1728]{1,0:T(8,128)(2,1)}), bf16[192,1728]{1,0:T(8,128)(2,1)}) %reduce-scatter.10.cloned.1.call-update) | async-done | bytes 663568
  695.2 14.4 %psum.74 = f32[2,192]{1,0:T(2,128)} all-reduce(f32[2,192]{1,0:T(2,128)S(1)} %pad_maximum_fusion.2), channel_id=1, replica_groups=mesh['exp'=8,'head'=4] {'exp'}, use_global_device_ids=true, to_apply=%region_45.46 | all-reduce | flops 384 | bytes 3072 | tf_op jit(solution)/shard_map/psum | solution.py:336
  709.6 43.0 %all-reduce = (f32[768]{0:T(1024)}, f32[768]{0:T(1024)}, f32[768]{0:T(1024)}, f32[768]{0:T(1024)}, f32[768]{0:T(1024)}, /*index=5*/f32[768,8]{0,1:T(8,128)}) all-reduce(f32[768]{0:T(1024)S(1)} %get-tuple-element.322, f32[768]{0:T(1024)S(1)} %get-tuple-element.327, ...), channel_id=1, replica_groups=mesh['exp'=8,'head'=4] {'exp','head'}, use_global_device_ids=true, to_apply=%region_39.40 | all-reduce | flops 9984 | bytes 79872 | tf_op jit(solution)/shard_map/psum | solution.py:324
  757.6 53.6 %all-reduce.4.cloned.1.call-done = (f32[768,3,192]{0,2,1:T(8,128)}, f32[192,768]{1,0:T(8,128)}) async-done(((f32[768,3,192]{0,2,1:T(8,128)}, f32[192,768]{1,0:T(8,128)}), (f32[768,3,192]{0,2,1:T(8,128)}, f32[192,768]{1,0:T(8,128)})) %all-reduce.4.cloned.1.call-update) | async-done | bytes 2359312 | tf_op jit(solution)/shard_map/psum | solution.py:336
  (345 shorter events, 253.7 us)
Async XLA Ops:
  7.2 243.8 %copy-start = (bf16[1,768,768]{2,1,0:T(8,128)(2,1)S(1)}, bf16[1,768,768]{2,1,0:T(8,128)(2,1)}, u32[]{:S(2)}) copy-start(bf16[1,768,768]{2,1,0:T(8,128)(2,1)} %param.41) | copy-start | bytes 3538948
  7.2 113.4 %all-gather.8.cloned.1.call-start = ((), (), s32[]{:S(2)}) async-start(), calls=%async_computation.11 | async-start | bytes 1474560 | tf_op jit(solution)/shard_map/all_gather | solution.py:165
  7.9 112.7 %all-gather.6.cloned.1.call-start = ((), (), s32[]{:S(2)}) async-start(), calls=%async_computation.10 | async-start | bytes 3440640 | tf_op jit(solution)/shard_map/all_gather | solution.py:191
  79.0 26.2 %all-to-all-start.4 = ((bf16[8,464,192]{1,2,0:T(8,128)(2,1)}), bf16[8,464,192]{1,2,0:T(8,128)(2,1)S(1)}, u32[]{:S(2)}, u32[]{:S(2)}) async-start(bf16[8,464,192]{1,2,0:T(8,128)(2,1)} %copy.138), calls=%async_computation.4 | async-start | bytes 3145728 | tf_op jit(solution)/shard_map/all_to_all | solution.py:113
  84.2 158.4 %all-gather.10.cloned.1.call-start = ((), (), s32[]{:S(2)}) async-start(), calls=%async_computation.12 | async-start | bytes 7127040 | tf_op jit(solution)/shard_map/all_gather | solution.py:171
  141.7 20.9 %all-to-all-start.3 = ((f32[8,1,464]{2,1,0:T(1,128)}), f32[8,1,464]{2,1,0:T(1,128)S(1)}, u32[]{:S(2)}, u32[]{:S(2)}) async-start(f32[8,1,464]{2,1,0:T(1,128)} %all_to_all.38), calls=%async_computation.3 | async-start | bytes 32768 | tf_op jit(solution)/shard_map/all_to_all | solution.py:113
  162.6 70.1 %copy-start.54 = (bf16[1,768,768]{2,1,0:T(8,128)(2,1)S(1)}, bf16[1,768,768]{2,1,0:T(8,128)(2,1)}, u32[]{:S(2)}) copy-start(bf16[1,768,768]{2,1,0:T(8,128)(2,1)} %param.39) | copy-start | bytes 3538948
  162.6 70.1 %all-to-all-start = ((bf16[8,464,768]{2,1,0:T(8,128)(2,1)}), bf16[8,464,768]{2,1,0:T(8,128)(2,1)}, u32[]{:S(2)}, u32[]{:S(2)}) async-start(bf16[8,464,768]{2,1,0:T(8,128)(2,1)} %bitcast.215), calls=%async_computation | async-start | bytes 11403264 | tf_op jit(solution)/shard_map/all_to_all | solution.py:113
  167.5 288.9 %reduce-scatter.6.cloned.1.call-start = ((), (), s32[]{:S(2)}) async-start(), calls=%async_computation.13 | async-start | bytes 3317760 | tf_op jit(solution)/shard_map/reduce_scatter | solution.py:250
  168.2 97.7 %copy-start.43 = (f32[768]{0:T(1024)}, f32[768]{0:T(1024)S(1)}, u32[]{:S(2)}) copy-start(f32[768]{0:T(1024)S(1)} %convert_reduce_fusion.7) | copy-start | bytes 9220
  375.4 46.7 %all-to-all-start.2 = ((bf16[4,432,192]{1,2,0:T(8,128)(2,1)}), bf16[4,432,192]{1,2,0:T(8,128)(2,1)S(1)}, u32[]{:S(2)}, u32[]{:S(2)}) async-start(bf16[4,432,192]{1,2,0:T(8,128)(2,1)} %copy.137), calls=%async_computation.2 | async-start | bytes 1572864 | tf_op jit(solution)/shard_map/all_to_all | solution.py:273
  380.3 76.1 %copy-start.29 = (bf16[768,8]{0,1:T(8,128)(2,1)S(1)}, bf16[768,8]{0,1:T(8,128)(2,1)}, u32[]{:S(2)}) copy-start(bf16[768,8]{0,1:T(8,128)(2,1)} %param.38) | copy-start | bytes 36868
  446.1 8.0 all-to-all-start.6
  449.4 65.4 %all-gather.12.cloned.1.call-start = ((), (), s32[]{:S(2)}) async-start(), calls=%async_computation.14 | async-start | bytes 3317760 | tf_op jit(solution)/shard_map/all_gather | solution.py:278
  463.0 51.8 %copy-start.18 = (bf16[192,768]{1,0:T(8,128)(2,1)S(1)}, bf16[192,768]{1,0:T(8,128)(2,1)}, u32[]{:S(2)}) copy-start(bf16[192,768]{1,0:T(8,128)(2,1)} %param.34) | copy-start | bytes 884740
  463.0 117.3 %all-to-all-start.1 = ((bf16[8,464,768]{2,1,0:T(8,128)(2,1)}), bf16[8,464,768]{2,1,0:T(8,128)(2,1)}, u32[]{:S(2)}, u32[]{:S(2)}) async-start(bf16[8,464,768]{2,1,0:T(8,128)(2,1)} %bitcast.214), calls=%async_computation.1 | async-start | bytes 11403264 | tf_op jit(solution)/shard_map/all_to_all | solution.py:113
  467.9 58.8 %copy-start.4 = (bf16[3,576,3,64]{1,3,2,0:T(8,128)(2,1)S(1)}, bf16[3,576,3,64]{1,3,2,0:T(8,128)(2,1)}, u32[]{:S(2)}) copy-start(bf16[3,576,3,64]{1,3,2,0:T(8,128)(2,1)} %copy-done.3) | copy-start | bytes 1990660
  467.9 58.8 %copy-start.6 = (bf16[3,576,3,64]{1,3,2,0:T(8,128)(2,1)S(1)}, bf16[3,576,3,64]{1,3,2,0:T(8,128)(2,1)}, u32[]{:S(2)}) copy-start(bf16[3,576,3,64]{1,3,2,0:T(8,128)(2,1)} %copy-done.5) | copy-start | bytes 1990660
  468.0 163.7 %reduce-scatter.8.cloned.1.call-start = ((), (), s32[]{:S(2)}) async-start(), calls=%async_computation.15 | async-start | bytes 3317760 | tf_op jit(solution)/shard_map/reduce_scatter | solution.py:307
  580.1 107.7 %reduce-scatter.10.cloned.1.call-start = ((), (), s32[]{:S(2)}) async-start(), calls=%async_computation.17 | async-start | bytes 3440640
  597.9 154.8 %all-gather.14.cloned.1.call-start = ((), (), s32[]{:S(2)}) async-start(), calls=%async_computation.16 | async-start | bytes 3317760 | tf_op jit(solution)/shard_map/all_gather | solution.py:321
  602.6 36.2 %copy-start.44 = (f32[768]{0:T(1024)S(1)}, f32[768]{0:T(1024)}, u32[]{:S(2)}) copy-start(f32[768]{0:T(1024)} %copy-done.43) | copy-start | bytes 9220
  638.8 172.4 %all-reduce.4.cloned.1.call-start = ((), (), s32[]{:S(2)}) async-start(), calls=%async_computation.18 | async-start | bytes 4718592 | tf_op jit(solution)/shard_map/psum | solution.py:336
  709.6 106.3 %copy-start.1 = (bf16[1,768,768]{2,1,0:T(8,128)(2,1)S(1)}, bf16[1,768,768]{2,1,0:T(8,128)(2,1)}, u32[]{:S(2)}) copy-start(bf16[1,768,768]{2,1,0:T(8,128)(2,1)} %param.41) | copy-start | bytes 3538948
  (49 other events, 416.5 us)
Sparse Core Ops, SparseCore 0:
  9.6 33.1 all-gather.7
  53.5 59.6 all-gather.5
  120.7 105.0 all-gather.9
  373.4 64.6 reduce-scatter.5
  463.2 51.6 all-gather.11
  580.2 51.3 reduce-scatter.7
  634.0 53.8 reduce-scatter.9
  689.4 56.1 all-gather.13
  749.4 61.7 all-reduce.3

commit v2 on v1

v2 whole, which is shorter than its diff:
```python
from functools import partial
import math

import jax
import jax.numpy as jnp
from jax import lax
from jax.experimental import pallas as pl
from jax.experimental.pallas import tpu as pltpu
from jax.sharding import PartitionSpec as P

HEAD_DIM = 64
LANES = 128
EPSILON = 1e-06
NEGATIVE = -1e30
CONTRACT_FIRST = (((0,), (0,)), ((), ()))
CONTRACT_LAST = (((1,), (1,)), ((), ()))
F32 = jnp.float32
BF16 = jnp.bfloat16
MESH = pl.DeviceIdType.MESH
VMEM_LIMIT = 48 * 1024 * 1024


def round_up(number, step):
    return (number + step - 1) // step * step


def whole():
    return pl.BlockSpec(memory_space=pltpu.VMEM)


def anywhere():
    return pl.BlockSpec(memory_space=pl.ANY)


def shaped(shape, dtype):
    return jax.ShapeDtypeStruct(shape, dtype)


def params(**more):
    return pltpu.CompilerParams(vmem_limit_bytes=VMEM_LIMIT, **more)


def cost(flops, moved):
    return pl.CostEstimate(flops=int(flops), bytes_accessed=int(moved), transcendentals=0)


def dot(left, right):
    return jnp.dot(left, right, preferred_element_type=F32)


def dot_last(left, right):
    return lax.dot_general(left, right, CONTRACT_LAST, preferred_element_type=F32)


def dot_first(left, right):
    return lax.dot_general(left, right, CONTRACT_FIRST, preferred_element_type=F32)


def standard(values):
    centred = values - jnp.mean(values, axis=-1, keepdims=True)
    scale = lax.rsqrt(jnp.mean(centred * centred, axis=-1, keepdims=True) + EPSILON)
    return centred * scale, scale


def norm_back(grad_rows, gain_row, normal, scale):
    inner = grad_rows * gain_row
    return scale * (
        inner
        - jnp.mean(inner, axis=-1, keepdims=True)
        - normal * jnp.mean(inner * normal, axis=-1, keepdims=True)
    )


def mask_penalty(seg_col, seg_row, live_row):
    shape = (seg_col.shape[0], seg_row.shape[1])
    diagonal = lax.broadcasted_iota(jnp.int32, shape, 0) == lax.broadcasted_iota(
        jnp.int32, shape, 1
    )
    allowed = (seg_col == seg_row) & ((live_row > 0) | diagonal)
    return jnp.where(allowed, 0.0, NEGATIVE)


def pack_rows(rows, half):
    count = rows.shape[0]
    third = rows[:, LANES:]
    return rows[:, :LANES], jnp.concatenate([third[:half], third[count - half :]], axis=1)


def unpack_rows(parts_of, into, head_parts, count, half):
    extra = HEAD_DIM
    width = LANES + extra
    for z in range(head_parts):
        packed = parts_of(z)
        into[:, z * width : z * width + LANES] = packed[:count]
        tail = packed[count : count + half]
        into[:half, z * width + LANES : (z + 1) * width] = tail[:, :extra]
        into[half:, z * width + LANES : (z + 1) * width] = tail[2 * half - count :, extra:]


def attend_kernel(
    tokens_ref, norm_ref, weight_ref, bias_ref, segc_ref, segr_ref, live_ref,
    first_ref, qkv_ref, context_ref, packed_ref, total_ref,
):
    normal, ignored = standard(tokens_ref[...].astype(F32))
    first = (normal * norm_ref[0:1] + norm_ref[1:2]).astype(BF16)
    first_ref[...] = first
    rows = (dot(first, weight_ref[...]) + bias_ref[...]).astype(BF16)
    qkv_ref[...] = rows
    penalty = mask_penalty(segc_ref[0], segr_ref[0], live_ref[0])
    seqlen = rows.shape[0]
    width = rows.shape[1] // 3
    parts = []
    for head in range(width // HEAD_DIM):
        lo = head * HEAD_DIM
        hi = lo + HEAD_DIM
        query = rows[:, lo:hi] * BF16(1.0 / math.sqrt(HEAD_DIM))
        scores = dot_last(query, rows[:, width + lo : width + hi]) + penalty
        largest = jnp.max(scores, axis=-1, keepdims=True)
        weights = jnp.exp(scores - largest)
        total = jnp.sum(weights, axis=-1, keepdims=True)
        values = rows[:, 2 * width + lo : 2 * width + hi]
        parts.append((dot(weights.astype(BF16), values) / total).astype(BF16))
        total_ref[:, head : head + 1] = largest + jnp.log(total)
    context = jnp.concatenate(parts, axis=1)
    context_ref[...] = context
    wide, tail = pack_rows(context, seqlen // 2)
    packed_ref[0, :seqlen] = wide
    packed_ref[0, seqlen:] = tail


def attend(tokens, norm_rows, flat_qkv, bias_row, seg_cols, seg_rows, live_rows):
    tok_count, model_width = tokens.shape
    seq_count, seqlen = seg_rows.shape[0], seg_rows.shape[2]
    wide = flat_qkv.shape[1]
    width = wide // 3
    step = lambda i: (i, 0)
    fixed = lambda i: (0, 0)
    deep = lambda i: (i, 0, 0)
    return pl.pallas_call(
        attend_kernel,
        grid=(seq_count,),
        in_specs=[
            pl.BlockSpec((seqlen, model_width), step),
            pl.BlockSpec((8, model_width), fixed),
            pl.BlockSpec((model_width, wide), fixed),
            pl.BlockSpec((1, wide), fixed),
            pl.BlockSpec((1, seqlen, 1), deep),
            pl.BlockSpec((1, 1, seqlen), deep),
            pl.BlockSpec((1, 1, seqlen), deep),
        ],
        out_specs=[
            pl.BlockSpec((seqlen, model_width), step),
            pl.BlockSpec((seqlen, wide), step),
            pl.BlockSpec((seqlen, width), step),
            pl.BlockSpec((1, seqlen + seqlen // 2, LANES), deep),
            pl.BlockSpec((seqlen, LANES), step),
        ],
        out_shape=[
            shaped((tok_count, model_width), BF16),
            shaped((tok_count, wide), BF16),
            shaped((tok_count, width), BF16),
            shaped((seq_count, seqlen + seqlen // 2, LANES), BF16),
            shaped((tok_count, LANES), F32),
        ],
        compiler_params=params(),
        cost_estimate=cost(4e9, 1e7),
        name="attend",
    )(tokens, norm_rows, flat_qkv, bias_row, seg_cols, seg_rows, live_rows)


def table_kernel(experts, capacity, stride, half, chunk, prio_ref, rows_ref, cot_ref, ids_ref, out_ref):
    tok_count = rows_ref.shape[1]
    numbers = lax.broadcasted_iota(jnp.int32, (experts, 1), 0)

    def hot(rows):
        live = rows[2:3] > 0
        first = jnp.where((rows[0:1] == numbers) & live, 1.0, 0.0)
        second = jnp.where((rows[1:2] == numbers) & live, 1.0, 0.0)
        return first, second

    rank_row = rows_ref[3:4]
    counts = jnp.zeros((2 * experts, tok_count), F32)
    for start in range(0, tok_count, chunk):
        first, second = hot(rows_ref[:, start : start + chunk])
        earlier = jnp.where(prio_ref[start : start + chunk] < rank_row, 1.0, 0.0).astype(BF16)
        counts = counts + dot(jnp.concatenate([first, second], axis=0).astype(BF16), earlier)
    first, second = hot(rows_ref[...])
    total = jnp.sum(first, axis=1, keepdims=True)
    places = [
        jnp.sum(first * counts[:experts], axis=0, keepdims=True),
        jnp.sum(second * (counts[experts:] + total), axis=0, keepdims=True),
    ]
    ids = []
    for pick in range(2):
        place = places[pick].astype(jnp.int32)
        kept = (place < capacity) & (rows_ref[2:3] > 0)
        ids.append(jnp.where(kept, rows_ref[pick : pick + 1] * stride + place, -1))
        ids_ref[pick : pick + 1] = ids[pick]
    ids_ref[2:8] = jnp.full((6, tok_count), -1, jnp.int32)

    def one(expert, carry):
        slots = expert * stride + lax.broadcasted_iota(jnp.int32, (stride, 1), 0)
        hit = (ids_ref[0:1] == slots) | (ids_ref[1:2] == slots)
        block = dot(jnp.where(hit, 1.0, 0.0).astype(BF16), cot_ref[...]).astype(BF16)
        wide, tail = pack_rows(block, half)
        out_ref[expert, :stride] = wide
        out_ref[expert, stride:] = tail
        return carry

    lax.fori_loop(0, experts, one, 0)


def tables(prio_col, rows, cotangent, experts, capacity, stride, half, chunk):
    tok_count = rows.shape[1]
    return pl.pallas_call(
        partial(table_kernel, experts, capacity, stride, half, chunk),
        in_specs=[whole()] * 3,
        out_specs=[whole()] * 2,
        out_shape=[
            shaped((8, tok_count), jnp.int32),
            shaped((experts, stride + half, LANES), BF16),
        ],
        compiler_params=params(),
        cost_estimate=cost(1e10, 1e7),
        name="tables",
    )(prio_col, rows, cotangent)


def gelu_parts(pre):
    root = math.sqrt(2.0 / math.pi)
    square = pre * pre
    wave = jnp.tanh(root * (pre + 0.044715 * pre * square))
    half_sum = 0.5 * (1.0 + wave)
    slope = half_sum + 0.5 * pre * (1.0 - wave * wave) * (
        root * (1.0 + 3.0 * 0.044715 * square)
    )
    return pre * half_sum, slope


def greet(peers):
    barrier = pltpu.get_barrier_semaphore()
    me = lax.axis_index("exp")
    here = lax.axis_index("head")

    def call(step, carry):
        other = lax.rem(me + step, peers)
        pl.semaphore_signal(barrier, inc=1, device_id=(other, here), device_id_type=MESH)
        return carry

    lax.fori_loop(1, peers, call, 0)
    return barrier


def forward_kernel(
    experts, stride, seq_count, head_parts,
    gathered_ref, tokens_ref, vectors_ref, out_weight_ref, router_ref, rows_ref, ids_ref,
    up_ref, up_bias_ref, down_ref, down_bias_ref,
    residual_ref, own_residual_ref, own_second_ref, gates_ref, arrived_ref, hidden_ref, result_ref,
    gate_col_ref, context_scr, second_scr, logit_scr, send_scr, gate_send, gate_recv,
    send_sem, recv_sem, gate_send_sem, gate_recv_sem,
):
    me = lax.axis_index("exp")
    here = lax.axis_index("head")
    barrier = greet(experts)
    tok_count = tokens_ref.shape[0]
    seqlen = tok_count // seq_count
    tok_part = tok_count // head_parts
    for seq in range(seq_count):
        span = slice(seq * seqlen, (seq + 1) * seqlen)
        unpack_rows(lambda z: gathered_ref[z, seq], context_scr, head_parts, seqlen, seqlen // 2)
        residual = (
            tokens_ref[span].astype(F32)
            + dot(context_scr[...], out_weight_ref[...])
            + vectors_ref[0:1]
        )
        residual_ref[span] = residual
        normal, ignored = standard(residual)
        second = (normal * vectors_ref[1:2] + vectors_ref[2:3]).astype(BF16)
        second_scr[span] = second
        logit_scr[:, span] = dot(second, router_ref[...]).T[:experts]
    own = pl.ds(pl.multiple_of(here * tok_part, tok_part), tok_part)
    own_residual_ref[...] = residual_ref[own]
    own_second_ref[...] = second_scr[own]

    logits = logit_scr[...]
    powers = jnp.exp(logits - jnp.max(logits, axis=0, keepdims=True))
    chances = powers / jnp.sum(powers, axis=0, keepdims=True)
    numbers = lax.broadcasted_iota(jnp.int32, (experts, 1), 0)
    for pick in range(2):
        chosen = jnp.where(rows_ref[pick : pick + 1] == numbers, chances, 0.0)
        gate = jnp.where(ids_ref[pick : pick + 1] >= 0, jnp.sum(chosen, axis=0, keepdims=True), 0.0)
        gates_ref[pick : pick + 1] = gate
    gates_ref[2:8] = jnp.zeros((6, tok_count), F32)
    pl.semaphore_wait(barrier, experts - 1)

    def copies(target, step):
        to = dict(device_id=(target, here), device_id_type=MESH)
        return (
            pltpu.make_async_remote_copy(
                src_ref=send_scr.at[step],
                dst_ref=arrived_ref.at[me],
                send_sem=send_sem.at[step],
                recv_sem=recv_sem.at[step],
                **to,
            ),
            pltpu.make_async_remote_copy(
                src_ref=gate_send.at[step],
                dst_ref=gate_recv.at[me],
                send_sem=gate_send_sem.at[step],
                recv_sem=gate_recv_sem.at[step],
                **to,
            ),
        )

    def fill(target):
        slots = target * stride + lax.broadcasted_iota(jnp.int32, (stride, 1), 0)
        first = ids_ref[0:1] == slots
        second = ids_ref[1:2] == slots
        block = dot(jnp.where(first | second, 1.0, 0.0).astype(BF16), second_scr[...]).astype(BF16)
        gate = jnp.sum(
            jnp.where(first, gates_ref[0:1], jnp.where(second, gates_ref[1:2], 0.0)),
            axis=1,
            keepdims=True,
        )
        return block, jnp.broadcast_to(gate, (stride, LANES)).T[:8]

    def send(step, carry):
        target = lax.rem(me + step, experts)
        block, gate = fill(target)
        send_scr[step] = block
        gate_send[step] = gate
        for copy in copies(target, step):
            copy.start()
        return carry

    lax.fori_loop(1, experts, send, 0)
    block, gate = fill(me)
    arrived_ref[me] = block
    gate_recv[me] = gate

    def work(source):
        pre = dot(arrived_ref[source], up_ref[...]) + up_bias_ref[...]
        hidden = gelu_parts(pre)[0].astype(BF16)
        hidden_ref[source] = hidden
        result_ref[source] = (dot(hidden, down_ref[...]) + down_bias_ref[...]).astype(BF16)

    work(me)

    def receive(step, carry):
        source = lax.rem(me + experts - step, experts)
        wide, narrow = copies(source, step)
        wide.wait_recv()
        narrow.wait_recv()
        work(source)
        return carry

    lax.fori_loop(1, experts, receive, 0)

    def finish(step, carry):
        for copy in copies(lax.rem(me + step, experts), step):
            copy.wait_send()
        return carry

    lax.fori_loop(1, experts, finish, 0)
    lane = lax.broadcasted_iota(jnp.int32, (LANES, stride), 0)
    square = jnp.zeros((LANES, stride), F32)
    for source in range(experts):
        square = jnp.where(lane == source, gate_recv[source, 0:1], square)
    gate_col_ref[...] = square.T


def forward(
    gathered, tokens, vectors, out_weight, router, rows, ids, up, up_bias, down, down_bias,
    experts, stride, seq_count, head_parts,
):
    tok_count, model_width = tokens.shape
    tok_part = tok_count // head_parts
    seqlen = tok_count // seq_count
    return pl.pallas_call(
        partial(forward_kernel, experts, stride, seq_count, head_parts),
        in_specs=[whole()] * 11,
        out_specs=[whole()] * 8,
        out_shape=[
            shaped((tok_count, model_width), F32),
            shaped((tok_part, model_width), F32),
            shaped((tok_part, model_width), BF16),
            shaped((8, tok_count), F32),
            shaped((experts, stride, model_width), BF16),
            shaped((experts, stride, up.shape[1]), BF16),
            shaped((experts, stride, model_width), BF16),
            shaped((stride, LANES), F32),
        ],
        scratch_shapes=[
            pltpu.VMEM((seqlen, model_width), BF16),
            pltpu.VMEM((tok_count, model_width), BF16),
            pltpu.VMEM((experts, tok_count), F32),
            pltpu.VMEM((experts, stride, model_width), BF16),
            pltpu.VMEM((experts, 8, stride), F32),
            pltpu.VMEM((experts, 8, stride), F32),
            pltpu.SemaphoreType.DMA((experts,)),
            pltpu.SemaphoreType.DMA((experts,)),
            pltpu.SemaphoreType.DMA((experts,)),
            pltpu.SemaphoreType.DMA((experts,)),
        ],
        compiler_params=params(collective_id=0, has_side_effects=True),
        cost_estimate=cost(8e10, 1e8),
        name="forward",
    )(gathered, tokens, vectors, out_weight, router, rows, ids, up, up_bias, down, down_bias)


def backward_kernel(
    experts, stride, half, head_parts, chunk,
    arrived_hbm, hidden_hbm, result_hbm, cot_hbm, gate_col_ref, ids_ref, up_ref, up_bias_ref, down_ref,
    sums_ref, grad_up_ref, grad_up_bias_ref, grad_down_ref, grad_down_bias_ref,
    rows_scr, result_scr, cot_scr, cot_wide, hidden_scr, pre_grad_scr, out_grad_scr,
    send_scr, recv_scr, gate_send, gate_recv, total_scr, gate_total,
    load_sem, send_sem, recv_sem, gate_send_sem, gate_recv_sem,
):
    me = lax.axis_index("exp")
    here = lax.axis_index("head")
    barrier = greet(experts)
    tok_count = ids_ref.shape[0]
    model_width = up_ref.shape[0]

    def loads(step):
        home = lax.rem(me + step, experts)
        slot = lax.rem(step, 2)
        return (
            pltpu.make_async_copy(arrived_hbm.at[home], rows_scr.at[slot], load_sem.at[slot, 0]),
            pltpu.make_async_copy(result_hbm.at[home], result_scr.at[slot], load_sem.at[slot, 1]),
            pltpu.make_async_copy(cot_hbm.at[:, home], cot_scr.at[slot], load_sem.at[slot, 2]),
        )

    def copies(target, step):
        to = dict(device_id=(target, here), device_id_type=MESH)
        return (
            pltpu.make_async_remote_copy(
                src_ref=send_scr.at[step],
                dst_ref=recv_scr.at[me],
                send_sem=send_sem.at[step],
                recv_sem=recv_sem.at[step],
                **to,
            ),
            pltpu.make_async_remote_copy(
                src_ref=gate_send.at[step],
                dst_ref=gate_recv.at[me],
                send_sem=gate_send_sem.at[step],
                recv_sem=gate_recv_sem.at[step],
                **to,
            ),
        )

    for copy in loads(1):
        copy.start()
    grad_up_ref[...] = jnp.zeros_like(grad_up_ref)
    grad_down_ref[...] = jnp.zeros_like(grad_down_ref)
    grad_up_bias_ref[...] = jnp.zeros_like(grad_up_bias_ref)
    grad_down_bias_ref[...] = jnp.zeros_like(grad_down_bias_ref)
    total_scr[...] = jnp.zeros_like(total_scr)
    gate_total[...] = jnp.zeros_like(gate_total)
    pl.semaphore_wait(barrier, experts - 1)

    def work(step):
        home = lax.rem(me + step, experts)
        slot = lax.rem(step, 2)
        for copy in loads(step):
            copy.wait()
        unpack_rows(lambda z: cot_scr[slot, z], cot_wide, head_parts, stride, half)
        out_rows = cot_wide[...].astype(F32)
        pre = dot(rows_scr[slot], up_ref[...]) + up_bias_ref[...]
        slope = gelu_parts(pre)[1]
        lane = lax.broadcasted_iota(jnp.int32, (stride, LANES), 1)
        gate = jnp.sum(jnp.where(lane == home, gate_col_ref[...], 0.0), axis=1, keepdims=True)
        out_grad = (gate * out_rows).astype(BF16)
        out_grad_scr[step] = out_grad
        grad_down_bias_ref[0:1] += jnp.sum(out_grad.astype(F32), axis=0, keepdims=True)
        pre_grad = (dot_last(out_grad, down_ref[...]) * slope).astype(BF16)
        pre_grad_scr[step] = pre_grad
        grad_up_bias_ref[0:1] += jnp.sum(pre_grad.astype(F32), axis=0, keepdims=True)
        gate_grad = jnp.sum(result_scr[slot].astype(F32) * out_rows, axis=1, keepdims=True)
        return (
            dot_last(pre_grad, up_ref[...]).astype(BF16),
            jnp.broadcast_to(gate_grad, (stride, LANES)).T[:8],
        )

    def send(step, carry):
        for copy in loads(lax.rem(step + 1, experts)):
            copy.start()
        block, gate = work(step)
        send_scr[step] = block
        gate_send[step] = gate
        for copy in copies(lax.rem(me + step, experts), step):
            copy.start()
        return carry

    lax.fori_loop(1, experts, send, 0)
    block, gate = work(0)
    recv_scr[me] = block
    gate_recv[me] = gate

    def row_loads(step):
        home = lax.rem(me + step, experts)
        slot = lax.rem(step, 2)
        return (
            pltpu.make_async_copy(arrived_hbm.at[home], rows_scr.at[slot], load_sem.at[slot, 0]),
            pltpu.make_async_copy(hidden_hbm.at[home], hidden_scr.at[slot], load_sem.at[slot, 1]),
        )

    def weigh(step):
        slot = lax.rem(step, 2)
        for copy in row_loads(step):
            copy.wait()
        grad_up_ref[...] += dot_first(rows_scr[slot], pre_grad_scr[step])
        grad_down_ref[...] += dot_first(hidden_scr[slot], out_grad_scr[step])

    def weigh_some(step, carry):
        for copy in row_loads(step + 1):
            copy.start()
        weigh(step)
        return carry

    for copy in row_loads(0):
        copy.start()
    lax.fori_loop(0, experts - 1, weigh_some, 0)
    weigh(experts - 1)

    def gather(source):
        slots = source * stride + lax.broadcasted_iota(jnp.int32, (1, stride), 1)
        lane = lax.broadcasted_iota(jnp.int32, (chunk, LANES), 1)

        def part(index, carry):
            span = pl.ds(pl.multiple_of(index * chunk, chunk), chunk)
            hit = (ids_ref[span, 0:1] == slots) | (ids_ref[span, 1:2] == slots)
            total_scr[span] += dot(jnp.where(hit, 1.0, 0.0).astype(BF16), recv_scr[source])
            gate = jnp.sum(jnp.where(hit, gate_recv[source, 0:1], 0.0), axis=1, keepdims=True)
            gate_total[span] = jnp.where(lane == source, gate, gate_total[span])
            return carry

        lax.fori_loop(0, tok_count // chunk, part, 0)

    gather(me)

    def receive(step, carry):
        source = lax.rem(me + experts - step, experts)
        for copy in copies(source, step):
            copy.wait_recv()
        gather(source)
        return carry

    lax.fori_loop(1, experts, receive, 0)

    def finish(step, carry):
        for copy in copies(lax.rem(me + step, experts), step):
            copy.wait_send()
        return carry

    lax.fori_loop(1, experts, finish, 0)
    sums_ref[:, :model_width] = total_scr[...].astype(BF16)
    sums_ref[:, model_width:] = gate_total[...].astype(BF16)


def backward(
    arrived, hidden, result, cot_rows, gate_col, id_cols, up, up_bias, down, half, head_parts, chunk
):
    experts, stride, model_width = arrived.shape
    tok_count = id_cols.shape[0]
    inner = up.shape[1]
    rows = (experts, stride, model_width)
    return pl.pallas_call(
        partial(backward_kernel, experts, stride, half, head_parts, chunk),
        in_specs=[anywhere()] * 4 + [whole()] * 5,
        out_specs=[whole()] * 5,
        out_shape=[
            shaped((tok_count, model_width + LANES), BF16),
            shaped((model_width, inner), F32),
            shaped((8, inner), F32),
            shaped((inner, model_width), F32),
            shaped((8, model_width), F32),
        ],
        scratch_shapes=[
            pltpu.VMEM((2, stride, model_width), BF16),
            pltpu.VMEM((2, stride, model_width), BF16),
            pltpu.VMEM((2, head_parts, stride + half, LANES), BF16),
            pltpu.VMEM((stride, model_width), BF16),
            pltpu.VMEM((2, stride, inner), BF16),
            pltpu.VMEM((experts, stride, inner), BF16),
            pltpu.VMEM(rows, BF16),
            pltpu.VMEM(rows, BF16),
            pltpu.VMEM(rows, BF16),
            pltpu.VMEM((experts, 8, stride), F32),
            pltpu.VMEM((experts, 8, stride), F32),
            pltpu.VMEM((tok_count, model_width), F32),
            pltpu.VMEM((tok_count, LANES), F32),
            pltpu.SemaphoreType.DMA((2, 3)),
            pltpu.SemaphoreType.DMA((experts,)),
            pltpu.SemaphoreType.DMA((experts,)),
            pltpu.SemaphoreType.DMA((experts,)),
            pltpu.SemaphoreType.DMA((experts,)),
        ],
        compiler_params=params(collective_id=1, has_side_effects=True),
        cost_estimate=cost(8e10, 1e8),
        name="backward",
    )(arrived, hidden, result, cot_rows, gate_col, id_cols, up, up_bias, down)


def middle_kernel(
    experts, sums_ref, residual_ref, second_ref, cot_ref, router_ref, vectors_ref,
    grad_ref, half_ref, router_grad_ref, rows_ref,
):
    model_width = residual_ref.shape[1]
    second = second_ref[...]
    lane = lax.broadcasted_iota(jnp.int32, (second.shape[0], LANES), 1)
    logits = jnp.where(lane < experts, dot(second, router_ref[...]), NEGATIVE)
    powers = jnp.exp(logits - jnp.max(logits, axis=1, keepdims=True))
    chances = powers / jnp.sum(powers, axis=1, keepdims=True)
    route_grad = sums_ref[:, model_width:].astype(F32)
    logit_grad = (
        chances * (route_grad - jnp.sum(chances * route_grad, axis=1, keepdims=True))
    ).astype(BF16)
    router_grad_ref[...] = dot_first(second, logit_grad)
    grad = sums_ref[:, :model_width].astype(F32) + dot_last(logit_grad, router_ref[...])
    normal, scale = standard(residual_ref[...])
    rows_ref[0:1] = jnp.sum(grad * normal, axis=0, keepdims=True)
    rows_ref[1:2] = jnp.sum(grad, axis=0, keepdims=True)
    total = cot_ref[...].astype(F32) + norm_back(grad, vectors_ref[1:2], normal, scale)
    grad_ref[...] = total
    half_ref[...] = total.astype(BF16)
    rows_ref[2:3] = jnp.sum(total, axis=0, keepdims=True)
    rows_ref[3:8] = jnp.zeros((5, model_width), F32)


def middle(sums, residual, second, cot_rows, router, vectors, experts):
    rows, model_width = residual.shape
    return pl.pallas_call(
        partial(middle_kernel, experts),
        in_specs=[whole()] * 6,
        out_specs=[whole()] * 4,
        out_shape=[
            shaped((rows, model_width), F32),
            shaped((rows, model_width), BF16),
            shaped((model_width, LANES), F32),
            shaped((8, model_width), F32),
        ],
        compiler_params=params(),
        cost_estimate=cost(5e9, 1e7),
        name="middle",
    )(sums, residual, second, cot_rows, router, vectors)


def attend_back_kernel(
    grad_ref, context_ref, first_ref, qkv_ref, total_ref, weight_ref, out_weight_ref,
    segc_ref, segr_ref, live_ref,
    first_grad_ref, weight_grad_ref, bias_grad_ref, out_grad_ref,
):
    rows = qkv_ref[...]
    width = rows.shape[1] // 3
    grad = grad_ref[...]
    context_grad = dot_last(grad, out_weight_ref[...]).astype(BF16)
    penalty = mask_penalty(segc_ref[0], segr_ref[0], live_ref[0])
    context = context_ref[...]
    query_parts, key_parts, value_parts = [], [], []
    factor = 1.0 / math.sqrt(HEAD_DIM)
    for head in range(width // HEAD_DIM):
        lo = head * HEAD_DIM
        hi = lo + HEAD_DIM
        query = rows[:, lo:hi] * BF16(factor)
        keys = rows[:, width + lo : width + hi]
        values = rows[:, 2 * width + lo : 2 * width + hi]
        back = context_grad[:, lo:hi]
        weights = jnp.exp(dot_last(query, keys) + penalty - total_ref[:, head : head + 1])
        value_parts.append(dot_first(weights.astype(BF16), back))
        weight_grad = dot_last(back, values)
        inner = jnp.sum(
            back.astype(F32) * context[:, lo:hi].astype(F32), axis=-1, keepdims=True
        )
        score_grad = (weights * (weight_grad - inner)).astype(BF16)
        query_parts.append(dot(score_grad, keys) * factor)
        key_parts.append(dot_first(score_grad, query))
    joined = jnp.concatenate(query_parts + key_parts + value_parts, axis=1).astype(BF16)
    first_grad_ref[...] = dot_last(joined, weight_ref[...]).astype(BF16)
    weight_grad = dot_first(first_ref[...], joined)
    out_grad = dot_first(context, grad)
    bias_grad = jnp.sum(joined.astype(F32), axis=0, keepdims=True)

    @pl.when(pl.program_id(0) == 0)
    def start():
        weight_grad_ref[...] = weight_grad
        out_grad_ref[...] = out_grad
        bias_grad_ref[...] = jnp.broadcast_to(bias_grad, bias_grad_ref.shape)

    @pl.when(pl.program_id(0) > 0)
    def more():
        weight_grad_ref[...] += weight_grad
        out_grad_ref[...] += out_grad
        bias_grad_ref[...] += jnp.broadcast_to(bias_grad, bias_grad_ref.shape)


def attend_back(
    grad, context, first, qkv, totals, flat_qkv, out_weight, seg_cols, seg_rows, live_rows
):
    tok_count, model_width = first.shape
    seq_count, seqlen = seg_rows.shape[0], seg_rows.shape[2]
    wide = flat_qkv.shape[1]
    width = wide // 3
    step = lambda i: (i, 0)
    fixed = lambda i: (0, 0)
    deep = lambda i: (i, 0, 0)
    return pl.pallas_call(
        attend_back_kernel,
        grid=(seq_count,),
        in_specs=[
            pl.BlockSpec((seqlen, model_width), step),
            pl.BlockSpec((seqlen, width), step),
            pl.BlockSpec((seqlen, model_width), step),
            pl.BlockSpec((seqlen, wide), step),
            pl.BlockSpec((seqlen, LANES), step),
            pl.BlockSpec((model_width, wide), fixed),
            pl.BlockSpec((width, model_width), fixed),
            pl.BlockSpec((1, seqlen, 1), deep),
            pl.BlockSpec((1, 1, seqlen), deep),
            pl.BlockSpec((1, 1, seqlen), deep),
        ],
        out_specs=[
            pl.BlockSpec((seqlen, model_width), step),
            pl.BlockSpec((model_width, wide), fixed),
            pl.BlockSpec((8, wide), fixed),
            pl.BlockSpec((width, model_width), fixed),
        ],
        out_shape=[
            shaped((tok_count, model_width), BF16),
            shaped((model_width, wide), F32),
            shaped((8, wide), F32),
            shaped((width, model_width), F32),
        ],
        compiler_params=params(),
        cost_estimate=cost(1e10, 1e7),
        name="attend_back",
    )(grad, context, first, qkv, totals, flat_qkv, out_weight, seg_cols, seg_rows, live_rows)


def last_kernel(grad_ref, tokens_ref, residual_grad_ref, norm_ref, out_ref, rows_ref):
    grad = grad_ref[...].astype(F32)
    normal, scale = standard(tokens_ref[...].astype(F32))
    rows_ref[0:1] = jnp.sum(grad * normal, axis=0, keepdims=True)
    rows_ref[1:2] = jnp.sum(grad, axis=0, keepdims=True)
    rows_ref[2:8] = jnp.zeros((6, grad.shape[1]), F32)
    total = residual_grad_ref[...] + norm_back(grad, norm_ref[0:1], normal, scale)
    out_ref[...] = total.astype(BF16)


def last(grad, tokens, residual_grad, norm_rows):
    rows, model_width = tokens.shape
    return pl.pallas_call(
        last_kernel,
        in_specs=[whole()] * 4,
        out_specs=[whole()] * 2,
        out_shape=[shaped((rows, model_width), BF16), shaped((8, model_width), F32)],
        compiler_params=params(),
        cost_estimate=cost(1e9, 1e7),
        name="last",
    )(grad, tokens, residual_grad, norm_rows)


def combine_kernel(stride, share, chunk, ids_ref, gates_ref, home_ref, residual_ref, out_ref, total_scr):
    experts = home_ref.shape[0]
    total_scr[...] = residual_ref[...] * share

    def one(source, carry):
        slots = source * stride + lax.broadcasted_iota(jnp.int32, (1, stride), 1)

        def part(index, carry):
            span = pl.ds(pl.multiple_of(index * chunk, chunk), chunk)
            weights = jnp.where(
                ids_ref[span, 0:1] == slots,
                gates_ref[span, 0:1],
                jnp.where(ids_ref[span, 1:2] == slots, gates_ref[span, 1:2], 0.0),
            ).astype(BF16)
            total_scr[span] += dot(weights, home_ref[source])
            return carry

        return lax.fori_loop(0, total_scr.shape[0] // chunk, part, carry)

    lax.fori_loop(0, experts, one, 0)
    out_ref[...] = total_scr[...].astype(BF16)


def combine(id_cols, gate_cols, home, residual, stride, share, chunk):
    return pl.pallas_call(
        partial(combine_kernel, stride, share, chunk),
        in_specs=[whole()] * 4,
        out_specs=whole(),
        out_shape=shaped(residual.shape, BF16),
        scratch_shapes=[pltpu.VMEM(residual.shape, F32)],
        compiler_params=params(),
        cost_estimate=cost(1.2e10, 1e7),
        name="combine",
    )(id_cols, gate_cols, home, residual)


def body(
    tokens,
    segments,
    live_mask,
    routes,
    priority,
    norm1_gain,
    norm1_bias,
    qkv_weight,
    qv_bias,
    out_weight,
    out_bias,
    norm2_gain,
    norm2_bias,
    router,
    up_weight,
    up_bias,
    down_weight,
    down_bias,
    cotangent,
):
    tok_count, model_width = tokens.shape
    seq_count, seqlen = segments.shape
    experts = lax.axis_size("exp")
    head_parts = lax.axis_size("head")
    head_index = lax.axis_index("head")
    quarter = model_width // head_parts
    tok_part = tok_count // head_parts
    capacity = (21 * tok_count + 10 * experts - 1) // (10 * experts)
    stride = round_up(capacity, 16)
    half = round_up(stride // 2, 16)
    local_width = qkv_weight.shape[2]

    def vector_rows(*vectors):
        rows = [v.astype(F32).reshape(1, -1) for v in vectors]
        rows.append(jnp.zeros((8 - len(rows), model_width), F32))
        return jnp.concatenate(rows, axis=0)

    norm_rows = vector_rows(norm1_gain, norm1_bias)
    vectors = vector_rows(out_bias, norm2_gain, norm2_bias)
    flat_qkv = qkv_weight.reshape(model_width, 3 * local_width)
    bias_row = jnp.concatenate(
        [qv_bias[0], jnp.zeros((local_width,), qv_bias.dtype), qv_bias[1]]
    ).astype(F32)[None]
    router_wide = jnp.pad(router, ((0, 0), (0, LANES - experts)))
    seg_rows = segments.reshape(seq_count, 1, seqlen)
    live_rows = live_mask.reshape(seq_count, 1, seqlen)
    seg_cols = segments.reshape(seq_count, seqlen, 1)
    down_bias_row = lax.dynamic_update_slice_in_dim(
        jnp.zeros((1, model_width), F32), down_bias.astype(F32), head_index * quarter, 1
    )
    up, down = up_weight[0], down_weight[0]
    up_bias_row = up_bias.astype(F32)

    out_full_weight = lax.all_gather(out_weight, "head", axis=0, tiled=True)
    first, qkv, context, packed, totals = attend(
        tokens, norm_rows, flat_qkv, bias_row, seg_cols, seg_rows, live_rows
    )
    gathered = lax.all_gather(packed, "head", axis=0)

    int_rows = jnp.concatenate(
        [
            routes.T,
            live_mask.reshape(1, tok_count),
            priority,
            jnp.zeros((4, tok_count), jnp.int32),
        ],
        axis=0,
    )
    ids, cot_slots = tables(
        priority.reshape(tok_count, 1), int_rows, cotangent, experts, capacity, stride, half, seqlen
    )
    id_cols = ids.T
    cot_moved = lax.all_to_all(cot_slots, "exp", split_axis=0, concat_axis=0, tiled=True)
    cot_rows = lax.all_gather(cot_moved, "head", axis=0)
    cot_own = lax.all_to_all(cotangent, "head", split_axis=0, concat_axis=1, tiled=True)

    residual, own_residual, own_second, gates, arrived, hidden, result, gate_col = forward(
        gathered, tokens, vectors, out_full_weight, router_wide, int_rows, ids,
        up, up_bias_row, down, down_bias_row, experts, stride, seq_count, head_parts,
    )
    sums, grad_up, grad_up_bias, grad_down, grad_down_bias = backward(
        arrived, hidden, result, cot_rows, gate_col, id_cols, up, up_bias_row, down, half, head_parts,
        seqlen,
    )
    own_sums = lax.psum_scatter(sums, "head", scatter_dimension=0, tiled=True)
    residual_grad, residual_half, router_grad, second_rows = middle(
        own_sums, own_residual, own_second, cot_own, router_wide, vectors, experts
    )
    grad_full = lax.all_gather(residual_half, "head", axis=0, tiled=True)

    home_out = lax.all_to_all(result, "exp", split_axis=0, concat_axis=0, tiled=True)
    block_sum = combine(id_cols, gates.T, home_out, residual, stride, 1.0 / head_parts, seqlen)
    block_out = lax.psum_scatter(block_sum, "head", scatter_dimension=1, tiled=True)

    first_grad, qkv_grad, bias_grad, out_grad = attend_back(
        grad_full, context, first, qkv, totals, flat_qkv, out_weight, seg_cols, seg_rows, live_rows
    )
    own_first = lax.psum_scatter(first_grad, "head", scatter_dimension=0, tiled=True)
    own_tokens = lax.dynamic_slice_in_dim(tokens, head_index * tok_part, tok_part, 0)
    own_grad, first_rows = last(own_first, own_tokens, residual_grad, norm_rows)
    grad_tokens = lax.all_gather(own_grad, "head", axis=0, tiled=True).astype(F32)

    small = lax.psum(
        jnp.concatenate([second_rows, first_rows, router_grad[:, :experts].T], axis=0),
        ("exp", "head"),
    )
    qkv_grad, bias_grad, out_grad = lax.psum((qkv_grad, bias_grad[0:1], out_grad), "exp")
    grad_qv_bias = jnp.concatenate(
        [bias_grad[:, :local_width], bias_grad[:, 2 * local_width :]], axis=0
    )
    return (
        block_out,
        grad_tokens,
        small[8],
        small[9],
        qkv_grad.reshape(model_width, 3, local_width),
        grad_qv_bias,
        out_grad,
        small[2],
        small[0],
        small[1],
        small[16 : 16 + experts].T,
        grad_up[None],
        grad_up_bias[0:1],
        grad_down[None],
        lax.dynamic_slice_in_dim(grad_down_bias[0:1], head_index * quarter, quarter, 1),
    )


def solution(mesh):
    in_specs = (
        P("exp", None),
        P("exp", None),
        P("exp", None),
        P("exp", None),
        P("exp", None),
        P(),
        P(),
        P(None, None, "head"),
        P(None, "head"),
        P("head", None),
        P(),
        P(),
        P(),
        P(),
        P("exp", None, "head"),
        P("exp", "head"),
        P("exp", "head", None),
        P("exp", "head"),
        P("exp", "head"),
    )
    out_specs = (
        P("exp", "head"),
        P("exp", None),
        P(),
        P(),
        P(None, None, "head"),
        P(None, "head"),
        P("head", None),
        P(),
        P(),
        P(),
        P(),
        P("exp", None, "head"),
        P("exp", "head"),
        P("exp", "head", None),
        P("exp", "head"),
    )
    return jax.shard_map(body, mesh=mesh, in_specs=in_specs, out_specs=out_specs, check_vma=False)
```

time: 829 us -> 835 us (level)
  Pallas kernels: 0 us -> 228 us
  matrix products: 195 us -> 0 us
  waiting for transfers between devices: 274 us -> 449 us
  blocking collectives: 144 us -> 61.9 us
  other arithmetic: 63 us -> 6 us
  local copies, waits for them, and re-layouts: 103 us -> 63.1 us
  starting transfers between devices: 27.3 us -> 5.46 us
    pallas_call x0 -> x8, Pallas kernels: none -> 228 us  [the longest x1 81.8 us: forward(): pl.pallas_call(partial(forward_kernel, experts, stride, seq_count, head_p...]
    dot_general x43 -> x0, matrix products: 195 us -> none  [the longest x2 26 us: to_slots(): jnp.dot(onehot.astype(jnp.bfloat16), rows, preferred_element_type=jnp.flo...]
    all_gather x4, waiting for transfers between devices: 46.5 us -> 171 us  [the longest x1 61.3 us: body(): grad_full = lax.all_gather(residual_half, 'head', axis=0, tiled=True)]
    all_to_all x6 -> x1, waiting for transfers between devices: 132 us -> 13.1 us  [body(): lax.all_to_all(result, 'exp', split_axis=0, concat_axis=0, tiled=True)]
    psum x1 -> x2, waiting for transfers between devices: 53.6 us -> 122 us  [the longest x1 66.9 us: body(): lax.psum((qkv_grad, bias_grad[0:1], out_grad), 'exp')]
    psum x3 -> x1, blocking collectives: 76.4 us -> 12.1 us  [body(): lax.psum((qkv_grad, bias_grad[0:1], out_grad), 'exp')]
    reduce_scatter x2, waiting for transfers between devices: 29 us -> 90 us  [the longest x1 46.3 us: body(): own_sums = lax.psum_scatter(sums, 'head', scatter_dimension=0, tiled=True)]
    unnamed x10 -> x11, waiting for transfers between devices: 13.4 us -> 52.9 us
  transfers between devices with their start and end apart: 15 -> 11, of which waited for: 8 -> 10; matrix products, arithmetic and copies ran while one was open for 34% -> 4% of each run, Pallas kernels for 0% -> 16%
where the time goes in v2:
time: 835 us; the launch traced here: 828 us
  waiting for transfers between devices  449 us (54%)
  Pallas kernels  228 us (27%)
  local copies, waits for them, and re-layouts  63.1 us (8%)
  blocking collectives  61.9 us (7%)
  between operations  14.8 us (2%)
    pallas_call x1, Pallas kernels, forward(): pl.pallas_call(partial(forward_kernel, experts, stride, seq_count, head_p...  81.8 us
    pallas_call x1, Pallas kernels, backward(): pl.pallas_call(partial(backward_kernel, experts, stride, half, head_parts...  71.3 us
    psum x1, waiting for transfers between devices, body(): lax.psum((qkv_grad, bias_grad[0:1], out_grad), 'exp')  66.9 us
    all_gather x1, waiting for transfers between devices, body(): grad_full = lax.all_gather(residual_half, 'head', axis=0, tiled=True)  61.3 us
    all_gather x1, waiting for transfers between devices, body(): lax.all_gather(own_grad, 'head', axis=0, tiled=True).astype(F32)  56.6 us
    psum x1, waiting for transfers between devices, body(): lax.psum(jnp.concatenate([second_rows, first_rows, router_grad[:, :expert...  55.1 us
    unnamed x11, waiting for transfers between devices  52.9 us
    reduce_scatter x1, waiting for transfers between devices, body(): own_sums = lax.psum_scatter(sums, 'head', scatter_dimension=0, tiled=True)  46.3 us
  transfers between devices with their start and end apart: 11, of which 10 were waited for; matrix products, arithmetic and copies ran while one was open for 4% of the time, Pallas kernels for 16%

profile of v2, /device:TPU:0, one launch (start us, length us, event | category | flops | bytes accessed | tf_op | source)
XLA Modules:
  0.0 828.2 jit_solution(13386000329343803115)
XLA Ops:
  12.9 13.1 %attend.1 = (bf16[1728,768]{1,0:T(8,128)(2,1)}, bf16[1728,576]{1,0:T(8,128)(2,1)}, bf16[1728,192]{1,0:T(8,128)(2,1)S(1)}, bf16[3,864,128]{2,1,0:T(8,128)(2,1)}, f32[1728,128]{1,0:T(8,128)S(1)}) custom-call(bf16[1728,768]{1,0:T(8,128)(2,1)} %tokens_ref.3, f32[8,768]{1,0:T(8,128)S(1)} %maximum_maximum_fusion.norm_ref, bf16[768,576]{1,0:T(8,128)(2,1)S(1)} %copy.60.weight_ref, ...), custom_call_target="tpu_custom_call" | custom-call | flops 4000000000 | bytes 10000000 | tf_op jit(solution)/shard_map/attend/pallas_call | solution.py:139
  30.9 8.0 tables.1
  39.6 24.8 %all_to_all.29 = bf16[8,704,128]{2,1,0:T(8,128)(2,1)} all-to-all(bf16[8,704,128]{2,1,0:T(8,128)(2,1)S(1)} %get-tuple-element.52), channel_id=1, replica_groups=mesh['exp'=8,'head'=4] {'exp'}, dimensions={0} | all-to-all | bytes 2883584 | tf_op jit(solution)/shard_map/all_to_all | solution.py:873
  65.6 33.8 %all-gather.14.cloned.1.call-done = bf16[12,864,128]{2,1,0:T(8,128)(2,1)} async-done(((bf16[3,864,128]{2,1,0:T(8,128)(2,1)}), bf16[12,864,128]{2,1,0:T(8,128)(2,1)}) %all-gather.14.cloned.1.call-update) | async-done | bytes 2654224 | tf_op jit(solution)/shard_map/all_gather | solution.py:858
  103.2 81.8 %forward.1 = (f32[1728,768]{1,0:T(8,128)}, f32[432,768]{1,0:T(8,128)S(1)}, bf16[432,768]{1,0:T(8,128)(2,1)S(1)}, f32[8,1728]{1,0:T(8,128)S(1)}, bf16[8,464,768]{...) custom-call(bf16[4,3,864,128]{3,2,1,0:T(8,128)(2,1)} %bitcast.41, ...), custom_call_target="tpu_custom_call" | custom-call | flops 80000000000 | bytes 100000000 | tf_op jit(solution)/shard_map/forward/pallas_call | solution.py:379
  187.0 19.5 %all-gather.16.cloned.1.call-done = bf16[32,704,128]{2,1,0:T(8,128)(2,1)} async-done(((bf16[8,704,128]{2,1,0:T(8,128)(2,1)}), bf16[32,704,128]{2,1,0:T(8,128)(2,1)}) %all-gather.16.cloned.1.call-update) | async-done | bytes 5767184 | tf_op jit(solution)/shard_map/all_gather | solution.py:874
  209.1 71.3 %backward.1 = (bf16[1728,896]{1,0:T(8,128)(2,1)}, f32[768,768]{1,0:T(8,128)S(1)}, f32[8,768]{1,0:T(8,128)S(1)}, f32[768,768]{1,0:T(8,128)}, f32[8,768]{1,0:T(8,128)S(1)}) custom-call(bf16[8,464,768]{2,1,0:T(8,128)(2,1)} %get-tuple-element.50.arrived_hbm, bf16[8,464,768]{2,1,0:T(8,128)(2,1)} %get-tuple-element.51.hidden_hbm, ...), custom_call_target="tpu_custom_call" | custom-call | flops 80000000000 | bytes 100000000 | tf_op jit(solution)/shard_map/backward/pallas_call | solution.py:569
  286.2 25.0 %all_to_all.30 = bf16[4,432,192]{1,2,0:T(8,128)(2,1)} all-to-all(bf16[4,432,192]{1,2,0:T(8,128)(2,1)S(1)} %copy.64), channel_id=1, replica_groups=mesh['exp'=8,'head'=4] {'head'}, dimensions={0} | all-to-all | bytes 1327104 | tf_op jit(solution)/shard_map/all_to_all | solution.py:875
  312.6 46.3 %reduce-scatter.6.cloned.1.call-done.sums_ref = bf16[432,896]{1,0:T(8,128)(2,1)} async-done(((bf16[1728,896]{1,0:T(8,128)(2,1)}), bf16[432,896]{1,0:T(8,128)(2,1)}) %reduce-scatter.6.cloned.1.call-update) | async-done | bytes 774160 | tf_op jit(solution)/shard_map/reduce_scatter | solution.py:885
  363.4 2.9 middle.1
  368.2 61.3 %all-gather.10.cloned.1.call-done.grad_ref = bf16[1728,768]{1,0:T(8,128)(2,1)} async-done(((bf16[432,768]{1,0:T(8,128)(2,1)}), bf16[1728,768]{1,0:T(8,128)(2,1)}) %all-gather.10.cloned.1.call-update) | async-done | bytes 2654224 | tf_op jit(solution)/shard_map/all_gather | solution.py:889
  432.8 22.0 %attend_back.1 = (bf16[1728,768]{1,0:T(8,128)(2,1)}, f32[768,576]{1,0:T(8,128)}, f32[8,576]{1,0:T(8,128)S(1)}, f32[192,768]{1,0:T(8,128)}) custom-call(bf16[1728,768]{1,0:T(8,128)(2,1)} %all-gather.10.cloned.1.call-done.grad_ref, bf16[1728,192]{1,0:T(8,128)(2,1)S(1)} %copy-done.34, bf16[1728,768]{1,0:T(8,128)(2,1)} %get-tuple-element.59.first_ref, ...), custom_call_target="tpu_custom_call" | custom-call | flops 10000000000 | bytes 10000000 | tf_op jit(solution)/shard_map/attend_back/pallas_call | solution.py:708
  455.5 4.9 all-to-all-start
  463.3 43.7 %reduce-scatter.8.cloned.1.call-done.grad_ref = bf16[432,768]{1,0:T(8,128)(2,1)} async-done(((bf16[1728,768]{1,0:T(8,128)(2,1)}), bf16[432,768]{1,0:T(8,128)(2,1)}) %reduce-scatter.8.cloned.1.call-update) | async-done | bytes 663568 | tf_op jit(solution)/shard_map/reduce_scatter | solution.py:898
  512.7 13.1 %all-to-all-done.home_ref = bf16[8,464,768]{2,1,0:T(8,128)(2,1)} async-done(((bf16[8,464,768]{2,1,0:T(8,128)(2,1)}), bf16[8,464,768]{2,1,0:T(8,128)(2,1)}, u32[]{:S(2)}, u32[]{:S(2)}) %all-to-all-start) | async-done | bytes 5701664 | tf_op jit(solution)/shard_map/all_to_all | solution.py:891
  527.0 26.6 %combine.1 = bf16[1728,768]{1,0:T(8,128)(2,1)S(1)} custom-call(s32[1728,8]{1,0:T(8,128)S(1)} %bitcast.26, f32[1728,8]{1,0:T(8,128)S(1)} %bitcast.27, bf16[8,464,768]{2,1,0:T(8,128)(2,1)} %all-to-all-done.home_ref, f32[1728,768]{1,0:T(8,128)} %get-tuple-element.49.residual_ref), custom_call_target="tpu_custom_call" | custom-call | flops 12000000000 | bytes 10000000 | tf_op jit(solution)/shard_map/combine/pallas_call | solution.py:788
  553.5 4.3 copy.71
  564.5 12.1 %psum.30 = f32[1,576]{1,0:T(1,128)S(1)} all-reduce(f32[1,576]{1,0:T(1,128)S(1)} %slice.47), channel_id=1, replica_groups=mesh['exp'=8,'head'=4] {'exp'}, use_global_device_ids=true, to_apply=%region_5.6 | all-reduce | flops 576 | bytes 4608 | tf_op jit(solution)/shard_map/psum | solution.py:907
  577.2 55.1 %all-reduce.5.cloned.1.call-done = f32[24,768]{1,0:T(8,128)} async-done(((f32[24,768]{1,0:T(8,128)}), f32[24,768]{1,0:T(8,128)}) %all-reduce.5.cloned.1.call-update) | async-done | bytes 73744 | tf_op jit(solution)/shard_map/psum | solution.py:903
  635.2 56.6 %all-gather.12.cloned.1.call-done = bf16[1728,768]{1,0:T(8,128)(2,1)} async-done(((bf16[432,768]{1,0:T(8,128)(2,1)}), bf16[1728,768]{1,0:T(8,128)(2,1)}) %all-gather.12.cloned.1.call-update) | async-done | bytes 2654224 | tf_op jit(solution)/shard_map/all_gather | solution.py:901
  691.8 4.5 convert_element_type.29
  696.3 51.4 %reduce-scatter.10.cloned.1.call-done = bf16[192,1728]{1,0:T(8,128)(2,1)} async-done(((bf16[768,1728]{1,0:T(8,128)(2,1)}), bf16[192,1728]{1,0:T(8,128)(2,1)}) %reduce-scatter.10.cloned.1.call-update) | async-done | bytes 663568
  747.7 66.9 %all-reduce.7.cloned.1.call-done = (f32[768,3,192]{0,2,1:T(8,128)}, f32[192,768]{1,0:T(8,128)}) async-done(((f32[768,3,192]{0,2,1:T(8,128)}, f32[192,768]{1,0:T(8,128)}), (f32[768,3,192]{0,2,1:T(8,128)}, f32[192,768]{1,0:T(8,128)})) %all-reduce.7.cloned.1.call-update) | async-done | bytes 2359312 | tf_op jit(solution)/shard_map/psum | solution.py:907
  814.7 2.9 copy.79
  (186 shorter events, 61.4 us)
Async XLA Ops:
  7.2 58.4 %all-gather.8.cloned.1.call-start = ((), (), s32[]{:S(2)}) async-start(), calls=%async_computation.6 | async-start | bytes 1474560 | tf_op jit(solution)/shard_map/all_gather | solution.py:854
  7.9 91.5 %all-gather.14.cloned.1.call-start = ((), (), s32[]{:S(2)}) async-start(), calls=%async_computation.12 | async-start | bytes 3317760 | tf_op jit(solution)/shard_map/all_gather | solution.py:858
  27.9 178.6 %all-gather.16.cloned.1.call-start = ((), (), s32[]{:S(2)}) async-start(), calls=%async_computation.13 | async-start | bytes 7208960 | tf_op jit(solution)/shard_map/all_gather | solution.py:874
  39.5 25.5 %copy-start.54 = (bf16[768]{0:T(1024)(128)(2,1)S(1)}, bf16[768]{0:T(1024)(128)(2,1)}, u32[]{:S(2)}) copy-start(bf16[768]{0:T(1024)(128)(2,1)} %param.29) | copy-start | bytes 4612
  39.5 25.6 %copy-start.49 = (bf16[768,8]{0,1:T(8,128)(2,1)S(1)}, bf16[768,8]{0,1:T(8,128)(2,1)}, u32[]{:S(2)}) copy-start(bf16[768,8]{0,1:T(8,128)(2,1)} %param.32) | copy-start | bytes 36868
  39.6 25.8 %copy-start.51 = (bf16[1,768]{1,0:T(2,128)(2,1)S(1)}, bf16[1,768]{1,0:T(2,128)(2,1)}, u32[]{:S(2)}) copy-start(bf16[1,768]{1,0:T(2,128)(2,1)} %param.34) | copy-start | bytes 4612
  39.6 25.8 %copy-start.55 = (bf16[1,192]{1,0:T(2,128)(2,1)S(1)}, bf16[1,192]{1,0:T(2,128)(2,1)}, u32[]{:S(2)}) copy-start(bf16[1,192]{1,0:T(2,128)(2,1)} %param.36) | copy-start | bytes 1156
  39.6 59.8 %copy-start.10 = (s32[8,1728]{1,0:T(8,128)S(1)}, s32[8,1728]{1,0:T(8,128)}, u32[]{:S(2)}) copy-start(s32[8,1728]{1,0:T(8,128)} %copy-done.9) | copy-start | bytes 165892
  64.4 294.5 %reduce-scatter.6.cloned.1.call-start = ((), (), s32[]{:S(2)}) async-start(), calls=%async_computation.7 | async-start | bytes 3870720 | tf_op jit(solution)/shard_map/reduce_scatter | solution.py:885
  65.3 119.7 %copy-start.7 = (bf16[768,128]{1,0:T(8,128)(2,1)}, bf16[768,128]{1,0:T(8,128)(2,1)S(1)}, u32[]{:S(2)}) copy-start(bf16[768,128]{1,0:T(8,128)(2,1)S(1)} %pad.4.router_ref) | copy-start | bytes 589828
  65.6 119.4 %copy-start.15 = (f32[8,768]{1,0:T(8,128)}, f32[8,768]{1,0:T(8,128)S(1)}, u32[]{:S(2)}) copy-start(f32[8,768]{1,0:T(8,128)S(1)} %maximum_maximum_fusion.1.vectors_ref) | copy-start | bytes 73732
  281.8 147.7 %all-gather.10.cloned.1.call-start = ((), (), s32[]{:S(2)}) async-start(), calls=%async_computation.8 | async-start | bytes 3317760 | tf_op jit(solution)/shard_map/all_gather | solution.py:889
  284.9 74.0 %copy-start.16 = (f32[8,768]{1,0:T(8,128)S(1)}, f32[8,768]{1,0:T(8,128)}, u32[]{:S(2)}) copy-start(f32[8,768]{1,0:T(8,128)} %copy-done.15) | copy-start | bytes 73732
  363.4 66.2 %copy-start.18 = (s32[3,1,576]{2,1,0:T(1,128)S(1)}, s32[3,1,576]{2,1,0:T(1,128)}, u32[]{:S(2)}) copy-start(s32[3,1,576]{2,1,0:T(1,128)} %copy-done.17) | copy-start | bytes 20740
  363.4 66.2 %copy-start.20 = (s32[3,1,576]{2,1,0:T(1,128)S(1)}, s32[3,1,576]{2,1,0:T(1,128)}, u32[]{:S(2)}) copy-start(s32[3,1,576]{2,1,0:T(1,128)} %copy-done.19) | copy-start | bytes 20740
  368.2 138.9 %reduce-scatter.8.cloned.1.call-start = ((), (), s32[]{:S(2)}) async-start(), calls=%async_computation.9 | async-start | bytes 3317760 | tf_op jit(solution)/shard_map/reduce_scatter | solution.py:898
  455.5 51.5 %copy-start.14 = (f32[8,768]{1,0:T(8,128)S(1)}, f32[8,768]{1,0:T(8,128)}, u32[]{:S(2)}) copy-start(f32[8,768]{1,0:T(8,128)} %copy-done.13) | copy-start | bytes 73732
  455.5 51.5 %copy-start.32 = (f32[432,768]{1,0:T(8,128)S(1)}, f32[432,768]{1,0:T(8,128)}, u32[]{:S(2)}) copy-start(f32[432,768]{1,0:T(8,128)} %copy-done.31) | copy-start | bytes 3981316
  455.5 70.3 %all-to-all-start = ((bf16[8,464,768]{2,1,0:T(8,128)(2,1)}), bf16[8,464,768]{2,1,0:T(8,128)(2,1)}, u32[]{:S(2)}, u32[]{:S(2)}) async-start(bf16[8,464,768]{2,1,0:T(8,128)(2,1)} %get-tuple-element.48.result_hbm), calls=%async_computation | async-start | bytes 11403264 | tf_op jit(solution)/shard_map/all_to_all | solution.py:891
  460.4 171.9 %all-reduce.5.cloned.1.call-start = ((), (), s32[]{:S(2)}) async-start(), calls=%async_computation.11 | async-start | bytes 147456 | tf_op jit(solution)/shard_map/psum | solution.py:903
  510.6 181.2 %all-gather.12.cloned.1.call-start = ((), (), s32[]{:S(2)}) async-start(), calls=%async_computation.10 | async-start | bytes 3317760 | tf_op jit(solution)/shard_map/all_gather | solution.py:901
  511.4 236.3 %reduce-scatter.10.cloned.1.call-start = ((), (), s32[]{:S(2)}) async-start(), calls=%async_computation.14 | async-start | bytes 3440640
  557.8 256.9 %all-reduce.7.cloned.1.call-start = ((), (), s32[]{:S(2)}) async-start(), calls=%async_computation.15 | async-start | bytes 4718592 | tf_op jit(solution)/shard_map/psum | solution.py:907
  696.3 122.0 %copy-start.1 = (f32[768,768]{1,0:T(8,128)S(1)}, f32[768,768]{1,0:T(8,128)}, u32[]{:S(2)}) copy-start(f32[768,768]{1,0:T(8,128)} %copy-done) | copy-start | bytes 7077892
  (43 other events, 213.9 us)
Sparse Core Ops, SparseCore 0:
  9.6 33.1 all-gather.7
  44.9 54.4 all-gather.13
  101.0 105.4 all-gather.15
  281.9 76.9 reduce-scatter.5
  368.3 61.2 all-gather.9
  455.6 51.3 reduce-scatter.7
  514.1 118.1 all-reduce.4
  634.5 57.2 all-gather.11
  694.8 52.8 reduce-scatter.9
  751.8 62.8 all-reduce.6

commit v3 on v2

--- a/solution.py
+++ b/solution.py
@@ -17,7 +17,7 @@
 F32 = jnp.float32
 BF16 = jnp.bfloat16
 MESH = pl.DeviceIdType.MESH
-VMEM_LIMIT = 48 * 1024 * 1024
+VMEM_LIMIT = 54 * 1024 * 1024
 
 
 def round_up(number, step):
@@ -252,11 +252,11 @@
 
 
 def forward_kernel(
-    experts, stride, seq_count, head_parts,
+    experts, stride, half, seq_count, head_parts,
     gathered_ref, tokens_ref, vectors_ref, out_weight_ref, router_ref, rows_ref, ids_ref,
     up_ref, up_bias_ref, down_ref, down_bias_ref,
-    residual_ref, own_residual_ref, own_second_ref, gates_ref, arrived_ref, hidden_ref, result_ref,
-    gate_col_ref, context_scr, second_scr, logit_scr, send_scr, gate_send, gate_recv,
+    own_residual_ref, own_second_ref, own_columns_ref, gates_ref, arrived_ref, hidden_ref, result_ref,
+    gate_col_ref, residual_ref, context_scr, second_scr, logit_scr, send_scr, gate_send, gate_recv,
     send_sem, recv_sem, gate_send_sem, gate_recv_sem,
 ):
     me = lax.axis_index("exp")
@@ -264,7 +264,6 @@
     barrier = greet(experts)
     tok_count = tokens_ref.shape[0]
     seqlen = tok_count // seq_count
-    tok_part = tok_count // head_parts
     for seq in range(seq_count):
         span = slice(seq * seqlen, (seq + 1) * seqlen)
         unpack_rows(lambda z: gathered_ref[z, seq], context_scr, head_parts, seqlen, seqlen // 2)
@@ -278,9 +277,18 @@
         second = (normal * vectors_ref[1:2] + vectors_ref[2:3]).astype(BF16)
         second_scr[span] = second
         logit_scr[:, span] = dot(second, router_ref[...]).T[:experts]
-    own = pl.ds(pl.multiple_of(here * tok_part, tok_part), tok_part)
-    own_residual_ref[...] = residual_ref[own]
-    own_second_ref[...] = second_scr[own]
+    part = seqlen // head_parts
+    for seq in range(seq_count):
+        own = pl.ds(pl.multiple_of(seq * seqlen + here * part, part), part)
+        own_residual_ref[seq] = residual_ref[own]
+        own_second_ref[seq] = second_scr[own]
+    width = residual_ref.shape[1] // head_parts
+    for z in range(head_parts):
+
+        @pl.when(here == z)
+        def columns():
+            own_columns_ref[...] = residual_ref[:, z * width : (z + 1) * width]
+
 
     logits = logit_scr[...]
     powers = jnp.exp(logits - jnp.max(logits, axis=0, keepdims=True))
@@ -342,7 +350,11 @@
         pre = dot(arrived_ref[source], up_ref[...]) + up_bias_ref[...]
         hidden = gelu_parts(pre)[0].astype(BF16)
         hidden_ref[source] = hidden
-        result_ref[source] = (dot(hidden, down_ref[...]) + down_bias_ref[...]).astype(BF16)
+        result = (dot(hidden, down_ref[...]) + down_bias_ref[...]).astype(BF16)
+        for z in range(head_parts):
+            wide, tail = pack_rows(result[:, z * width : (z + 1) * width], half)
+            result_ref[z, source, :stride] = wide
+            result_ref[z, source, stride:] = tail
 
     work(me)
 
@@ -371,26 +383,27 @@
 
 def forward(
     gathered, tokens, vectors, out_weight, router, rows, ids, up, up_bias, down, down_bias,
-    experts, stride, seq_count, head_parts,
+    experts, stride, half, seq_count, head_parts,
 ):
     tok_count, model_width = tokens.shape
-    tok_part = tok_count // head_parts
     seqlen = tok_count // seq_count
+    part = seqlen // head_parts
     return pl.pallas_call(
-        partial(forward_kernel, experts, stride, seq_count, head_parts),
+        partial(forward_kernel, experts, stride, half, seq_count, head_parts),
         in_specs=[whole()] * 11,
         out_specs=[whole()] * 8,
         out_shape=[
-            shaped((tok_count, model_width), F32),
-            shaped((tok_part, model_width), F32),
-            shaped((tok_part, model_width), BF16),
+            shaped((seq_count, part, model_width), F32),
+            shaped((seq_count, part, model_width), BF16),
+            shaped((tok_count, model_width // head_parts), F32),
             shaped((8, tok_count), F32),
             shaped((experts, stride, model_width), BF16),
             shaped((experts, stride, up.shape[1]), BF16),
-            shaped((experts, stride, model_width), BF16),
+            shaped((head_parts, experts, stride + half, LANES), BF16),
             shaped((stride, LANES), F32),
         ],
         scratch_shapes=[
+            pltpu.VMEM((tok_count, model_width), F32),
             pltpu.VMEM((seqlen, model_width), BF16),
             pltpu.VMEM((tok_count, model_width), BF16),
             pltpu.VMEM((experts, tok_count), F32),
@@ -412,8 +425,8 @@
     experts, stride, half, head_parts, chunk,
     arrived_hbm, hidden_hbm, result_hbm, cot_hbm, gate_col_ref, ids_ref, up_ref, up_bias_ref, down_ref,
     sums_ref, grad_up_ref, grad_up_bias_ref, grad_down_ref, grad_down_bias_ref,
-    rows_scr, result_scr, cot_scr, cot_wide, hidden_scr, pre_grad_scr, out_grad_scr,
-    send_scr, recv_scr, gate_send, gate_recv, total_scr, gate_total,
+    rows_scr, result_scr, cot_scr, cot_wide, result_wide, hidden_scr, pre_grad_scr, out_grad_scr,
+    send_scr, recv_scr, gate_send, gate_recv, total_scr,
     load_sem, send_sem, recv_sem, gate_send_sem, gate_recv_sem,
 ):
     me = lax.axis_index("exp")
@@ -427,7 +440,7 @@
         slot = lax.rem(step, 2)
         return (
             pltpu.make_async_copy(arrived_hbm.at[home], rows_scr.at[slot], load_sem.at[slot, 0]),
-            pltpu.make_async_copy(result_hbm.at[home], result_scr.at[slot], load_sem.at[slot, 1]),
+            pltpu.make_async_copy(result_hbm.at[:, home], result_scr.at[slot], load_sem.at[slot, 1]),
             pltpu.make_async_copy(cot_hbm.at[:, home], cot_scr.at[slot], load_sem.at[slot, 2]),
         )
 
@@ -457,7 +470,6 @@
     grad_up_bias_ref[...] = jnp.zeros_like(grad_up_bias_ref)
     grad_down_bias_ref[...] = jnp.zeros_like(grad_down_bias_ref)
     total_scr[...] = jnp.zeros_like(total_scr)
-    gate_total[...] = jnp.zeros_like(gate_total)
     pl.semaphore_wait(barrier, experts - 1)
 
     def work(step):
@@ -466,6 +478,7 @@
         for copy in loads(step):
             copy.wait()
         unpack_rows(lambda z: cot_scr[slot, z], cot_wide, head_parts, stride, half)
+        unpack_rows(lambda z: result_scr[slot, z], result_wide, head_parts, stride, half)
         out_rows = cot_wide[...].astype(F32)
         pre = dot(rows_scr[slot], up_ref[...]) + up_bias_ref[...]
         slope = gelu_parts(pre)[1]
@@ -477,7 +490,7 @@
         pre_grad = (dot_last(out_grad, down_ref[...]) * slope).astype(BF16)
         pre_grad_scr[step] = pre_grad
         grad_up_bias_ref[0:1] += jnp.sum(pre_grad.astype(F32), axis=0, keepdims=True)
-        gate_grad = jnp.sum(result_scr[slot].astype(F32) * out_rows, axis=1, keepdims=True)
+        gate_grad = jnp.sum(result_wide[...].astype(F32) * out_rows, axis=1, keepdims=True)
         return (
             dot_last(pre_grad, up_ref[...]).astype(BF16),
             jnp.broadcast_to(gate_grad, (stride, LANES)).T[:8],
@@ -531,9 +544,13 @@
         def part(index, carry):
             span = pl.ds(pl.multiple_of(index * chunk, chunk), chunk)
             hit = (ids_ref[span, 0:1] == slots) | (ids_ref[span, 1:2] == slots)
-            total_scr[span] += dot(jnp.where(hit, 1.0, 0.0).astype(BF16), recv_scr[source])
+            total_scr[span, :model_width] += dot(
+                jnp.where(hit, 1.0, 0.0).astype(BF16), recv_scr[source]
+            )
             gate = jnp.sum(jnp.where(hit, gate_recv[source, 0:1], 0.0), axis=1, keepdims=True)
-            gate_total[span] = jnp.where(lane == source, gate, gate_total[span])
+            total_scr[span, model_width:] = jnp.where(
+                lane == source, gate, total_scr[span, model_width:]
+            )
             return carry
 
         lax.fori_loop(0, tok_count // chunk, part, 0)
@@ -548,6 +565,7 @@
         return carry
 
     lax.fori_loop(1, experts, receive, 0)
+    sums_ref[...] = total_scr[...].astype(BF16)
 
     def finish(step, carry):
         for copy in copies(lax.rem(me + step, experts), step):
@@ -555,15 +573,13 @@
         return carry
 
     lax.fori_loop(1, experts, finish, 0)
-    sums_ref[:, :model_width] = total_scr[...].astype(BF16)
-    sums_ref[:, model_width:] = gate_total[...].astype(BF16)
 
 
 def backward(
     arrived, hidden, result, cot_rows, gate_col, id_cols, up, up_bias, down, half, head_parts, chunk
 ):
+    tok_count = id_cols.shape[0]
     experts, stride, model_width = arrived.shape
-    tok_count = id_cols.shape[0]
     inner = up.shape[1]
     rows = (experts, stride, model_width)
     return pl.pallas_call(
@@ -579,8 +595,9 @@
         ],
         scratch_shapes=[
             pltpu.VMEM((2, stride, model_width), BF16),
-            pltpu.VMEM((2, stride, model_width), BF16),
             pltpu.VMEM((2, head_parts, stride + half, LANES), BF16),
+            pltpu.VMEM((2, head_parts, stride + half, LANES), BF16),
+            pltpu.VMEM((stride, model_width), BF16),
             pltpu.VMEM((stride, model_width), BF16),
             pltpu.VMEM((2, stride, inner), BF16),
             pltpu.VMEM((experts, stride, inner), BF16),
@@ -589,8 +606,7 @@
             pltpu.VMEM(rows, BF16),
             pltpu.VMEM((experts, 8, stride), F32),
             pltpu.VMEM((experts, 8, stride), F32),
-            pltpu.VMEM((tok_count, model_width), F32),
-            pltpu.VMEM((tok_count, LANES), F32),
+            pltpu.VMEM((tok_count, model_width + LANES), F32),
             pltpu.SemaphoreType.DMA((2, 3)),
             pltpu.SemaphoreType.DMA((experts,)),
             pltpu.SemaphoreType.DMA((experts,)),
@@ -603,198 +619,648 @@
     )(arrived, hidden, result, cot_rows, gate_col, id_cols, up, up_bias, down)
 
 
-def middle_kernel(
-    experts, sums_ref, residual_ref, second_ref, cot_ref, router_ref, vectors_ref,
-    grad_ref, half_ref, router_grad_ref, rows_ref,
+def tail_kernel(
+    experts, stride, half, seq_count, head_parts,
+    sums_ref, id_cols_ref, gate_cols_ref, own_residual_ref, own_second_ref, cot_own_ref,
+    own_columns_hbm, router_ref, vectors_ref, own_tokens_ref, norm_ref, result_ref,
+    context_hbm, first_hbm, qkv_hbm, totals_hbm, weight_ref, out_weight_ref,
+    segc_ref, segr_ref, live_ref,
+    tokens_hbm, block_ref, qkv_sum_ref, out_sum_ref, bias_sum_ref, small_ref,
+    columns_scr, part_two, down_one, up_one, down_two, up_two, own_scr,
+    full_one, full_two, grad_scr,
+    context_scr, first_scr, qkv_scr, totals_scr, back_scr, penalty_scr, joined_scr,
+    qkv_grad, out_grad, bias_grad, rows_acc, router_acc,
+    result_home, result_wide,
+    qkv_send, qkv_recv, qkv_all, out_send, out_recv, out_all, bias_recv, small_head, small_recv,
+    columns_sem, load_sem, stage_sem, result_send_sem, result_recv_sem,
+    down_one_sem, up_one_sem, down_two_sem, up_two_sem, down_one_out, up_one_out, down_two_out, up_two_out,
+    full_one_sem, full_two_sem, full_one_out, full_two_out,
+    sum_send_sem, sum_recv_sem, all_send_sem, all_recv_sem,
+    bias_send_sem, bias_recv_sem, head_send_sem, head_recv_sem, small_send_sem, small_recv_sem,
 ):
-    model_width = residual_ref.shape[1]
-    second = second_ref[...]
-    lane = lax.broadcasted_iota(jnp.int32, (second.shape[0], LANES), 1)
-    logits = jnp.where(lane < experts, dot(second, router_ref[...]), NEGATIVE)
-    powers = jnp.exp(logits - jnp.max(logits, axis=1, keepdims=True))
-    chances = powers / jnp.sum(powers, axis=1, keepdims=True)
-    route_grad = sums_ref[:, model_width:].astype(F32)
-    logit_grad = (
-        chances * (route_grad - jnp.sum(chances * route_grad, axis=1, keepdims=True))
-    ).astype(BF16)
-    router_grad_ref[...] = dot_first(second, logit_grad)
-    grad = sums_ref[:, :model_width].astype(F32) + dot_last(logit_grad, router_ref[...])
-    normal, scale = standard(residual_ref[...])
-    rows_ref[0:1] = jnp.sum(grad * normal, axis=0, keepdims=True)
-    rows_ref[1:2] = jnp.sum(grad, axis=0, keepdims=True)
-    total = cot_ref[...].astype(F32) + norm_back(grad, vectors_ref[1:2], normal, scale)
-    grad_ref[...] = total
-    half_ref[...] = total.astype(BF16)
-    rows_ref[2:3] = jnp.sum(total, axis=0, keepdims=True)
-    rows_ref[3:8] = jnp.zeros((5, model_width), F32)
-
-
-def middle(sums, residual, second, cot_rows, router, vectors, experts):
-    rows, model_width = residual.shape
-    return pl.pallas_call(
-        partial(middle_kernel, experts),
-        in_specs=[whole()] * 6,
-        out_specs=[whole()] * 4,
-        out_shape=[
-            shaped((rows, model_width), F32),
-            shaped((rows, model_width), BF16),
-            shaped((model_width, LANES), F32),
-            shaped((8, model_width), F32),
-        ],
-        compiler_params=params(),
-        cost_estimate=cost(5e9, 1e7),
-        name="middle",
-    )(sums, residual, second, cot_rows, router, vectors)
-
-
-def attend_back_kernel(
-    grad_ref, context_ref, first_ref, qkv_ref, total_ref, weight_ref, out_weight_ref,
-    segc_ref, segr_ref, live_ref,
-    first_grad_ref, weight_grad_ref, bias_grad_ref, out_grad_ref,
-):
-    rows = qkv_ref[...]
-    width = rows.shape[1] // 3
-    grad = grad_ref[...]
-    context_grad = dot_last(grad, out_weight_ref[...]).astype(BF16)
-    penalty = mask_penalty(segc_ref[0], segr_ref[0], live_ref[0])
-    context = context_ref[...]
-    query_parts, key_parts, value_parts = [], [], []
+    me = lax.axis_index("exp")
+    here = lax.axis_index("head")
+    ends = head_parts - 1
+    seqlen = segr_ref.shape[2]
+    part = seqlen // head_parts
+    model_width = vectors_ref.shape[1]
+    width = out_weight_ref.shape[0]
     factor = 1.0 / math.sqrt(HEAD_DIM)
-    for head in range(width // HEAD_DIM):
+
+    barrier = greet(experts)
+
+    def call(step, carry):
+        other = lax.rem(here + step, head_parts)
+        pl.semaphore_signal(barrier, inc=1, device_id=(me, other), device_id_type=MESH)
+        return carry
+
+    lax.fori_loop(1, head_parts, call, 0)
+
+    def chunk_loads(seq):
+        span = pl.ds(pl.multiple_of(seq * seqlen, seqlen), seqlen)
+        return (
+            pltpu.make_async_copy(context_hbm.at[span], context_scr, load_sem.at[0]),
+            pltpu.make_async_copy(first_hbm.at[span], first_scr, load_sem.at[1]),
+            pltpu.make_async_copy(qkv_hbm.at[span], qkv_scr, load_sem.at[2]),
+            pltpu.make_async_copy(totals_hbm.at[span], totals_scr, load_sem.at[3]),
+        )
+
+    for copy in chunk_loads(0):
+        copy.start()
+    qkv_grad[...] = jnp.zeros_like(qkv_grad)
+    out_grad[...] = jnp.zeros_like(out_grad)
+    bias_grad[...] = jnp.zeros_like(bias_grad)
+    rows_acc[...] = jnp.zeros_like(rows_acc)
+    router_acc[...] = jnp.zeros_like(router_acc)
+    pl.semaphore_wait(barrier, experts - 1 + ends)
+
+    def to_exp(target):
+        return dict(device_id=(target, here), device_id_type=MESH)
+
+    def to_head(target):
+        return dict(device_id=(me, target), device_id_type=MESH)
+
+    def each_peer(action):
+        def one(step, carry):
+            action(step, lax.rem(me + step, experts), lax.rem(me + experts - step, experts))
+            return carry
+
+        lax.fori_loop(1, experts, one, 0)
+
+    def result_copy(step, target):
+        return pltpu.make_async_remote_copy(
+            src_ref=result_ref.at[target],
+            dst_ref=result_home.at[me],
+            send_sem=result_send_sem.at[step],
+            recv_sem=result_recv_sem.at[step],
+            **to_exp(target),
+        )
+
+    each_peer(lambda step, target, source: result_copy(step, target).start())
+    result_home[me] = result_ref[me]
+
+    def down_copy(buffer, sems, outs, seq, shard):
+        return pltpu.make_async_remote_copy(
+            src_ref=buffer.at[seq, shard],
+            dst_ref=buffer.at[seq, shard],
+            send_sem=outs.at[seq, shard],
+            recv_sem=sems.at[seq, shard],
+            **to_head(here - 1),
+        )
+
+    def up_copy(buffer, sems, outs, seq, shard):
+        return pltpu.make_async_remote_copy(
+            src_ref=buffer.at[seq, shard - 1],
+            dst_ref=buffer.at[seq, shard - 1],
+            send_sem=outs.at[seq, shard - 1],
+            recv_sem=sems.at[seq, shard - 1],
+            **to_head(here + 1),
+        )
+
+    one_down = (down_one, down_one_sem, down_one_out)
+    one_up = (up_one, up_one_sem, up_one_out)
+    two_down = (down_two, down_two_sem, down_two_out)
+    two_up = (up_two, up_two_sem, up_two_out)
+
+    def reduce_hop(partial_ref, base, down, up, seq, hop):
+        low = hop - ends + here
+        high = ends - hop + here
+
+        @pl.when((low >= 0) & (low < here))
+        def downward():
+            rows = partial_ref[pl.ds(pl.multiple_of(base + low * part, part), part)]
+
+            @pl.when(here < ends)
+            def add():
+                down_copy(*down, seq, low).wait_recv()
+                down[0][seq, low] = (down[0][seq, low].astype(F32) + rows.astype(F32)).astype(BF16)
+
+            @pl.when(here == ends)
+            def begin():
+                down[0][seq, low] = rows
+
+            down_copy(*down, seq, low).start()
+
+        @pl.when((high > here) & (high <= ends))
+        def upward():
+            rows = partial_ref[pl.ds(pl.multiple_of(base + high * part, part), part)]
+
+            @pl.when(here > 0)
+            def add():
+                up_copy(*up, seq, high).wait_recv()
+                up[0][seq, high - 1] = (
+                    up[0][seq, high - 1].astype(F32) + rows.astype(F32)
+                ).astype(BF16)
+
+            @pl.when(here == 0)
+            def begin():
+                up[0][seq, high - 1] = rows
+
+            up_copy(*up, seq, high).start()
+
+    def reduce_end(partial_ref, base, down, up, seq, columns):
+        own = pl.ds(pl.multiple_of(base + here * part, part), part)
+        own_scr[:, :columns] = partial_ref[own].astype(F32)
+
+        @pl.when(here < ends)
+        def below():
+            down_copy(*down, seq, here).wait_recv()
+            own_scr[:, :columns] += down[0][seq, here].astype(F32)
+
+        @pl.when(here > 0)
+        def above():
+            up_copy(*up, seq, here).wait_recv()
+            own_scr[:, :columns] += up[0][seq, here - 1].astype(F32)
+
+    def reduce_drain(down, up, seq):
+        for shard in range(ends):
+
+            @pl.when(shard < here)
+            def downward():
+                down_copy(*down, seq, shard).wait_send()
+
+            @pl.when(shard + 1 > here)
+            def upward():
+                up_copy(*up, seq, shard + 1).wait_send()
+
+    def full_copy(buffer, sems, outs, seq, shard, side):
+        rows = pl.ds(pl.multiple_of(shard * part, part), part)
+        return pltpu.make_async_remote_copy(
+            src_ref=buffer.at[seq, rows],
+            dst_ref=buffer.at[seq, rows],
+            send_sem=outs.at[seq, shard, side],
+            recv_sem=sems.at[seq, shard],
+            **to_head(here + 1 - 2 * side),
+        )
+
+    one_full = (full_one, full_one_sem, full_one_out)
+    two_full = (full_two, full_two_sem, full_two_out)
+
+    def spread_hop(full, seq, hop):
+        for side in range(2):
+            shard = here - hop if side == 0 else here + hop
+            there = shard >= 0 if side == 0 else shard <= ends
+            onward = here < ends if side == 0 else here > 0
+
+            @pl.when(there)
+            def arrived():
+                if hop > 0:
+                    full_copy(*full, seq, shard, side).wait_recv()
+                if hop < ends:
+
+                    @pl.when(onward)
+                    def pass_on():
+                        full_copy(*full, seq, shard, side).start()
+
+    def spread_drain(full, seq):
+        for hop in range(ends):
+            for side in range(2):
+                shard = here - hop if side == 0 else here + hop
+                there = shard >= 0 if side == 0 else shard <= ends
+                onward = here < ends if side == 0 else here > 0
+
+                @pl.when(there & onward)
+                def sent():
+                    full_copy(*full, seq, shard, side).wait_send()
+
+    def middle(seq):
+        second = own_second_ref[seq]
+        lane = lax.broadcasted_iota(jnp.int32, (part, LANES), 1)
+        logits = jnp.where(lane < experts, dot(second, router_ref[...]), NEGATIVE)
+        powers = jnp.exp(logits - jnp.max(logits, axis=1, keepdims=True))
+        chances = powers / jnp.sum(powers, axis=1, keepdims=True)
+        route_grad = own_scr[:, model_width:]
+        logit_grad = (
+            chances * (route_grad - jnp.sum(chances * route_grad, axis=1, keepdims=True))
+        ).astype(BF16)
+        router_acc[...] += dot_first(second, logit_grad)
+        grad = own_scr[:, :model_width] + dot_last(logit_grad, router_ref[...])
+        normal, scale = standard(own_residual_ref[seq])
+        rows_acc[0:1] += jnp.sum(grad * normal, axis=0, keepdims=True)
+        rows_acc[1:2] += jnp.sum(grad, axis=0, keepdims=True)
+        total = cot_own_ref[seq].astype(F32) + norm_back(grad, vectors_ref[1:2], normal, scale)
+        rows_acc[2:3] += jnp.sum(total, axis=0, keepdims=True)
+        grad_scr[seq] = total
+        full_one[seq, pl.ds(pl.multiple_of(here * part, part), part)] = total.astype(BF16)
+
+    def attend_start(seq):
+        for copy in chunk_loads(seq):
+            copy.wait()
+        grad = full_one[seq]
+        back_scr[...] = dot_last(grad, out_weight_ref[...]).astype(BF16)
+        out_grad[...] += dot_first(context_scr[...], grad)
+        penalty_scr[...] = mask_penalty(segc_ref[seq], segr_ref[seq], live_ref[seq]).astype(BF16)
+
+    def attend_head(head):
         lo = head * HEAD_DIM
         hi = lo + HEAD_DIM
-        query = rows[:, lo:hi] * BF16(factor)
-        keys = rows[:, width + lo : width + hi]
-        values = rows[:, 2 * width + lo : 2 * width + hi]
-        back = context_grad[:, lo:hi]
-        weights = jnp.exp(dot_last(query, keys) + penalty - total_ref[:, head : head + 1])
-        value_parts.append(dot_first(weights.astype(BF16), back))
-        weight_grad = dot_last(back, values)
+        query = qkv_scr[:, lo:hi] * BF16(factor)
+        keys = qkv_scr[:, width + lo : width + hi]
+        values = qkv_scr[:, 2 * width + lo : 2 * width + hi]
+        back = back_scr[:, lo:hi]
+        weights = jnp.exp(
+            dot_last(query, keys) + penalty_scr[...].astype(F32) - totals_scr[:, head : head + 1]
+        )
+        joined_scr[:, 2 * width + lo : 2 * width + hi] = dot_first(
+            weights.astype(BF16), back
+        ).astype(BF16)
         inner = jnp.sum(
-            back.astype(F32) * context[:, lo:hi].astype(F32), axis=-1, keepdims=True
-        )
-        score_grad = (weights * (weight_grad - inner)).astype(BF16)
-        query_parts.append(dot(score_grad, keys) * factor)
-        key_parts.append(dot_first(score_grad, query))
-    joined = jnp.concatenate(query_parts + key_parts + value_parts, axis=1).astype(BF16)
-    first_grad_ref[...] = dot_last(joined, weight_ref[...]).astype(BF16)
-    weight_grad = dot_first(first_ref[...], joined)
-    out_grad = dot_first(context, grad)
-    bias_grad = jnp.sum(joined.astype(F32), axis=0, keepdims=True)
-
-    @pl.when(pl.program_id(0) == 0)
-    def start():
-        weight_grad_ref[...] = weight_grad
-        out_grad_ref[...] = out_grad
-        bias_grad_ref[...] = jnp.broadcast_to(bias_grad, bias_grad_ref.shape)
-
-    @pl.when(pl.program_id(0) > 0)
-    def more():
-        weight_grad_ref[...] += weight_grad
-        out_grad_ref[...] += out_grad
-        bias_grad_ref[...] += jnp.broadcast_to(bias_grad, bias_grad_ref.shape)
-
-
-def attend_back(
-    grad, context, first, qkv, totals, flat_qkv, out_weight, seg_cols, seg_rows, live_rows
+            back.astype(F32) * context_scr[:, lo:hi].astype(F32), axis=-1, keepdims=True
+        )
+        score_grad = (weights * (dot_last(back, values) - inner)).astype(BF16)
+        joined_scr[:, lo:hi] = (dot(score_grad, keys) * factor).astype(BF16)
+        joined_scr[:, width + lo : width + hi] = dot_first(score_grad, query).astype(BF16)
+
+    def attend_end(seq):
+        joined = joined_scr[...]
+        part_two[...] = dot_last(joined, weight_ref[...]).astype(BF16)
+        qkv_grad[...] += dot_first(first_scr[...], joined)
+        bias_grad[0:1] += jnp.sum(joined.astype(F32), axis=0, keepdims=True)
+
+        @pl.when(seq + 1 < seq_count)
+        def more():
+            for copy in chunk_loads(seq + 1):
+                copy.start()
+
+    def last(seq):
+        grad = own_scr[:, :model_width]
+        normal, scale = standard(own_tokens_ref[seq].astype(F32))
+        rows_acc[3:4] += jnp.sum(grad * normal, axis=0, keepdims=True)
+        rows_acc[4:5] += jnp.sum(grad, axis=0, keepdims=True)
+        total = grad_scr[seq] + norm_back(grad, norm_ref[0:1], normal, scale)
+        full_two[seq, pl.ds(pl.multiple_of(here * part, part), part)] = total.astype(BF16)
+
+    def stage_copy(seq):
+        span = pl.ds(pl.multiple_of(seq * seqlen, seqlen), seqlen)
+        return pltpu.make_async_copy(full_two.at[seq], tokens_hbm.at[span], stage_sem.at[seq])
+
+    def open_results():
+        each_peer(lambda step, target, source: result_copy(step, target).wait_recv())
+
+        def one(expert, carry):
+            packed = result_home[expert]
+            result_wide[expert, :, :LANES] = packed[:stride]
+            tail = packed[stride:]
+            result_wide[expert, :half, LANES:] = tail[:, :HEAD_DIM]
+            result_wide[expert, half:, LANES:] = tail[2 * half - stride :, HEAD_DIM:]
+            return carry
+
+        lax.fori_loop(0, experts, one, 0)
+
+    def combine(seq):
+        span = pl.ds(pl.multiple_of(seq * seqlen, seqlen), seqlen)
+        first = id_cols_ref[span, 0:1]
+        second = id_cols_ref[span, 1:2]
+        pltpu.make_async_copy(own_columns_hbm.at[span], columns_scr, columns_sem.at[0]).start()
+        pltpu.make_async_copy(own_columns_hbm.at[span], columns_scr, columns_sem.at[0]).wait()
+        first_gate = gate_cols_ref[span, 0:1]
+        second_gate = gate_cols_ref[span, 1:2]
+
+        def one(expert, total):
+            slots = expert * stride + lax.broadcasted_iota(jnp.int32, (1, stride), 1)
+            weights = jnp.where(
+                first == slots, first_gate, jnp.where(second == slots, second_gate, 0.0)
+            )
+            return total + dot(weights.astype(BF16), result_wide[expert])
+
+        block_ref[span] = lax.fori_loop(0, experts, one, columns_scr[...]).astype(BF16)
+
+    qkv_rows = qkv_grad.shape[0] // experts
+    out_rows = out_grad.shape[0] // experts
+
+    def sum_copies(step, target):
+        return (
+            pltpu.make_async_remote_copy(
+                src_ref=qkv_send.at[target],
+                dst_ref=qkv_recv.at[me],
+                send_sem=sum_send_sem.at[step, 0],
+                recv_sem=sum_recv_sem.at[step, 0],
+                **to_exp(target),
+            ),
+            pltpu.make_async_remote_copy(
+                src_ref=out_send.at[target],
+                dst_ref=out_recv.at[me],
+                send_sem=sum_send_sem.at[step, 1],
+                recv_sem=sum_recv_sem.at[step, 1],
+                **to_exp(target),
+            ),
+        )
+
+    def all_copies(step, target):
+        return (
+            pltpu.make_async_remote_copy(
+                src_ref=qkv_all.at[me],
+                dst_ref=qkv_all.at[me],
+                send_sem=all_send_sem.at[step, 0],
+                recv_sem=all_recv_sem.at[step, 0],
+                **to_exp(target),
+            ),
+            pltpu.make_async_remote_copy(
+                src_ref=out_all.at[me],
+                dst_ref=out_all.at[me],
+                send_sem=all_send_sem.at[step, 1],
+                recv_sem=all_recv_sem.at[step, 1],
+                **to_exp(target),
+            ),
+        )
+
+    def all_arrivals(step, source):
+        return (
+            pltpu.make_async_remote_copy(
+                src_ref=qkv_all.at[source],
+                dst_ref=qkv_all.at[source],
+                send_sem=all_send_sem.at[step, 0],
+                recv_sem=all_recv_sem.at[step, 0],
+                **to_exp(source),
+            ),
+            pltpu.make_async_remote_copy(
+                src_ref=out_all.at[source],
+                dst_ref=out_all.at[source],
+                send_sem=all_send_sem.at[step, 1],
+                recv_sem=all_recv_sem.at[step, 1],
+                **to_exp(source),
+            ),
+        )
+
+    def bias_copy(step, target):
+        return pltpu.make_async_remote_copy(
+            src_ref=bias_grad,
+            dst_ref=bias_recv.at[me],
+            send_sem=bias_send_sem.at[step],
+            recv_sem=bias_recv_sem.at[step],
+            **to_exp(target),
+        )
+
+    def start_sums():
+        for block in range(experts):
+            qkv_send[block] = qkv_grad[block * qkv_rows : (block + 1) * qkv_rows].astype(BF16)
+            out_send[block] = out_grad[block * out_rows : (block + 1) * out_rows].astype(BF16)
+
+        def begin(step, target, source):
+            for copy in sum_copies(step, target):
+                copy.start()
+            bias_copy(step, target).start()
+
+        each_peer(begin)
+        qkv_recv[me] = qkv_send[me]
+        out_recv[me] = out_send[me]
+        bias_recv[me] = bias_grad[...]
+
+    def spread_sums():
+        def arrive(step, target, source):
+            for copy in sum_copies(step, target):
+                copy.wait_recv()
+            bias_copy(step, target).wait_recv()
+
+        each_peer(arrive)
+
+        def add(source, totals):
+            return (
+                totals[0] + qkv_recv[source].astype(F32),
+                totals[1] + out_recv[source].astype(F32),
+                totals[2] + bias_recv[source],
+            )
+
+        qkv_total, out_total, bias_total = lax.fori_loop(
+            1,
+            experts,
+            add,
+            (qkv_recv[0].astype(F32), out_recv[0].astype(F32), bias_recv[0]),
+        )
+        qkv_all[me] = qkv_total.astype(BF16)
+        out_all[me] = out_total.astype(BF16)
+        bias_sum_ref[...] = bias_total
+
+        def begin(step, target, source):
+            for copy in all_copies(step, target):
+                copy.start()
+
+        each_peer(begin)
+
+    def end_sums():
+        def arrive(step, target, source):
+            for copy in all_arrivals(step, source):
+                copy.wait_recv()
+
+        each_peer(arrive)
+        for block in range(experts):
+            qkv_sum_ref[block * qkv_rows : (block + 1) * qkv_rows] = qkv_all[block].astype(F32)
+            out_sum_ref[block * out_rows : (block + 1) * out_rows] = out_all[block].astype(F32)
+
+    def head_copy(step):
+        return pltpu.make_async_remote_copy(
+            src_ref=small_head.at[here],
+            dst_ref=small_head.at[here],
+            send_sem=head_send_sem.at[step],
+            recv_sem=head_recv_sem.at[step],
+            **to_head(lax.rem(here + step, head_parts)),
+        )
+
+    def head_arrival(step):
+        source = lax.rem(here + head_parts - step, head_parts)
+        return pltpu.make_async_remote_copy(
+            src_ref=small_head.at[source],
+            dst_ref=small_head.at[source],
+            send_sem=head_send_sem.at[step],
+            recv_sem=head_recv_sem.at[step],
+            **to_head(source),
+        )
+
+    def small_copy(step, target):
+        return pltpu.make_async_remote_copy(
+            src_ref=small_recv.at[me],
+            dst_ref=small_recv.at[me],
+            send_sem=small_send_sem.at[step],
+            recv_sem=small_recv_sem.at[step],
+            **to_exp(target),
+        )
+
+    def small_arrival(step, source):
+        return pltpu.make_async_remote_copy(
+            src_ref=small_recv.at[source],
+            dst_ref=small_recv.at[source],
+            send_sem=small_send_sem.at[step],
+            recv_sem=small_recv_sem.at[step],
+            **to_exp(source),
+        )
+
+    heads = width // HEAD_DIM
+    router_rows = small_head.shape[1] - 8
+
+    def at(step, offset, action):
+        seq = step - offset
+
+        @pl.when((seq >= 0) & (seq < seq_count))
+        def run():
+            action(seq)
+
+    def time_step(step, carry):
+        at(step, 2, attend_start)
+        for hop in range(max(ends, heads)):
+            if hop < ends:
+                at(
+                    step,
+                    0,
+                    lambda seq: reduce_hop(sums_ref, seq * seqlen, one_down, one_up, seq, hop),
+                )
+                at(step, 3, lambda seq: reduce_hop(part_two, 0, two_down, two_up, seq, hop))
+                at(step, 1, lambda seq: spread_hop(one_full, seq, hop))
+                at(step, 4, lambda seq: spread_hop(two_full, seq, hop))
+            if hop < heads:
+                at(step, 2, lambda seq: attend_head(hop))
+
+        def first_end(seq):
+            reduce_end(sums_ref, seq * seqlen, one_down, one_up, seq, model_width + LANES)
+            middle(seq)
+
+        def second_end(seq):
+            reduce_end(part_two, 0, two_down, two_up, seq, model_width)
+            last(seq)
+
+        def tokens_end(seq):
+            spread_hop(two_full, seq, ends)
+            stage_copy(seq).start()
+
+        at(step, 0, first_end)
+        at(step, 3, second_end)
+        at(step, 2, attend_end)
+        at(step, 1, lambda seq: spread_hop(one_full, seq, ends))
+
+        @pl.when(step == seq_count + 1)
+        def sums():
+            start_sums()
+            open_results()
+
+        at(step, 4, combine)
+
+        @pl.when(step == seq_count + 2)
+        def small():
+            small_head[here, :8] = rows_acc[...]
+            small_head[here, 8:] = router_acc[...].T[:router_rows]
+            for other in range(1, head_parts):
+                head_copy(other).start()
+            spread_sums()
+
+        at(step, 4, tokens_end)
+        return carry
+
+    lax.fori_loop(0, seq_count + 4, time_step, 0)
+
+    for other in range(1, head_parts):
+        head_arrival(other).wait_recv()
+    total = small_head[0]
+    for other in range(1, head_parts):
+        total = total + small_head[other]
+    small_recv[me] = total
+    each_peer(lambda step, target, source: small_copy(step, target).start())
+    end_sums()
+    each_peer(lambda step, target, source: small_arrival(step, source).wait_recv())
+    small_ref[...] = lax.fori_loop(
+        1, experts, lambda source, total: total + small_recv[source], small_recv[0]
+    )
+    for seq in range(seq_count):
+        stage_copy(seq).wait()
+        reduce_drain(one_down, one_up, seq)
+        reduce_drain(two_down, two_up, seq)
+        spread_drain(one_full, seq)
+        spread_drain(two_full, seq)
+    for other in range(1, head_parts):
+        head_copy(other).wait_send()
+
+    def sent(step, target, source):
+        result_copy(step, target).wait_send()
+        for copy in sum_copies(step, target):
+            copy.wait_send()
+        bias_copy(step, target).wait_send()
+        for copy in all_copies(step, target):
+            copy.wait_send()
+        small_copy(step, target).wait_send()
+
+    each_peer(sent)
+
+
+def tail(
+    sums, id_cols, gate_cols, own_residual, own_second, cot_own, own_columns, router, vectors,
+    own_tokens, norm_rows, result, context, first, qkv, totals, flat_qkv, out_weight,
+    seg_cols, seg_rows, live_rows, stride, half, head_parts,
 ):
-    tok_count, model_width = first.shape
-    seq_count, seqlen = seg_rows.shape[0], seg_rows.shape[2]
+    experts = result.shape[0]
+    model_width = first.shape[1]
+    seq_count, part = own_residual.shape[:2]
+    seqlen = part * head_parts
+    tok_count = seq_count * seqlen
     wide = flat_qkv.shape[1]
     width = wide // 3
-    step = lambda i: (i, 0)
-    fixed = lambda i: (0, 0)
-    deep = lambda i: (i, 0, 0)
+    ends = head_parts - 1
+    small_rows = 8 + round_up(experts, 8)
+    dma = pltpu.SemaphoreType.DMA
     return pl.pallas_call(
-        attend_back_kernel,
-        grid=(seq_count,),
-        in_specs=[
-            pl.BlockSpec((seqlen, model_width), step),
-            pl.BlockSpec((seqlen, width), step),
-            pl.BlockSpec((seqlen, model_width), step),
-            pl.BlockSpec((seqlen, wide), step),
-            pl.BlockSpec((seqlen, LANES), step),
-            pl.BlockSpec((model_width, wide), fixed),
-            pl.BlockSpec((width, model_width), fixed),
-            pl.BlockSpec((1, seqlen, 1), deep),
-            pl.BlockSpec((1, 1, seqlen), deep),
-            pl.BlockSpec((1, 1, seqlen), deep),
-        ],
-        out_specs=[
-            pl.BlockSpec((seqlen, model_width), step),
-            pl.BlockSpec((model_width, wide), fixed),
-            pl.BlockSpec((8, wide), fixed),
-            pl.BlockSpec((width, model_width), fixed),
-        ],
+        partial(tail_kernel, experts, stride, half, seq_count, head_parts),
+        in_specs=[whole()] * 6 + [anywhere()] + [whole()] * 5 + [anywhere()] * 4 + [whole()] * 5,
+        out_specs=[anywhere()] + [whole()] * 5,
         out_shape=[
             shaped((tok_count, model_width), BF16),
+            shaped((tok_count, width), BF16),
             shaped((model_width, wide), F32),
+            shaped((width, model_width), F32),
             shaped((8, wide), F32),
-            shaped((width, model_width), F32),
+            shaped((small_rows, model_width), F32),
         ],
-        compiler_params=params(),
-        cost_estimate=cost(1e10, 1e7),
-        name="attend_back",
-    )(grad, context, first, qkv, totals, flat_qkv, out_weight, seg_cols, seg_rows, live_rows)
-
-
-def last_kernel(grad_ref, tokens_ref, residual_grad_ref, norm_ref, out_ref, rows_ref):
-    grad = grad_ref[...].astype(F32)
-    normal, scale = standard(tokens_ref[...].astype(F32))
-    rows_ref[0:1] = jnp.sum(grad * normal, axis=0, keepdims=True)
-    rows_ref[1:2] = jnp.sum(grad, axis=0, keepdims=True)
-    rows_ref[2:8] = jnp.zeros((6, grad.shape[1]), F32)
-    total = residual_grad_ref[...] + norm_back(grad, norm_ref[0:1], normal, scale)
-    out_ref[...] = total.astype(BF16)
-
-
-def last(grad, tokens, residual_grad, norm_rows):
-    rows, model_width = tokens.shape
-    return pl.pallas_call(
-        last_kernel,
-        in_specs=[whole()] * 4,
-        out_specs=[whole()] * 2,
-        out_shape=[shaped((rows, model_width), BF16), shaped((8, model_width), F32)],
-        compiler_params=params(),
-        cost_estimate=cost(1e9, 1e7),
-        name="last",
-    )(grad, tokens, residual_grad, norm_rows)
-
-
-def combine_kernel(stride, share, chunk, ids_ref, gates_ref, home_ref, residual_ref, out_ref, total_scr):
-    experts = home_ref.shape[0]
-    total_scr[...] = residual_ref[...] * share
-
-    def one(source, carry):
-        slots = source * stride + lax.broadcasted_iota(jnp.int32, (1, stride), 1)
-
-        def part(index, carry):
-            span = pl.ds(pl.multiple_of(index * chunk, chunk), chunk)
-            weights = jnp.where(
-                ids_ref[span, 0:1] == slots,
-                gates_ref[span, 0:1],
-                jnp.where(ids_ref[span, 1:2] == slots, gates_ref[span, 1:2], 0.0),
-            ).astype(BF16)
-            total_scr[span] += dot(weights, home_ref[source])
-            return carry
-
-        return lax.fori_loop(0, total_scr.shape[0] // chunk, part, carry)
-
-    lax.fori_loop(0, experts, one, 0)
-    out_ref[...] = total_scr[...].astype(BF16)
-
-
-def combine(id_cols, gate_cols, home, residual, stride, share, chunk):
-    return pl.pallas_call(
-        partial(combine_kernel, stride, share, chunk),
-        in_specs=[whole()] * 4,
-        out_specs=whole(),
-        out_shape=shaped(residual.shape, BF16),
-        scratch_shapes=[pltpu.VMEM(residual.shape, F32)],
-        compiler_params=params(),
-        cost_estimate=cost(1.2e10, 1e7),
-        name="combine",
-    )(id_cols, gate_cols, home, residual)
+        scratch_shapes=[
+            pltpu.VMEM((seqlen, width), F32),
+            pltpu.VMEM((seqlen, model_width), BF16),
+            pltpu.VMEM((seq_count, ends, part, model_width + LANES), BF16),
+            pltpu.VMEM((seq_count, ends, part, model_width + LANES), BF16),
+            pltpu.VMEM((seq_count, ends, part, model_width), BF16),
+            pltpu.VMEM((seq_count, ends, part, model_width), BF16),
+            pltpu.VMEM((part, model_width + LANES), F32),
+            pltpu.VMEM((seq_count, seqlen, model_width), BF16),
+            pltpu.VMEM((seq_count, seqlen, model_width), BF16),
+            pltpu.VMEM((seq_count, part, model_width), F32),
+            pltpu.VMEM((seqlen, width), BF16),
+            pltpu.VMEM((seqlen, model_width), BF16),
+            pltpu.VMEM((seqlen, wide), BF16),
+            pltpu.VMEM((seqlen, LANES), F32),
+            pltpu.VMEM((seqlen, width), BF16),
+            pltpu.VMEM((seqlen, seqlen), BF16),
+            pltpu.VMEM((seqlen, wide), BF16),
+            pltpu.VMEM((model_width, wide), F32),
+            pltpu.VMEM((width, model_width), F32),
+            pltpu.VMEM((8, wide), F32),
+            pltpu.VMEM((8, model_width), F32),
+            pltpu.VMEM((model_width, LANES), F32),
+            pltpu.VMEM((experts, stride + half, LANES), BF16),
+            pltpu.VMEM((experts, stride, width), BF16),
+            pltpu.VMEM((experts, model_width // experts, wide), BF16),
+            pltpu.VMEM((experts, model_width // experts, wide), BF16),
+            pltpu.VMEM((experts, model_width // experts, wide), BF16),
+            pltpu.VMEM((experts, width // experts, model_width), BF16),
+            pltpu.VMEM((experts, width // experts, model_width), BF16),
+            pltpu.VMEM((experts, width // experts, model_width), BF16),
+            pltpu.VMEM((experts, 8, wide), F32),
+            pltpu.VMEM((head_parts, small_rows, model_width), F32),
+            pltpu.VMEM((experts, small_rows, model_width), F32),
+            dma((1,)),
+            dma((4,)),
+            dma((seq_count,)),
+            dma((experts,)),
+            dma((experts,)),
+        ]
+        + [dma((seq_count, ends))] * 8
+        + [dma((seq_count, head_parts))] * 2
+        + [dma((seq_count, head_parts, 2))] * 2
+        + [dma((experts, 2))] * 4
+        + [dma((experts,))] * 2
+        + [dma((head_parts,))] * 2
+        + [dma((experts,))] * 2,
+        compiler_params=params(collective_id=2, has_side_effects=True),
+        cost_estimate=cost(1e11, 1e8),
+        name="tail",
+    )(
+        sums, id_cols, gate_cols, own_residual, own_second, cot_own, own_columns, router, vectors,
+        own_tokens, norm_rows, result, context, first, qkv, totals, flat_qkv, out_weight,
+        seg_cols, seg_rows, live_rows,
+    )
 
 
 def body(
@@ -824,7 +1290,6 @@
     head_parts = lax.axis_size("head")
     head_index = lax.axis_index("head")
     quarter = model_width // head_parts
-    tok_part = tok_count // head_parts
     capacity = (21 * tok_count + 10 * experts - 1) // (10 * experts)
     stride = round_up(capacity, 16)
     half = round_up(stride // 2, 16)
@@ -872,54 +1337,48 @@
     id_cols = ids.T
     cot_moved = lax.all_to_all(cot_slots, "exp", split_axis=0, concat_axis=0, tiled=True)
     cot_rows = lax.all_gather(cot_moved, "head", axis=0)
-    cot_own = lax.all_to_all(cotangent, "head", split_axis=0, concat_axis=1, tiled=True)
-
-    residual, own_residual, own_second, gates, arrived, hidden, result, gate_col = forward(
+    part = seqlen // head_parts
+    cot_own = lax.all_to_all(
+        cotangent.reshape(seq_count, head_parts, part, quarter),
+        "head",
+        split_axis=1,
+        concat_axis=3,
+        tiled=True,
+    ).reshape(seq_count, part, model_width)
+    own_tokens = lax.dynamic_slice_in_dim(
+        tokens.reshape(seq_count, seqlen, model_width), head_index * part, part, 1
+    )
+
+    own_residual, own_second, own_columns, gates, arrived, hidden, result, gate_col = forward(
         gathered, tokens, vectors, out_full_weight, router_wide, int_rows, ids,
-        up, up_bias_row, down, down_bias_row, experts, stride, seq_count, head_parts,
-    )
+        up, up_bias_row, down, down_bias_row, experts, stride, half, seq_count, head_parts,
+    )
+    gate_cols = gates.T
+    own_result = lax.psum_scatter(result, "head", scatter_dimension=0, tiled=True)[0]
     sums, grad_up, grad_up_bias, grad_down, grad_down_bias = backward(
         arrived, hidden, result, cot_rows, gate_col, id_cols, up, up_bias_row, down, half, head_parts,
         seqlen,
     )
-    own_sums = lax.psum_scatter(sums, "head", scatter_dimension=0, tiled=True)
-    residual_grad, residual_half, router_grad, second_rows = middle(
-        own_sums, own_residual, own_second, cot_own, router_wide, vectors, experts
-    )
-    grad_full = lax.all_gather(residual_half, "head", axis=0, tiled=True)
-
-    home_out = lax.all_to_all(result, "exp", split_axis=0, concat_axis=0, tiled=True)
-    block_sum = combine(id_cols, gates.T, home_out, residual, stride, 1.0 / head_parts, seqlen)
-    block_out = lax.psum_scatter(block_sum, "head", scatter_dimension=1, tiled=True)
-
-    first_grad, qkv_grad, bias_grad, out_grad = attend_back(
-        grad_full, context, first, qkv, totals, flat_qkv, out_weight, seg_cols, seg_rows, live_rows
-    )
-    own_first = lax.psum_scatter(first_grad, "head", scatter_dimension=0, tiled=True)
-    own_tokens = lax.dynamic_slice_in_dim(tokens, head_index * tok_part, tok_part, 0)
-    own_grad, first_rows = last(own_first, own_tokens, residual_grad, norm_rows)
-    grad_tokens = lax.all_gather(own_grad, "head", axis=0, tiled=True).astype(F32)
-
-    small = lax.psum(
-        jnp.concatenate([second_rows, first_rows, router_grad[:, :experts].T], axis=0),
-        ("exp", "head"),
-    )
-    qkv_grad, bias_grad, out_grad = lax.psum((qkv_grad, bias_grad[0:1], out_grad), "exp")
+    grad_tokens, block_out, qkv_grad, out_grad, bias_grad, small = tail(
+        sums, id_cols, gate_cols, own_residual, own_second, cot_own, own_columns,
+        router_wide, vectors, own_tokens, norm_rows, own_result, context, first, qkv, totals,
+        flat_qkv, out_weight, seg_cols, seg_rows, live_rows, stride, half, head_parts,
+    )
     grad_qv_bias = jnp.concatenate(
-        [bias_grad[:, :local_width], bias_grad[:, 2 * local_width :]], axis=0
+        [bias_grad[0:1, :local_width], bias_grad[0:1, 2 * local_width :]], axis=0
     )
     return (
         block_out,
-        grad_tokens,
-        small[8],
-        small[9],
+        grad_tokens.astype(F32),
+        small[3],
+        small[4],
         qkv_grad.reshape(model_width, 3, local_width),
         grad_qv_bias,
         out_grad,
         small[2],
         small[0],
         small[1],
-        small[16 : 16 + experts].T,
+        small[8 : 8 + experts].T,
         grad_up[None],
         grad_up_bias[0:1],
         grad_down[None],

time: 835 us -> 540 us (0.65)
  waiting for transfers between devices: 449 us -> 81.7 us
  Pallas kernels: 228 us -> 365 us
  blocking collectives: 61.9 us -> 25 us
  local copies, waits for them, and re-layouts: 63.1 us -> 35 us
    pallas_call x5 -> x2, Pallas kernels: 135 us -> 266 us  [the longest x1 184 us: tail(): pl.pallas_call(partial(tail_kernel, experts, stride, half, seq_count, hea...]
    psum x2 -> x0, waiting for transfers between devices: 122 us -> none  [the longest x1 66.9 us: body(): lax.psum((qkv_grad, bias_grad[0:1], out_grad), 'exp')]
    all_gather x2 -> x0, waiting for transfers between devices: 118 us -> none  [the longest x1 61.3 us: body(): grad_full = lax.all_gather(residual_half, 'head', axis=0, tiled=True)]
    reduce_scatter x2 -> x1, waiting for transfers between devices: 90 us -> 19.3 us  [body(): lax.psum_scatter(result, 'head', scatter_dimension=0, tiled=True)[0]]
    unnamed x11 -> x4, waiting for transfers between devices: 52.9 us -> 0.73 us
    unnamed x119 -> x46, local copies, waits for them, and re-layouts: 39.6 us -> 9.57 us
    all_to_all x1 -> x0, blocking collectives: 25 us -> none  [body(): lax.all_to_all(cotangent, 'head', split_axis=0, concat_axis=1, tiled=True)]
    all_to_all x1, waiting for transfers between devices: 13.1 us -> 32.8 us  [body(): lax.all_to_all(cotangent.reshape(seq_count, head_parts, part, quarter), '...]
  transfers between devices with their start and end apart: 11 -> 5, of which waited for: 10 -> 3; matrix products, arithmetic and copies ran while one was open for 4% -> 4% of each run, Pallas kernels for 16% -> 34%
where the time goes in v3:
time: 540 us; the launch traced here: 534 us
  Pallas kernels  365 us (68%)
  waiting for transfers between devices  81.7 us (15%)
  local copies, waits for them, and re-layouts  35 us (6%)
  blocking collectives  25 us (5%)
  between operations  14.2 us (3%)
  other arithmetic  8.33 us (2%)
    pallas_call x1, Pallas kernels, tail(): pl.pallas_call(partial(tail_kernel, experts, stride, half, seq_count, hea...  184 us
    pallas_call x1, Pallas kernels, forward(): pl.pallas_call(partial(forward_kernel, experts, stride, half, seq_count,...  82.5 us
    pallas_call x1, Pallas kernels, backward(): pl.pallas_call(partial(backward_kernel, experts, stride, half, head_parts...  75 us
    all_to_all x1, waiting for transfers between devices, body(): lax.all_to_all(cotangent.reshape(seq_count, head_parts, part, quarter), '...  32.8 us
    all_gather x1, waiting for transfers between devices, body(): gathered = lax.all_gather(packed, 'head', axis=0)  28.9 us
    all_to_all x1, blocking collectives, body(): lax.all_to_all(cot_slots, 'exp', split_axis=0, concat_axis=0, tiled=True)  25 us
    reduce_scatter x1, waiting for transfers between devices, body(): lax.psum_scatter(result, 'head', scatter_dimension=0, tiled=True)[0]  19.3 us
    pallas_call x1, Pallas kernels, attend(): pl.pallas_call(attend_kernel, grid=(seq_count,), in_specs=[pl.BlockSpec((...  13.3 us
  transfers between devices with their start and end apart: 5, of which 3 were waited for; matrix products, arithmetic and copies ran while one was open for 4% of the time, Pallas kernels for 34%

profile of v3, /device:TPU:0, one launch (start us, length us, event | category | flops | bytes accessed | tf_op | source)
XLA Modules:
  0.0 533.8 jit_solution(10055869524070024754)
XLA Ops:
  8.0 2.2 copy.55.weight_ref
  10.2 1.3 reshape.129.segr_ref
  11.5 2.0 copy.56.segc_ref
  15.6 13.3 %attend.1 = (bf16[1728,768]{1,0:T(8,128)(2,1)}, bf16[1728,576]{1,0:T(8,128)(2,1)}, bf16[1728,192]{1,0:T(8,128)(2,1)}, bf16[3,864,128]{2,1,0:T(8,128)(2,1)}, f32[1728,128]{1,0:T(8,128)}) custom-call(bf16[1728,768]{1,0:T(8,128)(2,1)} %tokens_ref.3, f32[8,768]{1,0:T(8,128)} %maximum_maximum_fusion.norm_ref, bf16[768,576]{1,0:T(8,128)(2,1)} %copy.55.weight_ref, ...), custom_call_target="tpu_custom_call" | custom-call | flops 4000000000 | bytes 10000000 | tf_op jit(solution)/shard_map/attend/pallas_call | solution.py:139
  32.3 10.6 %tables.1 = (s32[8,1728]{1,0:T(8,128)}, bf16[8,704,128]{2,1,0:T(8,128)(2,1)}) custom-call(s32[1728,1]{1,0:T(8,128)} %copy.58.prio_ref, s32[8,1728]{1,0:T(8,128)} %add_add_fusion.rows_ref, bf16[1728,192]{1,0:T(8,128)(2,1)} %copy.59.cot_ref), custom_call_target="tpu_custom_call" | custom-call | flops 10000000000 | bytes 10000000 | tf_op jit(solution)/shard_map/tables/pallas_call | solution.py:215
  42.9 25.0 %all_to_all.20 = bf16[8,704,128]{2,1,0:T(8,128)(2,1)} all-to-all(bf16[8,704,128]{2,1,0:T(8,128)(2,1)} %get-tuple-element.46), channel_id=1, replica_groups=mesh['exp'=8,'head'=4] {'exp'}, dimensions={0} | all-to-all | bytes 2883584 | tf_op jit(solution)/shard_map/all_to_all | solution.py:1338
  70.6 28.9 %all-gather.8.cloned.1.call-done = bf16[12,864,128]{2,1,0:T(8,128)(2,1)} async-done(((bf16[3,864,128]{2,1,0:T(8,128)(2,1)}), bf16[12,864,128]{2,1,0:T(8,128)(2,1)}) %all-gather.8.cloned.1.call-update) | async-done | bytes 2654224 | tf_op jit(solution)/shard_map/all_gather | solution.py:1323
  99.4 82.5 %forward.1 = (f32[3,144,768]{2,1,0:T(8,128)}, bf16[3,144,768]{2,1,0:T(8,128)(2,1)}, f32[1728,192]{1,0:T(8,128)}, f32[8,1728]{1,0:T(8,128)}, bf16[8,464,768]{2,1,...) custom-call(bf16[4,3,864,128]{3,2,1,0:T(8,128)(2,1)} %bitcast.37, ...), custom_call_target="tpu_custom_call" | custom-call | flops 80000000000 | bytes 100000000 | tf_op jit(solution)/shard_map/forward/pallas_call | solution.py:391
  184.1 3.9 all-to-all-start.1
  189.3 2.0 constant_dynamic-slice_fusion.1.own_tokens_ref
  191.3 32.8 %all-to-all-done.1 = bf16[3,4,144,192]{3,2,0,1:T(8,128)(2,1)S(1)} async-done(((bf16[3,4,144,192]{3,2,0,1:T(8,128)(2,1)}), bf16[3,4,144,192]{3,2,0,1:T(8,128)(2,1)S(1)}, u32[]{:S(2)}, u32[]{:S(2)}) %all-to-all-start.1) | async-done | bytes 663584 | tf_op jit(solution)/shard_map/all_to_all | solution.py:1341
  224.5 1.6 reshape.140.cot_own_ref
  226.2 1.3 copy.61
  227.4 75.0 %backward.1 = (bf16[1728,896]{1,0:T(8,128)(2,1)}, f32[768,768]{1,0:T(8,128)}, f32[8,768]{1,0:T(8,128)}, f32[768,768]{1,0:T(8,128)}, f32[8,768]{1,0:T(8,128)}) custom-call(bf16[8,464,768]{2,1,0:T(8,128)(2,1)} %get-tuple-element.43.arrived_hbm, bf16[8,464,768]{2,1,0:T(8,128)(2,1)} %get-tuple-element.44.hidden_hbm, ...), custom_call_target="tpu_custom_call" | custom-call | flops 80000000000 | bytes 100000000 | tf_op jit(solution)/shard_map/backward/pallas_call | solution.py:585
  303.2 1.3 slice.46
  305.1 19.3 %reduce-scatter.2.cloned.1.call-done = bf16[1,8,704,128]{3,2,1,0:T(8,128)(2,1)} async-done(((bf16[4,8,704,128]{3,2,1,0:T(8,128)(2,1)}), bf16[1,8,704,128]{3,2,1,0:T(8,128)(2,1)}) %reduce-scatter.2.cloned.1.call-update) | async-done | bytes 1441808 | tf_op jit(solution)/shard_map/reduce_scatter | solution.py:1357
  324.4 184.0 %tail.1 = (bf16[1728,768]{1,0:T(8,128)(2,1)}, bf16[1728,192]{1,0:T(8,128)(2,1)}, f32[768,576]{1,0:T(8,128)}, f32[192,768]{1,0:T(8,128)}, f32[8,576]{1,0:T(8,128)}, /*index=5*/f32[16,768]{1,0:T(8,128)}) custom-call(bf16[1728,896]{1,0:T(8,128)(2,1)} %get-tuple-element.48.sums_ref, s32[1728,8]{1,0:T(8,128)} %bitcast.30, f32[1728,8]{1,0:T(8,128)} %bitcast.31, ...), custom_call_target="tpu_custom_call" | custom-call | flops 99999997952 | bytes 100000000 | tf_op jit(solution)/shard_map/tail/pallas_call | solution.py:1197
  508.4 1.3 slice_bitcast_fusion
  509.7 1.7 slice_reduce_fusion
  512.1 4.5 convert_element_type.29
  516.6 2.9 copy.67
  521.3 1.9 copy.73
  523.2 1.4 copy.74
  525.7 1.4 copy.75
  (86 shorter events, 17.6 us)
Async XLA Ops:
  7.2 6.3 %copy-start.14 = (bf16[768]{0:T(1024)(128)(2,1)S(1)}, bf16[768]{0:T(1024)(128)(2,1)}, u32[]{:S(2)}) copy-start(bf16[768]{0:T(1024)(128)(2,1)} %param.24) | copy-start | bytes 4612
  7.2 6.3 %copy-start.15 = (bf16[768]{0:T(1024)(128)(2,1)S(1)}, bf16[768]{0:T(1024)(128)(2,1)}, u32[]{:S(2)}) copy-start(bf16[768]{0:T(1024)(128)(2,1)} %param.25) | copy-start | bytes 4612
  7.2 6.3 %copy-start.7 = (s32[3,576]{1,0:T(4,128)S(1)}, s32[3,576]{1,0:T(4,128)}, u32[]{:S(2)}) copy-start(s32[3,576]{1,0:T(4,128)} %param.21) | copy-start | bytes 20740
  7.2 7.1 %copy-start.11 = (bf16[2,192]{1,0:T(2,128)(2,1)S(1)}, bf16[2,192]{1,0:T(2,128)(2,1)}, u32[]{:S(2)}) copy-start(bf16[2,192]{1,0:T(2,128)(2,1)} %param.27) | copy-start | bytes 2308
  7.2 63.4 %all-gather.6.cloned.1.call-start = ((), (), s32[]{:S(2)}) async-start(), calls=%async_computation.3 | async-start | bytes 1474560 | tf_op jit(solution)/shard_map/all_gather | solution.py:1319
  8.0 91.5 %all-gather.8.cloned.1.call-start = ((), (), s32[]{:S(2)}) async-start(), calls=%async_computation.5 | async-start | bytes 3317760 | tf_op jit(solution)/shard_map/all_gather | solution.py:1323
  15.5 13.5 %copy-start.4 = (bf16[1728,192]{0,1:T(8,128)(2,1)S(1)}, bf16[1728,192]{0,1:T(8,128)(2,1)}, u32[]{:S(2)}) copy-start(bf16[1728,192]{0,1:T(8,128)(2,1)} %param.37) | copy-start | bytes 1990660
  15.5 14.8 %copy-start.8 = (s32[1,1728]{1,0:T(1,128)S(1)}, s32[1,1728]{1,0:T(1,128)}, u32[]{:S(2)}) copy-start(s32[1,1728]{1,0:T(1,128)} %param.23) | copy-start | bytes 20740
  28.9 2.7 copy-start.9
  28.9 198.5 %all-gather.10.cloned.1.call-start = ((), (), s32[]{:S(2)}) async-start(), calls=%async_computation.6 | async-start | bytes 7208960 | tf_op jit(solution)/shard_map/all_gather | solution.py:1339
  42.9 25.3 %copy-start.19 = (bf16[1,192]{1,0:T(2,128)(2,1)S(1)}, bf16[1,192]{1,0:T(2,128)(2,1)}, u32[]{:S(2)}) copy-start(bf16[1,192]{1,0:T(2,128)(2,1)} %param.36) | copy-start | bytes 1156
  42.9 25.3 %copy-start.10 = (bf16[768,8]{0,1:T(8,128)(2,1)S(1)}, bf16[768,8]{0,1:T(8,128)(2,1)}, u32[]{:S(2)}) copy-start(bf16[768,8]{0,1:T(8,128)(2,1)} %param.32) | copy-start | bytes 36868
  42.9 26.2 %copy-start.16 = (bf16[768]{0:T(1024)(128)(2,1)S(1)}, bf16[768]{0:T(1024)(128)(2,1)}, u32[]{:S(2)}) copy-start(bf16[768]{0:T(1024)(128)(2,1)} %param.29) | copy-start | bytes 4612
  42.9 26.2 %copy-start.17 = (bf16[768]{0:T(1024)(128)(2,1)S(1)}, bf16[768]{0:T(1024)(128)(2,1)}, u32[]{:S(2)}) copy-start(bf16[768]{0:T(1024)(128)(2,1)} %param.30) | copy-start | bytes 4612
  42.9 26.2 %copy-start.18 = (bf16[768]{0:T(1024)(128)(2,1)S(1)}, bf16[768]{0:T(1024)(128)(2,1)}, u32[]{:S(2)}) copy-start(bf16[768]{0:T(1024)(128)(2,1)} %param.31) | copy-start | bytes 4612
  42.9 26.3 %copy-start.12 = (bf16[1,768]{1,0:T(2,128)(2,1)S(1)}, bf16[1,768]{1,0:T(2,128)(2,1)}, u32[]{:S(2)}) copy-start(bf16[1,768]{1,0:T(2,128)(2,1)} %param.34) | copy-start | bytes 4612
  67.9 256.5 %reduce-scatter.2.cloned.1.call-start = ((), (), s32[]{:S(2)}) async-start(), calls=%async_computation.4 | async-start | bytes 7208960 | tf_op jit(solution)/shard_map/reduce_scatter | solution.py:1357
  69.9 29.6 %copy-start.13 = (f32[1,768]{1,0:T(1,128)}, f32[1,768]{1,0:T(1,128)S(1)}, u32[]{:S(2)}) copy-start(f32[1,768]{1,0:T(1,128)S(1)} %dynamic_update_slice.3.down_bias_ref) | copy-start | bytes 9220
  182.0 6.1 %copy-start.5 = (s32[8,1728]{1,0:T(8,128)S(1)}, s32[8,1728]{1,0:T(8,128)}, u32[]{:S(2)}) copy-start(s32[8,1728]{1,0:T(8,128)} %get-tuple-element.42.ids_ref) | copy-start | bytes 165892
  184.1 40.0 %all-to-all-start.1 = ((bf16[3,4,144,192]{3,2,0,1:T(8,128)(2,1)}), bf16[3,4,144,192]{3,2,0,1:T(8,128)(2,1)S(1)}, u32[]{:S(2)}, u32[]{:S(2)}) async-start(bf16[3,4,144,192]{3,2,0,1:T(8,128)(2,1)} %copy.63), calls=%async_computation.1 | async-start | bytes 1769472 | tf_op jit(solution)/shard_map/all_to_all | solution.py:1341
  189.3 36.9 %copy-start.6 = (f32[8,1728]{1,0:T(8,128)S(1)}, f32[8,1728]{1,0:T(8,128)}, u32[]{:S(2)}) copy-start(f32[8,1728]{1,0:T(8,128)} %get-tuple-element.49) | copy-start | bytes 165892
  516.6 2.9 copy-start.3
  516.6 6.6 %copy-start.2 = (f32[768,768]{1,0:T(8,128)S(1)}, f32[768,768]{1,0:T(8,128)}, u32[]{:S(2)}) copy-start(f32[768,768]{1,0:T(8,128)} %get-tuple-element.63) | copy-start | bytes 7077892
  523.2 2.5 copy-start.1
  (1 other events, 1.2 us)
Sparse Core Ops, SparseCore 0:
  9.6 33.1 all-gather.5
  44.9 54.4 all-gather.7
  101.0 121.4 all-gather.9
  224.7 99.6 reduce-scatter.1

commit v4 on v3

--- a/solution.py
+++ b/solution.py
@@ -71,12 +71,14 @@
     )
 
 
-def mask_penalty(seg_col, seg_row, live_row):
-    shape = (seg_col.shape[0], seg_row.shape[1])
-    diagonal = lax.broadcasted_iota(jnp.int32, shape, 0) == lax.broadcasted_iota(
-        jnp.int32, shape, 1
+def mask_penalty(seg_row, live_row):
+    count = seg_row.shape[1]
+    diagonal = lax.broadcasted_iota(jnp.int32, (count, count), 0) == lax.broadcasted_iota(
+        jnp.int32, (count, count), 1
     )
-    allowed = (seg_col == seg_row) & ((live_row > 0) | diagonal)
+    number = seg_row.astype(F32)
+    column = jnp.sum(jnp.where(diagonal, number, 0.0), axis=1, keepdims=True)
+    allowed = (column == number) & ((live_row > 0) | diagonal)
     return jnp.where(allowed, 0.0, NEGATIVE)
 
 
@@ -97,79 +99,127 @@
         into[half:, z * width + LANES : (z + 1) * width] = tail[2 * half - count :, extra:]
 
 
-def attend_kernel(
-    tokens_ref, norm_ref, weight_ref, bias_ref, segc_ref, segr_ref, live_ref,
-    first_ref, qkv_ref, context_ref, packed_ref, total_ref,
+def greet(peers):
+    barrier = pltpu.get_barrier_semaphore()
+    me = lax.axis_index("exp")
+    here = lax.axis_index("head")
+
+    def call(step, carry):
+        other = lax.rem(me + step, peers)
+        pl.semaphore_signal(barrier, inc=1, device_id=(other, here), device_id_type=MESH)
+        return carry
+
+    lax.fori_loop(1, peers, call, 0)
+    return barrier
+
+
+def greet_both(peers, head_parts):
+    barrier = greet(peers)
+    me = lax.axis_index("exp")
+    here = lax.axis_index("head")
+
+    def call(step, carry):
+        other = lax.rem(here + step, head_parts)
+        pl.semaphore_signal(barrier, inc=1, device_id=(me, other), device_id_type=MESH)
+        return carry
+
+    lax.fori_loop(1, head_parts, call, 0)
+    return barrier
+
+
+def head_kernel(
+    experts, capacity, stride, half, part_half, seq_count, head_parts,
+    tokens_ref, norm_ref, weight_ref, bias_ref, seg_ref, live_ref, prio_ref, rows_ref, cot_ref,
+    first_ref, qkv_ref, context_ref, total_ref, gathered_ref, ids_ref, cot_recv, own_send, own_tokens_ref,
+    cot_send,
+    gather_sem, gather_out, cot_send_sem, cot_recv_sem,
 ):
-    normal, ignored = standard(tokens_ref[...].astype(F32))
-    first = (normal * norm_ref[0:1] + norm_ref[1:2]).astype(BF16)
-    first_ref[...] = first
-    rows = (dot(first, weight_ref[...]) + bias_ref[...]).astype(BF16)
-    qkv_ref[...] = rows
-    penalty = mask_penalty(segc_ref[0], segr_ref[0], live_ref[0])
-    seqlen = rows.shape[0]
-    width = rows.shape[1] // 3
-    parts = []
-    for head in range(width // HEAD_DIM):
-        lo = head * HEAD_DIM
-        hi = lo + HEAD_DIM
-        query = rows[:, lo:hi] * BF16(1.0 / math.sqrt(HEAD_DIM))
-        scores = dot_last(query, rows[:, width + lo : width + hi]) + penalty
-        largest = jnp.max(scores, axis=-1, keepdims=True)
-        weights = jnp.exp(scores - largest)
-        total = jnp.sum(weights, axis=-1, keepdims=True)
-        values = rows[:, 2 * width + lo : 2 * width + hi]
-        parts.append((dot(weights.astype(BF16), values) / total).astype(BF16))
-        total_ref[:, head : head + 1] = largest + jnp.log(total)
-    context = jnp.concatenate(parts, axis=1)
-    context_ref[...] = context
-    wide, tail = pack_rows(context, seqlen // 2)
-    packed_ref[0, :seqlen] = wide
-    packed_ref[0, seqlen:] = tail
-
-
-def attend(tokens, norm_rows, flat_qkv, bias_row, seg_cols, seg_rows, live_rows):
-    tok_count, model_width = tokens.shape
-    seq_count, seqlen = seg_rows.shape[0], seg_rows.shape[2]
-    wide = flat_qkv.shape[1]
-    width = wide // 3
-    step = lambda i: (i, 0)
-    fixed = lambda i: (0, 0)
-    deep = lambda i: (i, 0, 0)
-    return pl.pallas_call(
-        attend_kernel,
-        grid=(seq_count,),
-        in_specs=[
-            pl.BlockSpec((seqlen, model_width), step),
-            pl.BlockSpec((8, model_width), fixed),
-            pl.BlockSpec((model_width, wide), fixed),
-            pl.BlockSpec((1, wide), fixed),
-            pl.BlockSpec((1, seqlen, 1), deep),
-            pl.BlockSpec((1, 1, seqlen), deep),
-            pl.BlockSpec((1, 1, seqlen), deep),
-        ],
-        out_specs=[
-            pl.BlockSpec((seqlen, model_width), step),
-            pl.BlockSpec((seqlen, wide), step),
-            pl.BlockSpec((seqlen, width), step),
-            pl.BlockSpec((1, seqlen + seqlen // 2, LANES), deep),
-            pl.BlockSpec((seqlen, LANES), step),
-        ],
-        out_shape=[
-            shaped((tok_count, model_width), BF16),
-            shaped((tok_count, wide), BF16),
-            shaped((tok_count, width), BF16),
-            shaped((seq_count, seqlen + seqlen // 2, LANES), BF16),
-            shaped((tok_count, LANES), F32),
-        ],
-        compiler_params=params(),
-        cost_estimate=cost(4e9, 1e7),
-        name="attend",
-    )(tokens, norm_rows, flat_qkv, bias_row, seg_cols, seg_rows, live_rows)
-
-
-def table_kernel(experts, capacity, stride, half, chunk, prio_ref, rows_ref, cot_ref, ids_ref, out_ref):
-    tok_count = rows_ref.shape[1]
+    me = lax.axis_index("exp")
+    here = lax.axis_index("head")
+    barrier = greet_both(experts, head_parts)
+    ends = head_parts - 1
+    tok_count = tokens_ref.shape[0]
+    seqlen = tok_count // seq_count
+    part = seqlen // head_parts
+    pl.semaphore_wait(barrier, experts - 1 + ends)
+
+    def own_rows():
+        for seq in range(seq_count):
+            own = pl.ds(pl.multiple_of(seq * seqlen + here * part, part), part)
+            own_tokens_ref[seq] = tokens_ref[own]
+            for z in range(head_parts):
+                start = seq * seqlen + z * part
+                wide, tail = pack_rows(cot_ref[start : start + part], part_half)
+                own_send[z, seq, :part] = wide
+                own_send[z, seq, part:] = tail
+
+    def attend(seq):
+        span = pl.ds(pl.multiple_of(seq * seqlen, seqlen), seqlen)
+        normal, ignored = standard(tokens_ref[span].astype(F32))
+        first = (normal * norm_ref[0:1] + norm_ref[1:2]).astype(BF16)
+        first_ref[span] = first
+        rows = (dot(first, weight_ref[...]) + bias_ref[...]).astype(BF16)
+        qkv_ref[span] = rows
+        penalty = mask_penalty(seg_ref[pl.ds(seq, 1)], live_ref[pl.ds(seq, 1)])
+        width = rows.shape[1] // 3
+        parts = []
+        for head in range(width // HEAD_DIM):
+            lo = head * HEAD_DIM
+            hi = lo + HEAD_DIM
+            query = rows[:, lo:hi] * BF16(1.0 / math.sqrt(HEAD_DIM))
+            scores = dot_last(query, rows[:, width + lo : width + hi]) + penalty
+            largest = jnp.max(scores, axis=-1, keepdims=True)
+            weights = jnp.exp(scores - largest)
+            total = jnp.sum(weights, axis=-1, keepdims=True)
+            values = rows[:, 2 * width + lo : 2 * width + hi]
+            parts.append((dot(weights.astype(BF16), values) / total).astype(BF16))
+            total_ref[span, head : head + 1] = largest + jnp.log(total)
+        context = jnp.concatenate(parts, axis=1)
+        context_ref[span] = context
+        wide, tail = pack_rows(context, seqlen // 2)
+        gathered_ref[here, seq, :seqlen] = wide
+        gathered_ref[here, seq, seqlen:] = tail
+
+    def full_copy(seq, shard, side):
+        return pltpu.make_async_remote_copy(
+            src_ref=gathered_ref.at[shard, seq],
+            dst_ref=gathered_ref.at[shard, seq],
+            send_sem=gather_out.at[seq, shard, side],
+            recv_sem=gather_sem.at[seq, shard],
+            device_id=(me, here + 1 - 2 * side),
+            device_id_type=MESH,
+        )
+
+    def each_side(hop, action):
+        for side in range(2):
+            shard = here - hop if side == 0 else here + hop
+            there = shard >= 0 if side == 0 else shard <= ends
+            onward = here < ends if side == 0 else here > 0
+            action(side, shard, there, onward)
+
+    def spread_hop(seq, hop):
+        def one(side, shard, there, onward):
+            @pl.when(there)
+            def arrived():
+                if hop > 0:
+                    full_copy(seq, shard, side).wait_recv()
+                if hop < ends:
+
+                    @pl.when(onward)
+                    def pass_on():
+                        full_copy(seq, shard, side).start()
+
+        each_side(hop, one)
+
+    def spread_drain(seq):
+        def one(side, shard, there, onward):
+            @pl.when(there & onward)
+            def sent():
+                full_copy(seq, shard, side).wait_send()
+
+        for hop in range(ends):
+            each_side(hop, one)
+
     numbers = lax.broadcasted_iota(jnp.int32, (experts, 1), 0)
 
     def hot(rows):
@@ -178,52 +228,133 @@
         second = jnp.where((rows[1:2] == numbers) & live, 1.0, 0.0)
         return first, second
 
-    rank_row = rows_ref[3:4]
-    counts = jnp.zeros((2 * experts, tok_count), F32)
-    for start in range(0, tok_count, chunk):
-        first, second = hot(rows_ref[:, start : start + chunk])
-        earlier = jnp.where(prio_ref[start : start + chunk] < rank_row, 1.0, 0.0).astype(BF16)
-        counts = counts + dot(jnp.concatenate([first, second], axis=0).astype(BF16), earlier)
-    first, second = hot(rows_ref[...])
-    total = jnp.sum(first, axis=1, keepdims=True)
-    places = [
-        jnp.sum(first * counts[:experts], axis=0, keepdims=True),
-        jnp.sum(second * (counts[experts:] + total), axis=0, keepdims=True),
-    ]
-    ids = []
-    for pick in range(2):
-        place = places[pick].astype(jnp.int32)
-        kept = (place < capacity) & (rows_ref[2:3] > 0)
-        ids.append(jnp.where(kept, rows_ref[pick : pick + 1] * stride + place, -1))
-        ids_ref[pick : pick + 1] = ids[pick]
-    ids_ref[2:8] = jnp.full((6, tok_count), -1, jnp.int32)
-
-    def one(expert, carry):
-        slots = expert * stride + lax.broadcasted_iota(jnp.int32, (stride, 1), 0)
+    def tables():
+        rank_row = rows_ref[3:4]
+        counts = jnp.zeros((2 * experts, tok_count), F32)
+        for start in range(0, tok_count, seqlen):
+            first, second = hot(rows_ref[:, start : start + seqlen])
+            earlier = jnp.where(prio_ref[start : start + seqlen] < rank_row, 1.0, 0.0)
+            both = jnp.concatenate([first, second], axis=0)
+            counts = counts + dot(both.astype(BF16), earlier.astype(BF16))
+        first, second = hot(rows_ref[...])
+        total = jnp.sum(first, axis=1, keepdims=True)
+        places = [
+            jnp.sum(first * counts[:experts], axis=0, keepdims=True),
+            jnp.sum(second * (counts[experts:] + total), axis=0, keepdims=True),
+        ]
+        for pick in range(2):
+            place = places[pick].astype(jnp.int32)
+            kept = (place < capacity) & (rows_ref[2:3] > 0)
+            ids_ref[pick : pick + 1] = jnp.where(
+                kept, rows_ref[pick : pick + 1] * stride + place, -1
+            )
+        ids_ref[2:8] = jnp.full((6, tok_count), -1, jnp.int32)
+
+    def cot_copy(step, target):
+        return pltpu.make_async_remote_copy(
+            src_ref=cot_send.at[target],
+            dst_ref=cot_recv.at[me],
+            send_sem=cot_send_sem.at[step],
+            recv_sem=cot_recv_sem.at[step],
+            device_id=(target, here),
+            device_id_type=MESH,
+        )
+
+    def fill(target):
+        slots = target * stride + lax.broadcasted_iota(jnp.int32, (stride, 1), 0)
         hit = (ids_ref[0:1] == slots) | (ids_ref[1:2] == slots)
         block = dot(jnp.where(hit, 1.0, 0.0).astype(BF16), cot_ref[...]).astype(BF16)
-        wide, tail = pack_rows(block, half)
-        out_ref[expert, :stride] = wide
-        out_ref[expert, stride:] = tail
+        return pack_rows(block, half)
+
+    def dispatch():
+        def one(step, carry):
+            target = lax.rem(me + step, experts)
+            wide, tail = fill(target)
+            cot_send[target, :stride] = wide
+            cot_send[target, stride:] = tail
+            cot_copy(step, target).start()
+            return carry
+
+        lax.fori_loop(1, experts, one, 0)
+        wide, tail = fill(me)
+        cot_recv[me, :stride] = wide
+        cot_recv[me, stride:] = tail
+
+    def time_step(step, carry):
+        @pl.when(step == seq_count + 1)
+        def send():
+            dispatch()
+
+        for hop in range(ends, 0, -1):
+
+            @pl.when((step >= hop) & (step - hop < seq_count))
+            def move():
+                spread_hop(step - hop, hop)
+
+        @pl.when(step < seq_count)
+        def work():
+            attend(step)
+            spread_hop(step, 0)
+
+        @pl.when(step == seq_count)
+        def places():
+            tables()
+
+        @pl.when(step == seq_count + 1)
+        def rows():
+            own_rows()
+
         return carry
 
-    lax.fori_loop(0, experts, one, 0)
-
-
-def tables(prio_col, rows, cotangent, experts, capacity, stride, half, chunk):
-    tok_count = rows.shape[1]
+    lax.fori_loop(0, seq_count + ends, time_step, 0)
+    for seq in range(seq_count):
+        spread_drain(seq)
+
+    def finish(step, carry):
+        cot_copy(step, lax.rem(me + step, experts)).wait()
+        return carry
+
+    lax.fori_loop(1, experts, finish, 0)
+
+
+def head(
+    tokens, norm_rows, flat_qkv, bias_row, segments, live, prio_col, rows, cotangent,
+    experts, capacity, stride, half, part_half, head_parts,
+):
+    tok_count, model_width = tokens.shape
+    seq_count, seqlen = segments.shape
+    part = seqlen // head_parts
+    wide = flat_qkv.shape[1]
+    width = wide // 3
+    dma = pltpu.SemaphoreType.DMA
+    own = (head_parts, seq_count, part + part_half, LANES)
+    slots = (experts, stride + half, LANES)
     return pl.pallas_call(
-        partial(table_kernel, experts, capacity, stride, half, chunk),
-        in_specs=[whole()] * 3,
-        out_specs=[whole()] * 2,
+        partial(head_kernel, experts, capacity, stride, half, part_half, seq_count, head_parts),
+        in_specs=[whole()] * 9,
+        out_specs=[whole()] * 9,
         out_shape=[
+            shaped((tok_count, model_width), BF16),
+            shaped((tok_count, wide), BF16),
+            shaped((tok_count, width), BF16),
+            shaped((tok_count, LANES), F32),
+            shaped((head_parts, seq_count, seqlen + seqlen // 2, LANES), BF16),
             shaped((8, tok_count), jnp.int32),
-            shaped((experts, stride + half, LANES), BF16),
+            shaped(slots, BF16),
+            shaped(own, BF16),
+            shaped((seq_count, part, model_width), BF16),
         ],
-        compiler_params=params(),
-        cost_estimate=cost(1e10, 1e7),
-        name="tables",
-    )(prio_col, rows, cotangent)
+        scratch_shapes=[
+            pltpu.VMEM(slots, BF16),
+            dma((seq_count, head_parts)),
+            dma((seq_count, head_parts, 2)),
+            dma((experts,)),
+            dma((experts,)),
+        ],
+        compiler_params=params(collective_id=3, has_side_effects=True),
+        cost_estimate=cost(6e10, 1e7),
+        name="head",
+    )(tokens, norm_rows, flat_qkv, bias_row, segments, live, prio_col, rows, cotangent)
 
 
 def gelu_parts(pre):
@@ -237,32 +368,66 @@
     return pre * half_sum, slope
 
 
-def greet(peers):
-    barrier = pltpu.get_barrier_semaphore()
-    me = lax.axis_index("exp")
-    here = lax.axis_index("head")
-
-    def call(step, carry):
-        other = lax.rem(me + step, peers)
-        pl.semaphore_signal(barrier, inc=1, device_id=(other, here), device_id_type=MESH)
-        return carry
-
-    lax.fori_loop(1, peers, call, 0)
-    return barrier
-
-
 def forward_kernel(
     experts, stride, half, seq_count, head_parts,
     gathered_ref, tokens_ref, vectors_ref, out_weight_ref, router_ref, rows_ref, ids_ref,
-    up_ref, up_bias_ref, down_ref, down_bias_ref,
+    up_ref, up_bias_ref, down_ref, down_bias_ref, cot_hbm,
     own_residual_ref, own_second_ref, own_columns_ref, gates_ref, arrived_ref, hidden_ref, result_ref,
-    gate_col_ref, residual_ref, context_scr, second_scr, logit_scr, send_scr, gate_send, gate_recv,
-    send_sem, recv_sem, gate_send_sem, gate_recv_sem,
+    gate_col_ref, cot_all, residual_ref, context_scr, second_scr, logit_scr, send_scr, gate_send, gate_recv,
+    send_sem, recv_sem, gate_send_sem, gate_recv_sem, cot_sem, cot_out, local_sem,
 ):
     me = lax.axis_index("exp")
     here = lax.axis_index("head")
-    barrier = greet(experts)
+    barrier = greet_both(experts, head_parts)
+    ends = head_parts - 1
+    pieces = cot_sem.shape[1]
+    piece_rows = experts // pieces
     tok_count = tokens_ref.shape[0]
+
+    def cot_copy(shard, piece, side, own=False):
+        span = pl.ds(piece * piece_rows, piece_rows)
+        return pltpu.make_async_remote_copy(
+            src_ref=cot_hbm.at[span] if own else cot_all.at[shard, span],
+            dst_ref=cot_all.at[shard, span],
+            send_sem=cot_out.at[shard, piece, side],
+            recv_sem=cot_sem.at[shard, piece],
+            device_id=(me, here + 1 - 2 * side),
+            device_id_type=MESH,
+        )
+
+    def cot_side(hop, side):
+        shard = here - hop if side == 0 else here + hop
+        there = shard >= 0 if side == 0 else shard <= ends
+        onward = here < ends if side == 0 else here > 0
+        return shard, there, onward
+
+    def cot_hop(hop, piece):
+        for side in range(2):
+            shard, there, onward = cot_side(hop, side)
+
+            @pl.when(there)
+            def arrived():
+                if hop > 0:
+                    cot_copy(shard, piece, side).wait_recv()
+                if hop < ends:
+
+                    @pl.when(onward)
+                    def pass_on():
+                        cot_copy(shard, piece, side, hop == 0).start()
+
+    def cot_drain(hop, piece):
+        for side in range(2):
+            shard, there, onward = cot_side(hop, side)
+
+            @pl.when(there & onward)
+            def sent():
+                cot_copy(shard, piece, side, hop == 0).wait_send()
+
+    local = pltpu.make_async_copy(cot_hbm, cot_all.at[here], local_sem.at[0])
+    local.start()
+    pl.semaphore_wait(barrier, experts - 1 + ends)
+    for piece in range(pieces):
+        cot_hop(0, piece)
     seqlen = tok_count // seq_count
     for seq in range(seq_count):
         span = slice(seq * seqlen, (seq + 1) * seqlen)
@@ -299,7 +464,6 @@
         gate = jnp.where(ids_ref[pick : pick + 1] >= 0, jnp.sum(chosen, axis=0, keepdims=True), 0.0)
         gates_ref[pick : pick + 1] = gate
     gates_ref[2:8] = jnp.zeros((6, tok_count), F32)
-    pl.semaphore_wait(barrier, experts - 1)
 
     def copies(target, step):
         to = dict(device_id=(target, here), device_id_type=MESH)
@@ -357,8 +521,18 @@
             result_ref[z, source, stride:] = tail
 
     work(me)
+    moves = [(hop, piece) for hop in range(1, ends) for piece in range(pieces)]
+    early = len(moves) - min(experts - 2, len(moves))
+    for move in moves[:early]:
+        cot_hop(*move)
 
     def receive(step, carry):
+        for place, move in enumerate(moves[early:]):
+
+            @pl.when(step == place + 1)
+            def pass_on():
+                cot_hop(*move)
+
         source = lax.rem(me + experts - step, experts)
         wide, narrow = copies(source, step)
         wide.wait_recv()
@@ -374,6 +548,11 @@
         return carry
 
     lax.fori_loop(1, experts, finish, 0)
+    for piece in range(pieces):
+        cot_hop(ends, piece)
+        for hop in range(ends):
+            cot_drain(hop, piece)
+    local.wait()
     lane = lax.broadcasted_iota(jnp.int32, (LANES, stride), 0)
     square = jnp.zeros((LANES, stride), F32)
     for source in range(experts):
@@ -382,7 +561,7 @@
 
 
 def forward(
-    gathered, tokens, vectors, out_weight, router, rows, ids, up, up_bias, down, down_bias,
+    gathered, tokens, vectors, out_weight, router, rows, ids, up, up_bias, down, down_bias, cot_slots,
     experts, stride, half, seq_count, head_parts,
 ):
     tok_count, model_width = tokens.shape
@@ -390,8 +569,8 @@
     part = seqlen // head_parts
     return pl.pallas_call(
         partial(forward_kernel, experts, stride, half, seq_count, head_parts),
-        in_specs=[whole()] * 11,
-        out_specs=[whole()] * 8,
+        in_specs=[whole()] * 11 + [anywhere()],
+        out_specs=[whole()] * 8 + [anywhere()],
         out_shape=[
             shaped((seq_count, part, model_width), F32),
             shaped((seq_count, part, model_width), BF16),
@@ -401,6 +580,7 @@
             shaped((experts, stride, up.shape[1]), BF16),
             shaped((head_parts, experts, stride + half, LANES), BF16),
             shaped((stride, LANES), F32),
+            shaped((head_parts, experts, stride + half, LANES), BF16),
         ],
         scratch_shapes=[
             pltpu.VMEM((tok_count, model_width), F32),
@@ -414,11 +594,14 @@
             pltpu.SemaphoreType.DMA((experts,)),
             pltpu.SemaphoreType.DMA((experts,)),
             pltpu.SemaphoreType.DMA((experts,)),
+            pltpu.SemaphoreType.DMA((head_parts, 4)),
+            pltpu.SemaphoreType.DMA((head_parts, 4, 2)),
+            pltpu.SemaphoreType.DMA((1,)),
         ],
         compiler_params=params(collective_id=0, has_side_effects=True),
         cost_estimate=cost(8e10, 1e8),
         name="forward",
-    )(gathered, tokens, vectors, out_weight, router, rows, ids, up, up_bias, down, down_bias)
+    )(gathered, tokens, vectors, out_weight, router, rows, ids, up, up_bias, down, down_bias, cot_slots)
 
 
 def backward_kernel(
@@ -620,19 +803,19 @@
 
 
 def tail_kernel(
-    experts, stride, half, seq_count, head_parts,
-    sums_ref, id_cols_ref, gate_cols_ref, own_residual_ref, own_second_ref, cot_own_ref,
-    own_columns_hbm, router_ref, vectors_ref, own_tokens_ref, norm_ref, result_ref,
+    experts, stride, half, part_half, seq_count, head_parts, gap,
+    sums_ref, id_cols_ref, gate_cols_ref, own_residual_ref, own_second_ref, cot_own_hbm,
+    own_columns_hbm, router_ref, vectors_ref, own_tokens_ref, norm_ref, result_hbm,
     context_hbm, first_hbm, qkv_hbm, totals_hbm, weight_ref, out_weight_ref,
-    segc_ref, segr_ref, live_ref,
+    seg_ref, live_ref,
     tokens_hbm, block_ref, qkv_sum_ref, out_sum_ref, bias_sum_ref, small_ref,
-    columns_scr, part_two, down_one, up_one, down_two, up_two, own_scr,
+    own_recv, cot_wide, columns_scr, part_two, down_one, up_one, down_two, up_two, own_scr,
     full_one, full_two, grad_scr,
-    context_scr, first_scr, qkv_scr, totals_scr, back_scr, penalty_scr, joined_scr,
+    context_scr, first_scr, qkv_scr, totals_scr, back_scr, joined_scr,
     qkv_grad, out_grad, bias_grad, rows_acc, router_acc,
     result_home, result_wide,
     qkv_send, qkv_recv, qkv_all, out_send, out_recv, out_all, bias_recv, small_head, small_recv,
-    columns_sem, load_sem, stage_sem, result_send_sem, result_recv_sem,
+    own_send_sem, own_recv_sem, columns_sem, load_sem, stage_sem, result_send_sem, result_recv_sem,
     down_one_sem, up_one_sem, down_two_sem, up_two_sem, down_one_out, up_one_out, down_two_out, up_two_out,
     full_one_sem, full_two_sem, full_one_out, full_two_out,
     sum_send_sem, sum_recv_sem, all_send_sem, all_recv_sem,
@@ -641,20 +824,13 @@
     me = lax.axis_index("exp")
     here = lax.axis_index("head")
     ends = head_parts - 1
-    seqlen = segr_ref.shape[2]
+    seqlen = seg_ref.shape[1]
     part = seqlen // head_parts
     model_width = vectors_ref.shape[1]
     width = out_weight_ref.shape[0]
     factor = 1.0 / math.sqrt(HEAD_DIM)
 
-    barrier = greet(experts)
-
-    def call(step, carry):
-        other = lax.rem(here + step, head_parts)
-        pl.semaphore_signal(barrier, inc=1, device_id=(me, other), device_id_type=MESH)
-        return carry
-
-    lax.fori_loop(1, head_parts, call, 0)
+    barrier = greet_both(experts, head_parts)
 
     def chunk_loads(seq):
         span = pl.ds(pl.multiple_of(seq * seqlen, seqlen), seqlen)
@@ -689,15 +865,26 @@
 
     def result_copy(step, target):
         return pltpu.make_async_remote_copy(
-            src_ref=result_ref.at[target],
+            src_ref=result_hbm.at[target],
             dst_ref=result_home.at[me],
             send_sem=result_send_sem.at[step],
             recv_sem=result_recv_sem.at[step],
             **to_exp(target),
         )
 
-    each_peer(lambda step, target, source: result_copy(step, target).start())
-    result_home[me] = result_ref[me]
+    def own_copy(seq, step):
+        target = lax.rem(here + step, head_parts)
+        return pltpu.make_async_remote_copy(
+            src_ref=cot_own_hbm.at[target, seq],
+            dst_ref=own_recv.at[here, seq],
+            send_sem=own_send_sem.at[seq, step],
+            recv_sem=own_recv_sem.at[seq, step],
+            **to_head(target),
+        )
+
+    own_local = pltpu.make_async_copy(cot_own_hbm.at[here], own_recv.at[here], columns_sem.at[1])
+    own_local.start()
+    own_local.wait()
 
     def down_copy(buffer, sems, outs, seq, shard):
         return pltpu.make_async_remote_copy(
@@ -838,7 +1025,10 @@
         normal, scale = standard(own_residual_ref[seq])
         rows_acc[0:1] += jnp.sum(grad * normal, axis=0, keepdims=True)
         rows_acc[1:2] += jnp.sum(grad, axis=0, keepdims=True)
-        total = cot_own_ref[seq].astype(F32) + norm_back(grad, vectors_ref[1:2], normal, scale)
+        for other in range(1, head_parts):
+            own_copy(seq, other).wait_recv()
+        unpack_rows(lambda z: own_recv[z, seq], cot_wide, head_parts, part, part_half)
+        total = cot_wide[...].astype(F32) + norm_back(grad, vectors_ref[1:2], normal, scale)
         rows_acc[2:3] += jnp.sum(total, axis=0, keepdims=True)
         grad_scr[seq] = total
         full_one[seq, pl.ds(pl.multiple_of(here * part, part), part)] = total.astype(BF16)
@@ -849,9 +1039,9 @@
         grad = full_one[seq]
         back_scr[...] = dot_last(grad, out_weight_ref[...]).astype(BF16)
         out_grad[...] += dot_first(context_scr[...], grad)
-        penalty_scr[...] = mask_penalty(segc_ref[seq], segr_ref[seq], live_ref[seq]).astype(BF16)
-
-    def attend_head(head):
+        return mask_penalty(seg_ref[pl.ds(seq, 1)], live_ref[pl.ds(seq, 1)])
+
+    def attend_head(head, penalty):
         lo = head * HEAD_DIM
         hi = lo + HEAD_DIM
         query = qkv_scr[:, lo:hi] * BF16(factor)
@@ -859,7 +1049,7 @@
         values = qkv_scr[:, 2 * width + lo : 2 * width + hi]
         back = back_scr[:, lo:hi]
         weights = jnp.exp(
-            dot_last(query, keys) + penalty_scr[...].astype(F32) - totals_scr[:, head : head + 1]
+            dot_last(query, keys) + penalty - totals_scr[:, head : head + 1]
         )
         joined_scr[:, 2 * width + lo : 2 * width + hi] = dot_first(
             weights.astype(BF16), back
@@ -873,7 +1063,8 @@
 
     def attend_end(seq):
         joined = joined_scr[...]
-        part_two[...] = dot_last(joined, weight_ref[...]).astype(BF16)
+        span = pl.ds(pl.multiple_of(lax.rem(seq, 2) * seqlen, seqlen), seqlen)
+        part_two[span] = dot_last(joined, weight_ref[...]).astype(BF16)
         qkv_grad[...] += dot_first(first_scr[...], joined)
         bias_grad[0:1] += jnp.sum(joined.astype(F32), axis=0, keepdims=True)
 
@@ -1087,64 +1278,94 @@
     heads = width // HEAD_DIM
     router_rows = small_head.shape[1] - 8
 
-    def at(step, offset, action):
-        seq = step - offset
-
-        @pl.when((seq >= 0) & (seq < seq_count))
-        def run():
-            action(seq)
-
-    def time_step(step, carry):
-        at(step, 2, attend_start)
-        for hop in range(max(ends, heads)):
-            if hop < ends:
-                at(
-                    step,
-                    0,
-                    lambda seq: reduce_hop(sums_ref, seq * seqlen, one_down, one_up, seq, hop),
-                )
-                at(step, 3, lambda seq: reduce_hop(part_two, 0, two_down, two_up, seq, hop))
-                at(step, 1, lambda seq: spread_hop(one_full, seq, hop))
-                at(step, 4, lambda seq: spread_hop(two_full, seq, hop))
-            if hop < heads:
-                at(step, 2, lambda seq: attend_head(hop))
+    second_start = 2 * ends
+    spread_start = second_start + ends
+    ticks = spread_start + ends + 1 + gap * (seq_count - 1)
+    final = gap * (seq_count - 1)
+
+    def tick(now, carry):
+        def on(offset, action):
+            since = now - offset
+
+            @pl.when((since >= 0) & (lax.rem(since, gap) == 0) & (since < gap * seq_count))
+            def run():
+                action(since // gap)
 
         def first_end(seq):
             reduce_end(sums_ref, seq * seqlen, one_down, one_up, seq, model_width + LANES)
             middle(seq)
 
+        def attend(seq):
+            spread_hop(one_full, seq, ends)
+            penalty = attend_start(seq)
+            for head in range(heads):
+                attend_head(head, penalty)
+            attend_end(seq)
+
         def second_end(seq):
-            reduce_end(part_two, 0, two_down, two_up, seq, model_width)
+            reduce_end(part_two, lax.rem(seq, 2) * seqlen, two_down, two_up, seq, model_width)
             last(seq)
 
         def tokens_end(seq):
             spread_hop(two_full, seq, ends)
             stage_copy(seq).start()
 
-        at(step, 0, first_end)
-        at(step, 3, second_end)
-        at(step, 2, attend_end)
-        at(step, 1, lambda seq: spread_hop(one_full, seq, ends))
-
-        @pl.when(step == seq_count + 1)
+        def own_begin(seq):
+            for other in range(1, head_parts):
+                own_copy(seq, other).start()
+
+        on(ends, first_end)
+        on(spread_start, second_end)
+        for hop in range(ends):
+            on(hop, lambda seq: reduce_hop(sums_ref, seq * seqlen, one_down, one_up, seq, hop))
+            on(ends + hop, lambda seq: spread_hop(one_full, seq, hop))
+            if hop > 0:
+                on(
+                    second_start + hop,
+                    lambda seq: reduce_hop(
+                        part_two, lax.rem(seq, 2) * seqlen, two_down, two_up, seq, hop
+                    ),
+                )
+            on(spread_start + hop, lambda seq: spread_hop(two_full, seq, hop))
+        on(0, own_begin)
+        on(second_start, attend)
+        on(
+            second_start,
+            lambda seq: reduce_hop(part_two, lax.rem(seq, 2) * seqlen, two_down, two_up, seq, 0),
+        )
+
+        @pl.when(now == 0)
+        def send_results():
+            each_peer(lambda step, target, source: result_copy(step, target).start())
+            local = pltpu.make_async_copy(result_hbm.at[me], result_home.at[me], columns_sem.at[1])
+            local.start()
+            local.wait()
+
+        @pl.when(now == ends + 1)
+        def results():
+            open_results()
+
+        on(ends + 2, combine)
+
+        @pl.when(now == final + second_start)
         def sums():
             start_sums()
-            open_results()
-
-        at(step, 4, combine)
-
-        @pl.when(step == seq_count + 2)
+
+        @pl.when(now == final + spread_start)
         def small():
             small_head[here, :8] = rows_acc[...]
             small_head[here, 8:] = router_acc[...].T[:router_rows]
             for other in range(1, head_parts):
                 head_copy(other).start()
+
+        @pl.when(now == final + spread_start + 1)
+        def share():
             spread_sums()
 
-        at(step, 4, tokens_end)
+        on(spread_start + ends, tokens_end)
         return carry
 
-    lax.fori_loop(0, seq_count + 4, time_step, 0)
+    lax.fori_loop(0, ticks, tick, 0)
 
     for other in range(1, head_parts):
         head_arrival(other).wait_recv()
@@ -1166,6 +1387,8 @@
         spread_drain(two_full, seq)
     for other in range(1, head_parts):
         head_copy(other).wait_send()
+        for seq in range(seq_count):
+            own_copy(seq, other).wait_send()
 
     def sent(step, target, source):
         result_copy(step, target).wait_send()
@@ -1182,7 +1405,7 @@
 def tail(
     sums, id_cols, gate_cols, own_residual, own_second, cot_own, own_columns, router, vectors,
     own_tokens, norm_rows, result, context, first, qkv, totals, flat_qkv, out_weight,
-    seg_cols, seg_rows, live_rows, stride, half, head_parts,
+    segments, live, stride, half, part_half, head_parts,
 ):
     experts = result.shape[0]
     model_width = first.shape[1]
@@ -1195,8 +1418,8 @@
     small_rows = 8 + round_up(experts, 8)
     dma = pltpu.SemaphoreType.DMA
     return pl.pallas_call(
-        partial(tail_kernel, experts, stride, half, seq_count, head_parts),
-        in_specs=[whole()] * 6 + [anywhere()] + [whole()] * 5 + [anywhere()] * 4 + [whole()] * 5,
+        partial(tail_kernel, experts, stride, half, part_half, seq_count, head_parts, 2),
+        in_specs=[whole()] * 5 + [anywhere()] * 2 + [whole()] * 4 + [anywhere()] * 5 + [whole()] * 4,
         out_specs=[anywhere()] + [whole()] * 5,
         out_shape=[
             shaped((tok_count, model_width), BF16),
@@ -1207,8 +1430,10 @@
             shaped((small_rows, model_width), F32),
         ],
         scratch_shapes=[
+            pltpu.VMEM(cot_own.shape, BF16),
+            pltpu.VMEM((part, model_width), BF16),
             pltpu.VMEM((seqlen, width), F32),
-            pltpu.VMEM((seqlen, model_width), BF16),
+            pltpu.VMEM((2 * seqlen, model_width), BF16),
             pltpu.VMEM((seq_count, ends, part, model_width + LANES), BF16),
             pltpu.VMEM((seq_count, ends, part, model_width + LANES), BF16),
             pltpu.VMEM((seq_count, ends, part, model_width), BF16),
@@ -1222,7 +1447,6 @@
             pltpu.VMEM((seqlen, wide), BF16),
             pltpu.VMEM((seqlen, LANES), F32),
             pltpu.VMEM((seqlen, width), BF16),
-            pltpu.VMEM((seqlen, seqlen), BF16),
             pltpu.VMEM((seqlen, wide), BF16),
             pltpu.VMEM((model_width, wide), F32),
             pltpu.VMEM((width, model_width), F32),
@@ -1240,7 +1464,9 @@
             pltpu.VMEM((experts, 8, wide), F32),
             pltpu.VMEM((head_parts, small_rows, model_width), F32),
             pltpu.VMEM((experts, small_rows, model_width), F32),
-            dma((1,)),
+            dma((seq_count, head_parts)),
+            dma((seq_count, head_parts)),
+            dma((2,)),
             dma((4,)),
             dma((seq_count,)),
             dma((experts,)),
@@ -1259,7 +1485,7 @@
     )(
         sums, id_cols, gate_cols, own_residual, own_second, cot_own, own_columns, router, vectors,
         own_tokens, norm_rows, result, context, first, qkv, totals, flat_qkv, out_weight,
-        seg_cols, seg_rows, live_rows,
+        segments, live,
     )
 
 
@@ -1307,9 +1533,6 @@
         [qv_bias[0], jnp.zeros((local_width,), qv_bias.dtype), qv_bias[1]]
     ).astype(F32)[None]
     router_wide = jnp.pad(router, ((0, 0), (0, LANES - experts)))
-    seg_rows = segments.reshape(seq_count, 1, seqlen)
-    live_rows = live_mask.reshape(seq_count, 1, seqlen)
-    seg_cols = segments.reshape(seq_count, seqlen, 1)
     down_bias_row = lax.dynamic_update_slice_in_dim(
         jnp.zeros((1, model_width), F32), down_bias.astype(F32), head_index * quarter, 1
     )
@@ -1317,11 +1540,6 @@
     up_bias_row = up_bias.astype(F32)
 
     out_full_weight = lax.all_gather(out_weight, "head", axis=0, tiled=True)
-    first, qkv, context, packed, totals = attend(
-        tokens, norm_rows, flat_qkv, bias_row, seg_cols, seg_rows, live_rows
-    )
-    gathered = lax.all_gather(packed, "head", axis=0)
-
     int_rows = jnp.concatenate(
         [
             routes.T,
@@ -1331,27 +1549,15 @@
         ],
         axis=0,
     )
-    ids, cot_slots = tables(
-        priority.reshape(tok_count, 1), int_rows, cotangent, experts, capacity, stride, half, seqlen
+    part_half = round_up(seqlen // head_parts // 2, 16)
+    first, qkv, context, totals, gathered, ids, cot_slots, cot_own, own_tokens = head(
+        tokens, norm_rows, flat_qkv, bias_row, segments, live_mask, priority.reshape(tok_count, 1),
+        int_rows, cotangent, experts, capacity, stride, half, part_half, head_parts,
     )
     id_cols = ids.T
-    cot_moved = lax.all_to_all(cot_slots, "exp", split_axis=0, concat_axis=0, tiled=True)
-    cot_rows = lax.all_gather(cot_moved, "head", axis=0)
-    part = seqlen // head_parts
-    cot_own = lax.all_to_all(
-        cotangent.reshape(seq_count, head_parts, part, quarter),
-        "head",
-        split_axis=1,
-        concat_axis=3,
-        tiled=True,
-    ).reshape(seq_count, part, model_width)
-    own_tokens = lax.dynamic_slice_in_dim(
-        tokens.reshape(seq_count, seqlen, model_width), head_index * part, part, 1
-    )
-
-    own_residual, own_second, own_columns, gates, arrived, hidden, result, gate_col = forward(
+    own_residual, own_second, own_columns, gates, arrived, hidden, result, gate_col, cot_rows = forward(
         gathered, tokens, vectors, out_full_weight, router_wide, int_rows, ids,
-        up, up_bias_row, down, down_bias_row, experts, stride, half, seq_count, head_parts,
+        up, up_bias_row, down, down_bias_row, cot_slots, experts, stride, half, seq_count, head_parts,
     )
     gate_cols = gates.T
     own_result = lax.psum_scatter(result, "head", scatter_dimension=0, tiled=True)[0]
@@ -1362,7 +1568,7 @@
     grad_tokens, block_out, qkv_grad, out_grad, bias_grad, small = tail(
         sums, id_cols, gate_cols, own_residual, own_second, cot_own, own_columns,
         router_wide, vectors, own_tokens, norm_rows, own_result, context, first, qkv, totals,
-        flat_qkv, out_weight, seg_cols, seg_rows, live_rows, stride, half, head_parts,
+        flat_qkv, out_weight, segments, live_mask, stride, half, part_half, head_parts,
     )
     grad_qv_bias = jnp.concatenate(
         [bias_grad[0:1, :local_width], bias_grad[0:1, 2 * local_width :]], axis=0

time: 540 us -> 516 us (0.956)
  Pallas kernels: 365 us -> 433 us
  waiting for transfers between devices: 81.7 us -> 22.7 us
  blocking collectives: 25 us -> 0 us
    pallas_call x3 -> x2, Pallas kernels: 208 us -> 251 us  [the longest x1 177 us: tail(): pl.pallas_call(partial(tail_kernel, experts, stride, half, part_half, seq...]
    all_to_all x1 -> x0, waiting for transfers between devices: 32.8 us -> none  [body(): lax.all_to_all(cotangent.reshape(seq_count, head_parts, part, quarter), '...]
    all_gather x2 -> x0, waiting for transfers between devices: 28.9 us -> none  [the longest x1 28.9 us: body(): gathered = lax.all_gather(packed, 'head', axis=0)]
    pallas_call x1, Pallas kernels: 82.5 us -> 108 us  [forward(): pl.pallas_call(partial(forward_kernel, experts, stride, half, seq_count,...]
    all_to_all x1 -> x0, blocking collectives: 25 us -> none  [body(): lax.all_to_all(cot_slots, 'exp', split_axis=0, concat_axis=0, tiled=True)]
    reshape x5 -> x0, local copies, waits for them, and re-layouts: 6.49 us -> none  [the longest x1 1.95 us: body(): seg_cols = segments.reshape(seq_count, seqlen, 1)]
    unnamed x46 -> x32, local copies, waits for them, and re-layouts: 9.57 us -> 11 us
  transfers between devices with their start and end apart: 5 -> 2, of which waited for: 3 -> 1; matrix products, arithmetic and copies ran while one was open for 4% -> 4% of each run, Pallas kernels for 34% -> 29%
where the time goes in v4:
time: 516 us; the launch traced here: 508 us
  Pallas kernels  433 us (84%)
  local copies, waits for them, and re-layouts  31.9 us (6%)
  waiting for transfers between devices  22.7 us (4%)
  between operations  14.4 us (3%)
  other arithmetic  5.92 us (1%)
    pallas_call x1, Pallas kernels, tail(): pl.pallas_call(partial(tail_kernel, experts, stride, half, part_half, seq...  177 us
    pallas_call x1, Pallas kernels, forward(): pl.pallas_call(partial(forward_kernel, experts, stride, half, seq_count,...  108 us
    pallas_call x1, Pallas kernels, backward(): pl.pallas_call(partial(backward_kernel, experts, stride, half, head_parts...  74.9 us
    pallas_call x1, Pallas kernels, head(): pl.pallas_call(partial(head_kernel, experts, capacity, stride, half, part...  73.8 us
    reduce_scatter x1, waiting for transfers between devices, body(): lax.psum_scatter(result, 'head', scatter_dimension=0, tiled=True)[0]  22 us
    unnamed x32, local copies, waits for them, and re-layouts  11 us
  transfers between devices with their start and end apart: 2, of which 1 were waited for; matrix products, arithmetic and copies ran while one was open for 4% of the time, Pallas kernels for 29%

profile of v4, /device:TPU:0, one launch (start us, length us, event | category | flops | bytes accessed | tf_op | source)
XLA Modules:
  0.0 508.4 jit_solution(14782861082570651036)
XLA Ops:
  8.2 0.8 fusion.3
  12.4 0.8 reshape.110
  13.2 2.3 copy.43.cot_ref
  15.5 1.9 copy.42.prio_ref
  17.5 1.3 copy.41.weight_ref
  20.8 73.8 %head.1 = (bf16[1728,768]{1,0:T(8,128)(2,1)}, bf16[1728,576]{1,0:T(8,128)(2,1)}, bf16[1728,192]{1,0:T(8,128)(2,1)}, f32[1728,128]{1,0:T(8,128)}, bf16[4,3,864,12...) custom-call(bf16[1728,768]{1,0:T(8,128)(2,1)} %tokens_ref.3, ...), custom_call_target="tpu_custom_call" | custom-call | flops 60000002048 | bytes 10000000 | tf_op jit(solution)/shard_map/head/pallas_call | solution.py:332
  96.9 107.7 %forward.1 = (f32[3,144,768]{2,1,0:T(8,128)}, bf16[3,144,768]{2,1,0:T(8,128)(2,1)}, f32[1728,192]{1,0:T(8,128)}, f32[8,1728]{1,0:T(8,128)}, bf16[8,464,768]{2,1,...) custom-call(bf16[4,3,864,128]{3,2,1,0:T(8,128)(2,1)} %get-tuple-elem, ...), custom_call_target="tpu_custom_call" | custom-call | flops 80000000000 | bytes 100000000 | tf_op jit(solution)/shard_map/forward/pallas_call | solution.py:570
  204.6 0.8 copy-done.5
  205.4 1.2 copy.45
  206.6 74.9 %backward.1 = (bf16[1728,896]{1,0:T(8,128)(2,1)}, f32[768,768]{1,0:T(8,128)}, f32[8,768]{1,0:T(8,128)}, f32[768,768]{1,0:T(8,128)}, f32[8,768]{1,0:T(8,128)}) custom-call(bf16[8,464,768]{2,1,0:T(8,128)(2,1)} %get-tuple-element.47.arrived_hbm, bf16[8,464,768]{2,1,0:T(8,128)(2,1)} %get-tuple-element.48.hidden_hbm, ...), custom_call_target="tpu_custom_call" | custom-call | flops 80000000000 | bytes 100000000 | tf_op jit(solution)/shard_map/backward/pallas_call | solution.py:768
  281.5 1.3 slice.46
  282.8 0.7 slice.47
  283.6 1.2 copy.46
  285.4 22.0 %reduce-scatter.2.cloned.1.call-done = bf16[1,8,704,128]{3,2,1,0:T(8,128)(2,1)} async-done(((bf16[4,8,704,128]{3,2,1,0:T(8,128)(2,1)}), bf16[1,8,704,128]{3,2,1,0:T(8,128)(2,1)}) %reduce-scatter.2.cloned.1.call-update) | async-done | bytes 1441808 | tf_op jit(solution)/shard_map/reduce_scatter | solution.py:1563
  307.4 177.0 %tail.1 = (bf16[1728,768]{1,0:T(8,128)(2,1)}, bf16[1728,192]{1,0:T(8,128)(2,1)}, f32[768,576]{1,0:T(8,128)}, f32[192,768]{1,0:T(8,128)}, f32[8,576]{1,0:T(8,128)}, /*index=5*/f32[16,768]{1,0:T(8,128)}) custom-call(bf16[1728,896]{1,0:T(8,128)(2,1)} %get-tuple-element.52.sums_ref, s32[1728,8]{1,0:T(8,128)} %bitcast.18, f32[1728,8]{1,0:T(8,128)} %bitcast.19, ...), custom_call_target="tpu_custom_call" | custom-call | flops 99999997952 | bytes 100000000 | tf_op jit(solution)/shard_map/tail/pallas_call | solution.py:1420
  484.4 1.6 slice_reduce_fusion
  486.0 1.3 slice_bitcast_fusion
  487.4 2.5 copy.49
  490.5 2.8 copy.48
  493.3 2.8 convert_element_type.29
  496.7 0.8 copy.54
  497.5 1.4 copy.55
  498.9 1.1 copy-done.1
  500.0 1.4 copy.56
  (54 shorter events, 10.6 us)
Async XLA Ops:
  7.2 12.3 %copy-start.7 = (s32[1,1728]{1,0:T(1,128)S(1)}, s32[1,1728]{1,0:T(1,128)}, u32[]{:S(2)}) copy-start(s32[1,1728]{1,0:T(1,128)} %param.23) | copy-start | bytes 20740
  7.2 10.3 %copy-start.3 = (bf16[768,3,192]{0,2,1:T(8,128)(2,1)S(1)}, bf16[768,3,192]{0,2,1:T(8,128)(2,1)}, u32[]{:S(2)}) copy-start(bf16[768,3,192]{0,2,1:T(8,128)(2,1)} %param.26) | copy-start | bytes 2654212
  7.2 12.2 %copy-start.8 = (s32[1728,2]{0,1:T(2,128)S(1)}, s32[1728,2]{0,1:T(2,128)}, u32[]{:S(2)}) copy-start(s32[1728,2]{0,1:T(2,128)} %param.22) | copy-start | bytes 41476
  7.2 89.1 %all-gather.2.cloned.1.call-start = ((), (), s32[]{:S(2)}) async-start(), calls=%async_computation.1 | async-start | bytes 1474560 | tf_op jit(solution)/shard_map/all_gather | solution.py:1542
  7.9 299.4 %reduce-scatter.2.cloned.1.call-start = ((), (), s32[]{:S(2)}) async-start(), calls=%async_computation.2 | async-start | bytes 7208960 | tf_op jit(solution)/shard_map/reduce_scatter | solution.py:1563
  20.8 73.9 %copy-start.12 = (bf16[1,192]{1,0:T(2,128)(2,1)S(1)}, bf16[1,192]{1,0:T(2,128)(2,1)}, u32[]{:S(2)}) copy-start(bf16[1,192]{1,0:T(2,128)(2,1)} %param.36) | copy-start | bytes 1156
  20.8 73.9 %copy-start.10 = (bf16[1,768]{1,0:T(2,128)(2,1)S(1)}, bf16[1,768]{1,0:T(2,128)(2,1)}, u32[]{:S(2)}) copy-start(bf16[1,768]{1,0:T(2,128)(2,1)} %param.34) | copy-start | bytes 4612
  20.8 74.5 %copy-start.9 = (bf16[768,8]{0,1:T(8,128)(2,1)S(1)}, bf16[768,8]{0,1:T(8,128)(2,1)}, u32[]{:S(2)}) copy-start(bf16[768,8]{0,1:T(8,128)(2,1)} %param.32) | copy-start | bytes 36868
  96.3 0.6 copy-start.11
  204.6 0.8 copy-start.5
  206.6 76.9 %copy-start.6 = (f32[8,1728]{1,0:T(8,128)S(1)}, f32[8,1728]{1,0:T(8,128)}, u32[]{:S(2)}) copy-start(f32[8,1728]{1,0:T(8,128)} %get-tuple-element.53) | copy-start | bytes 165892
  487.4 5.9 %copy-start = (bf16[1728,768]{1,0:T(8,128)(2,1)S(1)}, bf16[1728,768]{1,0:T(8,128)(2,1)}, u32[]{:S(2)}) copy-start(bf16[1728,768]{1,0:T(8,128)(2,1)} %get-tuple-element.64) | copy-start | bytes 7962628
  493.3 3.4 copy-start.4
  493.3 4.2 copy-start.2
  497.5 2.5 copy-start.1
Sparse Core Ops, SparseCore 0:
  9.6 36.4 all-gather.1
  204.7 102.5 reduce-scatter.1

commit v5 on v4

--- a/solution.py
+++ b/solution.py
@@ -71,15 +71,20 @@
     )
 
 
-def mask_penalty(seg_row, live_row):
-    count = seg_row.shape[1]
-    diagonal = lax.broadcasted_iota(jnp.int32, (count, count), 0) == lax.broadcasted_iota(
+def diagonal_of(count):
+    return lax.broadcasted_iota(jnp.int32, (count, count), 0) == lax.broadcasted_iota(
         jnp.int32, (count, count), 1
     )
-    number = seg_row.astype(F32)
-    column = jnp.sum(jnp.where(diagonal, number, 0.0), axis=1, keepdims=True)
-    allowed = (column == number) & ((live_row > 0) | diagonal)
-    return jnp.where(allowed, 0.0, NEGATIVE)
+
+
+def as_column(row, diagonal):
+    return jnp.sum(jnp.where(diagonal, row.astype(F32), 0.0), axis=1, keepdims=True)
+
+
+def mask_penalty(seg_row, live_row):
+    diagonal = diagonal_of(seg_row.shape[1])
+    same = as_column(seg_row, diagonal) == seg_row.astype(F32)
+    return jnp.where(same & ((live_row > 0) | diagonal), 0.0, NEGATIVE)
 
 
 def pack_rows(rows, half):
@@ -129,10 +134,11 @@
 
 def head_kernel(
     experts, capacity, stride, half, part_half, seq_count, head_parts,
-    tokens_ref, norm_ref, weight_ref, bias_ref, seg_ref, live_ref, prio_ref, rows_ref, cot_ref,
-    first_ref, qkv_ref, context_ref, total_ref, gathered_ref, ids_ref, cot_recv, own_send, own_tokens_ref,
-    cot_send,
-    gather_sem, gather_out, cot_send_sem, cot_recv_sem,
+    tokens_ref, norm_ref, weight_ref, bias_ref, seg_ref, live_ref, rows_ref, cot_ref, out_weight_ref,
+    first_hbm, qkv_hbm, context_hbm, total_hbm, out_full_ref, gathered_ref, ids_ref, cot_recv, own_send, own_tokens_ref,
+    cot_send, first_scr, qkv_scr, context_scr, total_scr,
+    gather_sem, gather_out, cot_send_sem, cot_recv_sem, store_sem,
+    weight_sem, weight_out, pair_send_sem, pair_recv_sem,
 ):
     me = lax.axis_index("exp")
     here = lax.axis_index("head")
@@ -153,13 +159,79 @@
                 own_send[z, seq, :part] = wide
                 own_send[z, seq, part:] = tail
 
+    core = lax.rem(me, 2)
+    weight_rows = out_weight_ref.shape[0]
+    half_rows = weight_rows // 2
+
+    def weight_span(shard, which):
+        start = pl.multiple_of(shard * weight_rows + which * half_rows, 16)
+        return pl.ds(start, half_rows)
+
+    def weight_copy(shard, side):
+        rows = weight_span(shard, core)
+        return pltpu.make_async_remote_copy(
+            src_ref=out_full_ref.at[rows],
+            dst_ref=out_full_ref.at[rows],
+            send_sem=weight_out.at[shard, side],
+            recv_sem=weight_sem.at[shard],
+            device_id=(me, here + 1 - 2 * side),
+            device_id_type=MESH,
+        )
+
+    def pair_copy(step, which):
+        rows = weight_span(lax.rem(here + step, head_parts), which)
+        return pltpu.make_async_remote_copy(
+            src_ref=out_full_ref.at[rows],
+            dst_ref=out_full_ref.at[rows],
+            send_sem=pair_send_sem.at[step],
+            recv_sem=pair_recv_sem.at[step],
+            device_id=(me + 1 - 2 * core, here),
+            device_id_type=MESH,
+        )
+
+    def weight_hop(hop):
+        def one(side, shard, there, onward):
+            @pl.when(there)
+            def arrived():
+                if hop > 0:
+                    weight_copy(shard, side).wait_recv()
+                if hop < ends:
+
+                    @pl.when(onward)
+                    def pass_on():
+                        weight_copy(shard, side).start()
+
+        each_side(hop, one)
+        if hop == ends:
+            for step in range(1, head_parts):
+                pair_copy(step, core).start()
+
+    def stores(seq):
+        slot = lax.rem(seq, 2)
+        span = pl.ds(pl.multiple_of(seq * seqlen, seqlen), seqlen)
+        return (
+            pltpu.make_async_copy(first_scr.at[slot], first_hbm.at[span], store_sem.at[slot, 0]),
+            pltpu.make_async_copy(qkv_scr.at[slot], qkv_hbm.at[span], store_sem.at[slot, 1]),
+            pltpu.make_async_copy(context_scr.at[slot], context_hbm.at[span], store_sem.at[slot, 2]),
+            pltpu.make_async_copy(total_scr.at[slot], total_hbm.at[span], store_sem.at[slot, 3]),
+        )
+
     def attend(seq):
+        slot = lax.rem(seq, 2)
         span = pl.ds(pl.multiple_of(seq * seqlen, seqlen), seqlen)
+
+        @pl.when(seq >= 2)
+        def free():
+            for copy in stores(seq - 2):
+                copy.wait()
+
         normal, ignored = standard(tokens_ref[span].astype(F32))
         first = (normal * norm_ref[0:1] + norm_ref[1:2]).astype(BF16)
-        first_ref[span] = first
-        rows = (dot(first, weight_ref[...]) + bias_ref[...]).astype(BF16)
-        qkv_ref[span] = rows
+        first_scr[slot] = first
+        bias = bias_ref[...].astype(F32)
+        bias_row = jnp.concatenate([bias[0:1], jnp.zeros_like(bias[0:1]), bias[1:2]], axis=1)
+        rows = (dot(first, weight_ref[...]) + bias_row).astype(BF16)
+        qkv_scr[slot] = rows
         penalty = mask_penalty(seg_ref[pl.ds(seq, 1)], live_ref[pl.ds(seq, 1)])
         width = rows.shape[1] // 3
         parts = []
@@ -173,9 +245,11 @@
             total = jnp.sum(weights, axis=-1, keepdims=True)
             values = rows[:, 2 * width + lo : 2 * width + hi]
             parts.append((dot(weights.astype(BF16), values) / total).astype(BF16))
-            total_ref[span, head : head + 1] = largest + jnp.log(total)
+            total_scr[slot, :, head : head + 1] = largest + jnp.log(total)
         context = jnp.concatenate(parts, axis=1)
-        context_ref[span] = context
+        context_scr[slot] = context
+        for copy in stores(seq):
+            copy.start()
         wide, tail = pack_rows(context, seqlen // 2)
         gathered_ref[here, seq, :seqlen] = wide
         gathered_ref[here, seq, seqlen:] = tail
@@ -229,11 +303,13 @@
         return first, second
 
     def tables():
-        rank_row = rows_ref[3:4]
+        rank_row = rows_ref[3:4].astype(F32)
+        diagonal = diagonal_of(seqlen)
         counts = jnp.zeros((2 * experts, tok_count), F32)
         for start in range(0, tok_count, seqlen):
             first, second = hot(rows_ref[:, start : start + seqlen])
-            earlier = jnp.where(prio_ref[start : start + seqlen] < rank_row, 1.0, 0.0)
+            rank_col = as_column(rank_row[:, start : start + seqlen], diagonal)
+            earlier = jnp.where(rank_col < rank_row, 1.0, 0.0)
             both = jnp.concatenate([first, second], axis=0)
             counts = counts + dot(both.astype(BF16), earlier.astype(BF16))
         first, second = hot(rows_ref[...])
@@ -280,7 +356,16 @@
         cot_recv[me, :stride] = wide
         cot_recv[me, stride:] = tail
 
+    out_full_ref[pl.ds(pl.multiple_of(here * weight_rows, 16), weight_rows)] = out_weight_ref[...]
+    weight_hop(0)
+
     def time_step(step, carry):
+        for hop in range(1, ends + 1):
+
+            @pl.when(step == hop)
+            def weights():
+                weight_hop(hop)
+
         @pl.when(step == seq_count + 1)
         def send():
             dispatch()
@@ -309,6 +394,20 @@
     lax.fori_loop(0, seq_count + ends, time_step, 0)
     for seq in range(seq_count):
         spread_drain(seq)
+    for seq in range(max(seq_count - 2, 0), seq_count):
+        for copy in stores(seq):
+            copy.wait()
+
+    def sent(side, shard, there, onward):
+        @pl.when(there & onward)
+        def drain():
+            weight_copy(shard, side).wait_send()
+
+    for hop in range(ends):
+        each_side(hop, sent)
+    for step in range(1, head_parts):
+        pair_copy(step, core).wait_send()
+        pair_copy(step, 1 - core).wait_recv()
 
     def finish(step, carry):
         cot_copy(step, lax.rem(me + step, experts)).wait()
@@ -318,7 +417,7 @@
 
 
 def head(
-    tokens, norm_rows, flat_qkv, bias_row, segments, live, prio_col, rows, cotangent,
+    tokens, vectors, flat_qkv, qv_bias, segments, live, rows, cotangent, out_weight,
     experts, capacity, stride, half, part_half, head_parts,
 ):
     tok_count, model_width = tokens.shape
@@ -332,12 +431,13 @@
     return pl.pallas_call(
         partial(head_kernel, experts, capacity, stride, half, part_half, seq_count, head_parts),
         in_specs=[whole()] * 9,
-        out_specs=[whole()] * 9,
+        out_specs=[anywhere()] * 4 + [whole()] * 6,
         out_shape=[
             shaped((tok_count, model_width), BF16),
             shaped((tok_count, wide), BF16),
             shaped((tok_count, width), BF16),
             shaped((tok_count, LANES), F32),
+            shaped((head_parts * out_weight.shape[0], model_width), BF16),
             shaped((head_parts, seq_count, seqlen + seqlen // 2, LANES), BF16),
             shaped((8, tok_count), jnp.int32),
             shaped(slots, BF16),
@@ -346,15 +446,24 @@
         ],
         scratch_shapes=[
             pltpu.VMEM(slots, BF16),
+            pltpu.VMEM((2, seqlen, model_width), BF16),
+            pltpu.VMEM((2, seqlen, wide), BF16),
+            pltpu.VMEM((2, seqlen, width), BF16),
+            pltpu.VMEM((2, seqlen, LANES), F32),
             dma((seq_count, head_parts)),
             dma((seq_count, head_parts, 2)),
             dma((experts,)),
             dma((experts,)),
+            dma((2, 4)),
+            dma((head_parts,)),
+            dma((head_parts, 2)),
+            dma((head_parts,)),
+            dma((head_parts,)),
         ],
         compiler_params=params(collective_id=3, has_side_effects=True),
         cost_estimate=cost(6e10, 1e7),
         name="head",
-    )(tokens, norm_rows, flat_qkv, bias_row, segments, live, prio_col, rows, cotangent)
+    )(tokens, vectors, flat_qkv, qv_bias, segments, live, rows, cotangent, out_weight)
 
 
 def gelu_parts(pre):
@@ -372,9 +481,10 @@
     experts, stride, half, seq_count, head_parts,
     gathered_ref, tokens_ref, vectors_ref, out_weight_ref, router_ref, rows_ref, ids_ref,
     up_ref, up_bias_ref, down_ref, down_bias_ref, cot_hbm,
-    own_residual_ref, own_second_ref, own_columns_ref, gates_ref, arrived_ref, hidden_ref, result_ref,
-    gate_col_ref, cot_all, residual_ref, context_scr, second_scr, logit_scr, send_scr, gate_send, gate_recv,
+    own_residual_ref, own_second_ref, own_columns_ref, gates_ref, arrived_hbm, hidden_hbm, result_hbm,
+    gate_col_ref, cot_all, arrived_ref, hidden_scr, result_scr, residual_ref, context_scr, second_scr, logit_scr, send_scr, gate_send, gate_recv,
     send_sem, recv_sem, gate_send_sem, gate_recv_sem, cot_sem, cot_out, local_sem,
+    arrived_sem, store_sem,
 ):
     me = lax.axis_index("exp")
     here = lax.axis_index("head")
@@ -435,11 +545,11 @@
         residual = (
             tokens_ref[span].astype(F32)
             + dot(context_scr[...], out_weight_ref[...])
-            + vectors_ref[0:1]
+            + vectors_ref[2:3]
         )
         residual_ref[span] = residual
         normal, ignored = standard(residual)
-        second = (normal * vectors_ref[1:2] + vectors_ref[2:3]).astype(BF16)
+        second = (normal * vectors_ref[3:4] + vectors_ref[4:5]).astype(BF16)
         second_scr[span] = second
         logit_scr[:, span] = dot(second, router_ref[...]).T[:experts]
     part = seqlen // head_parts
@@ -510,17 +620,47 @@
     arrived_ref[me] = block
     gate_recv[me] = gate
 
-    def work(source):
-        pre = dot(arrived_ref[source], up_ref[...]) + up_bias_ref[...]
+    def source_of(step):
+        return lax.rem(me + experts - step, experts)
+
+    def arrived_store(step):
+        source = source_of(step)
+        return pltpu.make_async_copy(
+            arrived_ref.at[source], arrived_hbm.at[source], arrived_sem.at[step]
+        )
+
+    def stores(step):
+        source = source_of(step)
+        slot = lax.rem(step, 2)
+        return (
+            pltpu.make_async_copy(hidden_scr.at[slot], hidden_hbm.at[source], store_sem.at[slot, 0]),
+            pltpu.make_async_copy(result_scr.at[slot], result_hbm.at[:, source], store_sem.at[slot, 1]),
+        )
+
+    def work(step):
+        source = source_of(step)
+        slot = lax.rem(step, 2)
+        arrived_store(step).start()
+        pre = dot(arrived_ref[source], up_ref[...]) + up_bias_ref[...].astype(F32)
         hidden = gelu_parts(pre)[0].astype(BF16)
-        hidden_ref[source] = hidden
-        result = (dot(hidden, down_ref[...]) + down_bias_ref[...]).astype(BF16)
+        result = dot(hidden, down_ref[...])
+        down_bias = down_bias_ref[...].astype(F32)
+
+        @pl.when(step >= 2)
+        def free():
+            for copy in stores(step - 2):
+                copy.wait()
+
+        hidden_scr[slot] = hidden
         for z in range(head_parts):
-            wide, tail = pack_rows(result[:, z * width : (z + 1) * width], half)
-            result_ref[z, source, :stride] = wide
-            result_ref[z, source, stride:] = tail
-
-    work(me)
+            columns = result[:, z * width : (z + 1) * width] + jnp.where(here == z, down_bias, 0.0)
+            wide, tail = pack_rows(columns.astype(BF16), half)
+            result_scr[slot, z, :stride] = wide
+            result_scr[slot, z, stride:] = tail
+        for copy in stores(step):
+            copy.start()
+
+    work(0)
     moves = [(hop, piece) for hop in range(1, ends) for piece in range(pieces)]
     early = len(moves) - min(experts - 2, len(moves))
     for move in moves[:early]:
@@ -537,10 +677,20 @@
         wide, narrow = copies(source, step)
         wide.wait_recv()
         narrow.wait_recv()
-        work(source)
+        work(step)
         return carry
 
     lax.fori_loop(1, experts, receive, 0)
+
+    for step in (experts - 2, experts - 1):
+        for copy in stores(step):
+            copy.wait()
+
+    def stored(step, carry):
+        arrived_store(step).wait()
+        return carry
+
+    lax.fori_loop(0, experts, stored, 0)
 
     def finish(step, carry):
         for copy in copies(lax.rem(me + step, experts), step):
@@ -570,7 +720,7 @@
     return pl.pallas_call(
         partial(forward_kernel, experts, stride, half, seq_count, head_parts),
         in_specs=[whole()] * 11 + [anywhere()],
-        out_specs=[whole()] * 8 + [anywhere()],
+        out_specs=[whole()] * 4 + [anywhere()] * 3 + [whole()] + [anywhere()],
         out_shape=[
             shaped((seq_count, part, model_width), F32),
             shaped((seq_count, part, model_width), BF16),
@@ -583,6 +733,9 @@
             shaped((head_parts, experts, stride + half, LANES), BF16),
         ],
         scratch_shapes=[
+            pltpu.VMEM((experts, stride, model_width), BF16),
+            pltpu.VMEM((2, stride, up.shape[1]), BF16),
+            pltpu.VMEM((2, head_parts, stride + half, LANES), BF16),
             pltpu.VMEM((tok_count, model_width), F32),
             pltpu.VMEM((seqlen, model_width), BF16),
             pltpu.VMEM((tok_count, model_width), BF16),
@@ -597,6 +750,8 @@
             pltpu.SemaphoreType.DMA((head_parts, 4)),
             pltpu.SemaphoreType.DMA((head_parts, 4, 2)),
             pltpu.SemaphoreType.DMA((1,)),
+            pltpu.SemaphoreType.DMA((experts,)),
+            pltpu.SemaphoreType.DMA((2, 2)),
         ],
         compiler_params=params(collective_id=0, has_side_effects=True),
         cost_estimate=cost(8e10, 1e8),
@@ -663,7 +818,7 @@
         unpack_rows(lambda z: cot_scr[slot, z], cot_wide, head_parts, stride, half)
         unpack_rows(lambda z: result_scr[slot, z], result_wide, head_parts, stride, half)
         out_rows = cot_wide[...].astype(F32)
-        pre = dot(rows_scr[slot], up_ref[...]) + up_bias_ref[...]
+        pre = dot(rows_scr[slot], up_ref[...]) + up_bias_ref[...].astype(F32)
         slope = gelu_parts(pre)[1]
         lane = lax.broadcasted_iota(jnp.int32, (stride, LANES), 1)
         gate = jnp.sum(jnp.where(lane == home, gate_col_ref[...], 0.0), axis=1, keepdims=True)
@@ -802,10 +957,30 @@
     )(arrived, hidden, result, cot_rows, gate_col, id_cols, up, up_bias, down)
 
 
+def copy_kernel(first_ref, second_ref, first_out, second_out):
+    first_out[...] = first_ref[...]
+    second_out[...] = second_ref[...]
+
+
+def copies_of(first, second):
+    rows = first.shape[0] // 4
+    specs = [pl.BlockSpec((rows, a.shape[1]), lambda i: (i, 0)) for a in (first, second)]
+    return pl.pallas_call(
+        copy_kernel,
+        grid=(4,),
+        in_specs=specs,
+        out_specs=specs,
+        out_shape=[shaped(first.shape, F32), shaped(second.shape, F32)],
+        compiler_params=params(),
+        cost_estimate=cost(0, 1e7),
+        name="copies",
+    )(first, second)
+
+
 def tail_kernel(
     experts, stride, half, part_half, seq_count, head_parts, gap,
     sums_ref, id_cols_ref, gate_cols_ref, own_residual_ref, own_second_ref, cot_own_hbm,
-    own_columns_hbm, router_ref, vectors_ref, own_tokens_ref, norm_ref, result_hbm,
+    own_columns_hbm, router_ref, vectors_ref, own_tokens_ref, result_hbm,
     context_hbm, first_hbm, qkv_hbm, totals_hbm, weight_ref, out_weight_ref,
     seg_ref, live_ref,
     tokens_hbm, block_ref, qkv_sum_ref, out_sum_ref, bias_sum_ref, small_ref,
@@ -1028,7 +1203,7 @@
         for other in range(1, head_parts):
             own_copy(seq, other).wait_recv()
         unpack_rows(lambda z: own_recv[z, seq], cot_wide, head_parts, part, part_half)
-        total = cot_wide[...].astype(F32) + norm_back(grad, vectors_ref[1:2], normal, scale)
+        total = cot_wide[...].astype(F32) + norm_back(grad, vectors_ref[3:4], normal, scale)
         rows_acc[2:3] += jnp.sum(total, axis=0, keepdims=True)
         grad_scr[seq] = total
         full_one[seq, pl.ds(pl.multiple_of(here * part, part), part)] = total.astype(BF16)
@@ -1078,7 +1253,7 @@
         normal, scale = standard(own_tokens_ref[seq].astype(F32))
         rows_acc[3:4] += jnp.sum(grad * normal, axis=0, keepdims=True)
         rows_acc[4:5] += jnp.sum(grad, axis=0, keepdims=True)
-        total = grad_scr[seq] + norm_back(grad, norm_ref[0:1], normal, scale)
+        total = grad_scr[seq] + norm_back(grad, vectors_ref[0:1], normal, scale)
         full_two[seq, pl.ds(pl.multiple_of(here * part, part), part)] = total.astype(BF16)
 
     def stage_copy(seq):
@@ -1351,6 +1526,10 @@
         def sums():
             start_sums()
 
+        @pl.when(now == final + second_start + 2)
+        def share():
+            spread_sums()
+
         @pl.when(now == final + spread_start)
         def small():
             small_head[here, :8] = rows_acc[...]
@@ -1359,22 +1538,21 @@
                 head_copy(other).start()
 
         @pl.when(now == final + spread_start + 1)
-        def share():
-            spread_sums()
+        def small_on():
+            for other in range(1, head_parts):
+                head_arrival(other).wait_recv()
+            total = small_head[0]
+            for other in range(1, head_parts):
+                total = total + small_head[other]
+            small_recv[me] = total
+            each_peer(lambda step, target, source: small_copy(step, target).start())
+            end_sums()
 
         on(spread_start + ends, tokens_end)
         return carry
 
     lax.fori_loop(0, ticks, tick, 0)
 
-    for other in range(1, head_parts):
-        head_arrival(other).wait_recv()
-    total = small_head[0]
-    for other in range(1, head_parts):
-        total = total + small_head[other]
-    small_recv[me] = total
-    each_peer(lambda step, target, source: small_copy(step, target).start())
-    end_sums()
     each_peer(lambda step, target, source: small_arrival(step, source).wait_recv())
     small_ref[...] = lax.fori_loop(
         1, experts, lambda source, total: total + small_recv[source], small_recv[0]
@@ -1404,7 +1582,7 @@
 
 def tail(
     sums, id_cols, gate_cols, own_residual, own_second, cot_own, own_columns, router, vectors,
-    own_tokens, norm_rows, result, context, first, qkv, totals, flat_qkv, out_weight,
+    own_tokens, result, context, first, qkv, totals, flat_qkv, out_weight,
     segments, live, stride, half, part_half, head_parts,
 ):
     experts = result.shape[0]
@@ -1419,7 +1597,7 @@
     dma = pltpu.SemaphoreType.DMA
     return pl.pallas_call(
         partial(tail_kernel, experts, stride, half, part_half, seq_count, head_parts, 2),
-        in_specs=[whole()] * 5 + [anywhere()] * 2 + [whole()] * 4 + [anywhere()] * 5 + [whole()] * 4,
+        in_specs=[whole()] * 5 + [anywhere()] * 2 + [whole()] * 3 + [anywhere()] * 5 + [whole()] * 4,
         out_specs=[anywhere()] + [whole()] * 5,
         out_shape=[
             shaped((tok_count, model_width), BF16),
@@ -1484,7 +1662,7 @@
         name="tail",
     )(
         sums, id_cols, gate_cols, own_residual, own_second, cot_own, own_columns, router, vectors,
-        own_tokens, norm_rows, result, context, first, qkv, totals, flat_qkv, out_weight,
+        own_tokens, result, context, first, qkv, totals, flat_qkv, out_weight,
         segments, live,
     )
 
@@ -1521,25 +1699,13 @@
     half = round_up(stride // 2, 16)
     local_width = qkv_weight.shape[2]
 
-    def vector_rows(*vectors):
-        rows = [v.astype(F32).reshape(1, -1) for v in vectors]
-        rows.append(jnp.zeros((8 - len(rows), model_width), F32))
-        return jnp.concatenate(rows, axis=0)
-
-    norm_rows = vector_rows(norm1_gain, norm1_bias)
-    vectors = vector_rows(out_bias, norm2_gain, norm2_bias)
+    rows_of = [norm1_gain, norm1_bias, out_bias, norm2_gain, norm2_bias]
+    spare = jnp.zeros(((8 - len(rows_of)) * model_width,), BF16)
+    vectors = jnp.concatenate(rows_of + [spare]).astype(F32).reshape(8, model_width)
     flat_qkv = qkv_weight.reshape(model_width, 3 * local_width)
-    bias_row = jnp.concatenate(
-        [qv_bias[0], jnp.zeros((local_width,), qv_bias.dtype), qv_bias[1]]
-    ).astype(F32)[None]
     router_wide = jnp.pad(router, ((0, 0), (0, LANES - experts)))
-    down_bias_row = lax.dynamic_update_slice_in_dim(
-        jnp.zeros((1, model_width), F32), down_bias.astype(F32), head_index * quarter, 1
-    )
     up, down = up_weight[0], down_weight[0]
-    up_bias_row = up_bias.astype(F32)
-
-    out_full_weight = lax.all_gather(out_weight, "head", axis=0, tiled=True)
+
     int_rows = jnp.concatenate(
         [
             routes.T,
@@ -1550,24 +1716,26 @@
         axis=0,
     )
     part_half = round_up(seqlen // head_parts // 2, 16)
-    first, qkv, context, totals, gathered, ids, cot_slots, cot_own, own_tokens = head(
-        tokens, norm_rows, flat_qkv, bias_row, segments, live_mask, priority.reshape(tok_count, 1),
-        int_rows, cotangent, experts, capacity, stride, half, part_half, head_parts,
+    first, qkv, context, totals, out_full_weight, gathered, ids, cot_slots, cot_own, own_tokens = head(
+        tokens, vectors, flat_qkv, qv_bias, segments, live_mask, int_rows, cotangent, out_weight, experts, capacity, stride, half, part_half, head_parts,
     )
     id_cols = ids.T
     own_residual, own_second, own_columns, gates, arrived, hidden, result, gate_col, cot_rows = forward(
         gathered, tokens, vectors, out_full_weight, router_wide, int_rows, ids,
-        up, up_bias_row, down, down_bias_row, cot_slots, experts, stride, half, seq_count, head_parts,
+        up, up_bias, down, down_bias, cot_slots, experts, stride, half, seq_count, head_parts,
     )
     gate_cols = gates.T
     own_result = lax.psum_scatter(result, "head", scatter_dimension=0, tiled=True)[0]
     sums, grad_up, grad_up_bias, grad_down, grad_down_bias = backward(
-        arrived, hidden, result, cot_rows, gate_col, id_cols, up, up_bias_row, down, half, head_parts,
+        arrived, hidden, result, cot_rows, gate_col, id_cols, up, up_bias, down, half, head_parts,
         seqlen,
+    )
+    grad_up, grad_down, own_result = lax.optimization_barrier(
+        (*copies_of(grad_up, grad_down), own_result)
     )
     grad_tokens, block_out, qkv_grad, out_grad, bias_grad, small = tail(
         sums, id_cols, gate_cols, own_residual, own_second, cot_own, own_columns,
-        router_wide, vectors, own_tokens, norm_rows, own_result, context, first, qkv, totals,
+        router_wide, vectors, own_tokens, own_result, context, first, qkv, totals,
         flat_qkv, out_weight, segments, live_mask, stride, half, part_half, head_parts,
     )
     grad_qv_bias = jnp.concatenate(

time: 516 us -> 493 us (0.955)
  local copies, waits for them, and re-layouts: 31.9 us -> 23.8 us
  Pallas kernels: 433 us -> 425 us
  waiting for transfers between devices: 22.7 us -> 16.8 us
    pallas_call x1, Pallas kernels: 73.8 us -> 68.3 us  [head(): pl.pallas_call(partial(head_kernel, experts, capacity, stride, half, part...]
    reshape x6 -> x0, local copies, waits for them, and re-layouts: 5.35 us -> none  [the longest x5 3.42 us: vector_rows(): rows = [v.astype(F32).reshape(1, -1) for v in vectors]]
    reduce_scatter x1, waiting for transfers between devices: 22 us -> 16.8 us  [body(): lax.psum_scatter(result, 'head', scatter_dimension=0, tiled=True)[0]]
    unnamed x32 -> x27, local copies, waits for them, and re-layouts: 11 us -> 8.48 us
  transfers between devices with their start and end apart: 2 -> 1, of which waited for: 1 -> 1; matrix products, arithmetic and copies ran while one was open for 4% -> 1% of each run, Pallas kernels for 29% -> 16%
where the time goes in v5:
time: 493 us; the launch traced here: 486 us
  Pallas kernels  425 us (86%)
  local copies, waits for them, and re-layouts  23.8 us (5%)
  waiting for transfers between devices  16.8 us (3%)
  between operations  14.3 us (3%)
  other arithmetic  5.96 us (1%)
    pallas_call x1, Pallas kernels, tail(): pl.pallas_call(partial(tail_kernel, experts, stride, half, part_half, seq...  173 us
    pallas_call x1, Pallas kernels, forward(): pl.pallas_call(partial(forward_kernel, experts, stride, half, seq_count,...  104 us
    pallas_call x1, Pallas kernels, backward(): pl.pallas_call(partial(backward_kernel, experts, stride, half, head_parts...  74.4 us
    pallas_call x1, Pallas kernels, head(): pl.pallas_call(partial(head_kernel, experts, capacity, stride, half, part...  68.3 us
    reduce_scatter x1, waiting for transfers between devices, body(): lax.psum_scatter(result, 'head', scatter_dimension=0, tiled=True)[0]  16.8 us
  transfers between devices with their start and end apart: 1, of which 1 were waited for; matrix products, arithmetic and copies ran while one was open for 1% of the time, Pallas kernels for 16%

profile of v5, /device:TPU:0, one launch (start us, length us, event | category | flops | bytes accessed | tf_op | source)
XLA Modules:
  0.0 485.6 jit_solution(17562932531063156646)
XLA Ops:
  7.3 0.9 dynamic-update-slice
  8.2 0.8 dynamic-update-slice.1
  9.1 0.9 dynamic-update-slice.2
  9.9 0.9 dynamic-update-slice.3
  10.8 0.9 dynamic-update-slice.4
  12.5 2.2 copy.41.weight_ref
  14.7 0.8 reshape.44
  15.6 1.2 copy.42.cot_ref
  18.4 68.3 %head.1 = (bf16[1728,768]{1,0:T(8,128)(2,1)}, bf16[1728,576]{1,0:T(8,128)(2,1)}, bf16[1728,192]{1,0:T(8,128)(2,1)}, f32[1728,128]{1,0:T(8,128)}, bf16[768,768]{1...) custom-call(bf16[1728,768]{1,0:T(8,128)(2,1)} %tokens_ref.3, ...), custom_call_target="tpu_custom_call" | custom-call | flops 60000002048 | bytes 10000000 | tf_op jit(solution)/shard_map/head/pallas_call | solution.py:431
  86.8 104.1 %forward.1 = (f32[3,144,768]{2,1,0:T(8,128)}, bf16[3,144,768]{2,1,0:T(8,128)(2,1)}, f32[1728,192]{1,0:T(8,128)}, f32[8,1728]{1,0:T(8,128)}, bf16[8,464,768]{2,1,...) custom-call(bf16[4,3,864,128]{3,2,1,0:T(8,128)(2,1)} %get-tuple-elem, ...), custom_call_target="tpu_custom_call" | custom-call | flops 80000000000 | bytes 100000000 | tf_op jit(solution)/shard_map/forward/pallas_call | solution.py:720
  190.9 0.8 copy-done.4
  191.7 1.2 copy.44
  192.9 1.2 copy.45
  194.2 74.4 %backward.1 = (bf16[1728,896]{1,0:T(8,128)(2,1)}, f32[768,768]{1,0:T(8,128)}, f32[8,768]{1,0:T(8,128)}, f32[768,768]{1,0:T(8,128)}, f32[8,768]{1,0:T(8,128)}) custom-call(bf16[8,464,768]{2,1,0:T(8,128)(2,1)} %get-tuple-element.54.arrived_hbm, bf16[8,464,768]{2,1,0:T(8,128)(2,1)} %get-tuple-element.55.hidden_hbm, ...), custom_call_target="tpu_custom_call" | custom-call | flops 80000000000 | bytes 100000000 | tf_op jit(solution)/shard_map/backward/pallas_call | solution.py:923
  269.3 1.3 slice.38
  270.6 5.0 %copies.1 = (f32[768,768]{1,0:T(8,128)}, f32[768,768]{1,0:T(8,128)}) custom-call(f32[768,768]{1,0:T(8,128)} %get-tuple-element.66.first_ref, f32[768,768]{1,0:T(8,128)} %get-tuple-element.67.second_ref), custom_call_target="tpu_custom_call" | custom-call | bytes 10000000 | tf_op jit(solution)/shard_map/copies/pallas_call | solution.py:968
  276.2 16.8 %reduce-scatter.2.cloned.1.call-done = bf16[1,8,704,128]{3,2,1,0:T(8,128)(2,1)} async-done(((bf16[4,8,704,128]{3,2,1,0:T(8,128)(2,1)}), bf16[1,8,704,128]{3,2,1,0:T(8,128)(2,1)}) %reduce-scatter.2.cloned.1.call-update) | async-done | bytes 1441808 | tf_op jit(solution)/shard_map/reduce_scatter | solution.py:1728
  293.0 172.9 %tail.1 = (bf16[1728,768]{1,0:T(8,128)(2,1)}, bf16[1728,192]{1,0:T(8,128)(2,1)}, f32[768,576]{1,0:T(8,128)}, f32[192,768]{1,0:T(8,128)}, f32[8,576]{1,0:T(8,128)}, /*index=5*/f32[16,768]{1,0:T(8,128)}) custom-call(bf16[1728,896]{1,0:T(8,128)(2,1)} %get-tuple-element.59.sums_ref, s32[1728,8]{1,0:T(8,128)} %bitcast.15, f32[1728,8]{1,0:T(8,128)} %bitcast.16, ...), custom_call_target="tpu_custom_call" | custom-call | flops 99999997952 | bytes 100000000 | tf_op jit(solution)/shard_map/tail/pallas_call | solution.py:1598
  465.9 1.3 slice_bitcast_fusion
  467.3 1.7 slice_reduce_fusion
  469.6 4.7 convert_element_type.14
  474.3 1.7 copy.47
  476.0 1.1 copy.48
  477.8 0.8 copy.56
  (32 shorter events, 5.3 us)
Async XLA Ops:
  7.2 8.4 %copy-start.2 = (bf16[1728,192]{0,1:T(8,128)(2,1)S(1)}, bf16[1728,192]{0,1:T(8,128)(2,1)}, u32[]{:S(2)}) copy-start(bf16[1728,192]{0,1:T(8,128)(2,1)} %param.37) | copy-start | bytes 1990660
  7.2 9.7 %copy-start.7 = (bf16[768,8]{0,1:T(8,128)(2,1)S(1)}, bf16[768,8]{0,1:T(8,128)(2,1)}, u32[]{:S(2)}) copy-start(bf16[768,8]{0,1:T(8,128)(2,1)} %param.32) | copy-start | bytes 36868
  7.2 10.5 %copy-start.6 = (s32[1728,2]{0,1:T(2,128)S(1)}, s32[1728,2]{0,1:T(2,128)}, u32[]{:S(2)}) copy-start(s32[1728,2]{0,1:T(2,128)} %param.22) | copy-start | bytes 41476
  7.2 10.5 %copy-start.8 = (s32[1,1728]{1,0:T(1,128)S(1)}, s32[1,1728]{1,0:T(1,128)}, u32[]{:S(2)}) copy-start(s32[1,1728]{1,0:T(1,128)} %param.23) | copy-start | bytes 20740
  7.2 285.8 %reduce-scatter.2.cloned.1.call-start = ((), (), s32[]{:S(2)}) async-start(), calls=%async_computation.1 | async-start | bytes 7208960 | tf_op jit(solution)/shard_map/reduce_scatter | solution.py:1728
  190.9 0.8 copy-start.4
  190.9 2.0 copy-start.5
  469.6 4.7 copy-start
  474.3 1.7 copy-start.1
  474.3 3.4 copy-start.3
Sparse Core Ops, SparseCore 0:
  191.1 101.8 reduce-scatter.1

commit v6 on v5

--- a/solution.py
+++ b/solution.py
@@ -134,8 +134,8 @@
 
 def head_kernel(
     experts, capacity, stride, half, part_half, seq_count, head_parts,
-    tokens_ref, norm_ref, weight_ref, bias_ref, seg_ref, live_ref, rows_ref, cot_ref, out_weight_ref,
-    first_hbm, qkv_hbm, context_hbm, total_hbm, out_full_ref, gathered_ref, ids_ref, cot_recv, own_send, own_tokens_ref,
+    tokens_ref, gain1_ref, bias1_ref, out_bias_ref, gain2_ref, bias2_ref, weight_ref, bias_ref, seg_ref, live_ref, rows_ref, cot_ref, out_weight_ref,
+    first_hbm, qkv_hbm, context_hbm, total_hbm, norm_ref, out_full_ref, gathered_ref, ids_ref, cot_recv, own_send, own_tokens_ref,
     cot_send, first_scr, qkv_scr, context_scr, total_scr,
     gather_sem, gather_out, cot_send_sem, cot_recv_sem, store_sem,
     weight_sem, weight_out, pair_send_sem, pair_recv_sem,
@@ -159,6 +159,9 @@
                 own_send[z, seq, :part] = wide
                 own_send[z, seq, part:] = tail
 
+    for row, vector in enumerate((gain1_ref, bias1_ref, out_bias_ref, gain2_ref, bias2_ref)):
+        norm_ref[row : row + 1] = vector[...].astype(F32).reshape(1, -1)
+    norm_ref[5:8] = jnp.zeros((3, norm_ref.shape[1]), F32)
     core = lax.rem(me, 2)
     weight_rows = out_weight_ref.shape[0]
     half_rows = weight_rows // 2
@@ -417,7 +420,7 @@
 
 
 def head(
-    tokens, vectors, flat_qkv, qv_bias, segments, live, rows, cotangent, out_weight,
+    tokens, norm_vectors, flat_qkv, qv_bias, segments, live, rows, cotangent, out_weight,
     experts, capacity, stride, half, part_half, head_parts,
 ):
     tok_count, model_width = tokens.shape
@@ -430,13 +433,14 @@
     slots = (experts, stride + half, LANES)
     return pl.pallas_call(
         partial(head_kernel, experts, capacity, stride, half, part_half, seq_count, head_parts),
-        in_specs=[whole()] * 9,
-        out_specs=[anywhere()] * 4 + [whole()] * 6,
+        in_specs=[whole()] * 13,
+        out_specs=[anywhere()] * 4 + [whole()] * 7,
         out_shape=[
             shaped((tok_count, model_width), BF16),
             shaped((tok_count, wide), BF16),
             shaped((tok_count, width), BF16),
             shaped((tok_count, LANES), F32),
+            shaped((8, model_width), F32),
             shaped((head_parts * out_weight.shape[0], model_width), BF16),
             shaped((head_parts, seq_count, seqlen + seqlen // 2, LANES), BF16),
             shaped((8, tok_count), jnp.int32),
@@ -463,7 +467,7 @@
         compiler_params=params(collective_id=3, has_side_effects=True),
         cost_estimate=cost(6e10, 1e7),
         name="head",
-    )(tokens, vectors, flat_qkv, qv_bias, segments, live, rows, cotangent, out_weight)
+    )(tokens, *norm_vectors, flat_qkv, qv_bias, segments, live, rows, cotangent, out_weight)
 
 
 def gelu_parts(pre):
@@ -762,7 +766,7 @@
 def backward_kernel(
     experts, stride, half, head_parts, chunk,
     arrived_hbm, hidden_hbm, result_hbm, cot_hbm, gate_col_ref, ids_ref, up_ref, up_bias_ref, down_ref,
-    sums_ref, grad_up_ref, grad_up_bias_ref, grad_down_ref, grad_down_bias_ref,
+    sums_ref, route_ref, grad_up_ref, grad_up_bias_ref, grad_down_ref, grad_down_bias_ref,
     rows_scr, result_scr, cot_scr, cot_wide, result_wide, hidden_scr, pre_grad_scr, out_grad_scr,
     send_scr, recv_scr, gate_send, gate_recv, total_scr,
     load_sem, send_sem, recv_sem, gate_send_sem, gate_recv_sem,
@@ -903,7 +907,12 @@
         return carry
 
     lax.fori_loop(1, experts, receive, 0)
-    sums_ref[...] = total_scr[...].astype(BF16)
+    sums_ref[...] = total_scr[:, :model_width].astype(BF16)
+    parts, seqs, kinds, count = route_ref.shape
+    for seq in range(seqs):
+        for z in range(parts):
+            start = (seq * parts + z) * count
+            route_ref[z, seq] = total_scr[start : start + count, model_width:].T[:kinds]
 
     def finish(step, carry):
         for copy in copies(lax.rem(me + step, experts), step):
@@ -923,9 +932,10 @@
     return pl.pallas_call(
         partial(backward_kernel, experts, stride, half, head_parts, chunk),
         in_specs=[anywhere()] * 4 + [whole()] * 5,
-        out_specs=[whole()] * 5,
+        out_specs=[whole()] * 6,
         out_shape=[
-            shaped((tok_count, model_width + LANES), BF16),
+            shaped((tok_count, model_width), BF16),
+            shaped((head_parts, tok_count // chunk, round_up(experts, 8), chunk // head_parts), F32),
             shaped((model_width, inner), F32),
             shaped((8, inner), F32),
             shaped((inner, model_width), F32),
@@ -979,18 +989,18 @@
 
 def tail_kernel(
     experts, stride, half, part_half, seq_count, head_parts, gap,
-    sums_ref, id_cols_ref, gate_cols_ref, own_residual_ref, own_second_ref, cot_own_hbm,
+    sums_ref, route_hbm, id_cols_ref, gate_cols_ref, own_residual_ref, own_second_ref, cot_own_hbm,
     own_columns_hbm, router_ref, vectors_ref, own_tokens_ref, result_hbm,
     context_hbm, first_hbm, qkv_hbm, totals_hbm, weight_ref, out_weight_ref,
     seg_ref, live_ref,
     tokens_hbm, block_ref, qkv_sum_ref, out_sum_ref, bias_sum_ref, small_ref,
-    own_recv, cot_wide, columns_scr, part_two, down_one, up_one, down_two, up_two, own_scr,
+    route_recv, own_recv, cot_wide, columns_scr, part_two, down_one, up_one, down_two, up_two, own_scr,
     full_one, full_two, grad_scr,
     context_scr, first_scr, qkv_scr, totals_scr, back_scr, joined_scr,
     qkv_grad, out_grad, bias_grad, rows_acc, router_acc,
     result_home, result_wide,
     qkv_send, qkv_recv, qkv_all, out_send, out_recv, out_all, bias_recv, small_head, small_recv,
-    own_send_sem, own_recv_sem, columns_sem, load_sem, stage_sem, result_send_sem, result_recv_sem,
+    route_send_sem, route_recv_sem, own_send_sem, own_recv_sem, columns_sem, load_sem, stage_sem, result_send_sem, result_recv_sem,
     down_one_sem, up_one_sem, down_two_sem, up_two_sem, down_one_out, up_one_out, down_two_out, up_two_out,
     full_one_sem, full_two_sem, full_one_out, full_two_out,
     sum_send_sem, sum_recv_sem, all_send_sem, all_recv_sem,
@@ -1057,6 +1067,21 @@
             **to_head(target),
         )
 
+    def route_copy(step):
+        target = lax.rem(here + step, head_parts)
+        return pltpu.make_async_remote_copy(
+            src_ref=route_hbm.at[target],
+            dst_ref=route_recv.at[here],
+            send_sem=route_send_sem.at[step],
+            recv_sem=route_recv_sem.at[step],
+            **to_head(target),
+        )
+
+    for other in range(1, head_parts):
+        route_copy(other).start()
+    route_local = pltpu.make_async_copy(route_hbm.at[here], route_recv.at[here], columns_sem.at[2])
+    route_local.start()
+    route_local.wait()
     own_local = pltpu.make_async_copy(cot_own_hbm.at[here], own_recv.at[here], columns_sem.at[1])
     own_local.start()
     own_local.wait()
@@ -1120,19 +1145,19 @@
 
             up_copy(*up, seq, high).start()
 
-    def reduce_end(partial_ref, base, down, up, seq, columns):
+    def reduce_end(partial_ref, base, down, up, seq):
         own = pl.ds(pl.multiple_of(base + here * part, part), part)
-        own_scr[:, :columns] = partial_ref[own].astype(F32)
+        own_scr[...] = partial_ref[own].astype(F32)
 
         @pl.when(here < ends)
         def below():
             down_copy(*down, seq, here).wait_recv()
-            own_scr[:, :columns] += down[0][seq, here].astype(F32)
+            own_scr[...] += down[0][seq, here].astype(F32)
 
         @pl.when(here > 0)
         def above():
             up_copy(*up, seq, here).wait_recv()
-            own_scr[:, :columns] += up[0][seq, here - 1].astype(F32)
+            own_scr[...] += up[0][seq, here - 1].astype(F32)
 
     def reduce_drain(down, up, seq):
         for shard in range(ends):
@@ -1191,12 +1216,21 @@
         logits = jnp.where(lane < experts, dot(second, router_ref[...]), NEGATIVE)
         powers = jnp.exp(logits - jnp.max(logits, axis=1, keepdims=True))
         chances = powers / jnp.sum(powers, axis=1, keepdims=True)
-        route_grad = own_scr[:, model_width:]
+        @pl.when(seq == 0)
+        def routes():
+            for other in range(1, head_parts):
+                route_copy(other).wait_recv()
+
+        route = route_recv[0, seq]
+        for other in range(1, head_parts):
+            route = route + route_recv[other, seq]
+        blank = jnp.zeros((LANES - route.shape[0], part), F32)
+        route_grad = jnp.concatenate([route, blank], axis=0).T
         logit_grad = (
             chances * (route_grad - jnp.sum(chances * route_grad, axis=1, keepdims=True))
         ).astype(BF16)
         router_acc[...] += dot_first(second, logit_grad)
-        grad = own_scr[:, :model_width] + dot_last(logit_grad, router_ref[...])
+        grad = own_scr[...] + dot_last(logit_grad, router_ref[...])
         normal, scale = standard(own_residual_ref[seq])
         rows_acc[0:1] += jnp.sum(grad * normal, axis=0, keepdims=True)
         rows_acc[1:2] += jnp.sum(grad, axis=0, keepdims=True)
@@ -1249,7 +1283,7 @@
                 copy.start()
 
     def last(seq):
-        grad = own_scr[:, :model_width]
+        grad = own_scr[...]
         normal, scale = standard(own_tokens_ref[seq].astype(F32))
         rows_acc[3:4] += jnp.sum(grad * normal, axis=0, keepdims=True)
         rows_acc[4:5] += jnp.sum(grad, axis=0, keepdims=True)
@@ -1467,7 +1501,7 @@
                 action(since // gap)
 
         def first_end(seq):
-            reduce_end(sums_ref, seq * seqlen, one_down, one_up, seq, model_width + LANES)
+            reduce_end(sums_ref, seq * seqlen, one_down, one_up, seq)
             middle(seq)
 
         def attend(seq):
@@ -1478,7 +1512,7 @@
             attend_end(seq)
 
         def second_end(seq):
-            reduce_end(part_two, lax.rem(seq, 2) * seqlen, two_down, two_up, seq, model_width)
+            reduce_end(part_two, lax.rem(seq, 2) * seqlen, two_down, two_up, seq)
             last(seq)
 
         def tokens_end(seq):
@@ -1565,6 +1599,7 @@
         spread_drain(two_full, seq)
     for other in range(1, head_parts):
         head_copy(other).wait_send()
+        route_copy(other).wait_send()
         for seq in range(seq_count):
             own_copy(seq, other).wait_send()
 
@@ -1581,7 +1616,7 @@
 
 
 def tail(
-    sums, id_cols, gate_cols, own_residual, own_second, cot_own, own_columns, router, vectors,
+    sums, route, id_cols, gate_cols, own_residual, own_second, cot_own, own_columns, router, vectors,
     own_tokens, result, context, first, qkv, totals, flat_qkv, out_weight,
     segments, live, stride, half, part_half, head_parts,
 ):
@@ -1597,7 +1632,7 @@
     dma = pltpu.SemaphoreType.DMA
     return pl.pallas_call(
         partial(tail_kernel, experts, stride, half, part_half, seq_count, head_parts, 2),
-        in_specs=[whole()] * 5 + [anywhere()] * 2 + [whole()] * 3 + [anywhere()] * 5 + [whole()] * 4,
+        in_specs=[whole(), anywhere()] + [whole()] * 4 + [anywhere()] * 2 + [whole()] * 3 + [anywhere()] * 5 + [whole()] * 4,
         out_specs=[anywhere()] + [whole()] * 5,
         out_shape=[
             shaped((tok_count, model_width), BF16),
@@ -1608,15 +1643,16 @@
             shaped((small_rows, model_width), F32),
         ],
         scratch_shapes=[
+            pltpu.VMEM(route.shape, F32),
             pltpu.VMEM(cot_own.shape, BF16),
             pltpu.VMEM((part, model_width), BF16),
             pltpu.VMEM((seqlen, width), F32),
             pltpu.VMEM((2 * seqlen, model_width), BF16),
-            pltpu.VMEM((seq_count, ends, part, model_width + LANES), BF16),
-            pltpu.VMEM((seq_count, ends, part, model_width + LANES), BF16),
             pltpu.VMEM((seq_count, ends, part, model_width), BF16),
             pltpu.VMEM((seq_count, ends, part, model_width), BF16),
-            pltpu.VMEM((part, model_width + LANES), F32),
+            pltpu.VMEM((seq_count, ends, part, model_width), BF16),
+            pltpu.VMEM((seq_count, ends, part, model_width), BF16),
+            pltpu.VMEM((part, model_width), F32),
             pltpu.VMEM((seq_count, seqlen, model_width), BF16),
             pltpu.VMEM((seq_count, seqlen, model_width), BF16),
             pltpu.VMEM((seq_count, part, model_width), F32),
@@ -1642,9 +1678,11 @@
             pltpu.VMEM((experts, 8, wide), F32),
             pltpu.VMEM((head_parts, small_rows, model_width), F32),
             pltpu.VMEM((experts, small_rows, model_width), F32),
+            dma((head_parts,)),
+            dma((head_parts,)),
             dma((seq_count, head_parts)),
             dma((seq_count, head_parts)),
-            dma((2,)),
+            dma((3,)),
             dma((4,)),
             dma((seq_count,)),
             dma((experts,)),
@@ -1661,7 +1699,7 @@
         cost_estimate=cost(1e11, 1e8),
         name="tail",
     )(
-        sums, id_cols, gate_cols, own_residual, own_second, cot_own, own_columns, router, vectors,
+        sums, route, id_cols, gate_cols, own_residual, own_second, cot_own, own_columns, router, vectors,
         own_tokens, result, context, first, qkv, totals, flat_qkv, out_weight,
         segments, live,
     )
@@ -1699,9 +1737,7 @@
     half = round_up(stride // 2, 16)
     local_width = qkv_weight.shape[2]
 
-    rows_of = [norm1_gain, norm1_bias, out_bias, norm2_gain, norm2_bias]
-    spare = jnp.zeros(((8 - len(rows_of)) * model_width,), BF16)
-    vectors = jnp.concatenate(rows_of + [spare]).astype(F32).reshape(8, model_width)
+    norm_vectors = [norm1_gain, norm1_bias, out_bias, norm2_gain, norm2_bias]
     flat_qkv = qkv_weight.reshape(model_width, 3 * local_width)
     router_wide = jnp.pad(router, ((0, 0), (0, LANES - experts)))
     up, down = up_weight[0], down_weight[0]
@@ -1716,8 +1752,8 @@
         axis=0,
     )
     part_half = round_up(seqlen // head_parts // 2, 16)
-    first, qkv, context, totals, out_full_weight, gathered, ids, cot_slots, cot_own, own_tokens = head(
-        tokens, vectors, flat_qkv, qv_bias, segments, live_mask, int_rows, cotangent, out_weight, experts, capacity, stride, half, part_half, head_parts,
+    first, qkv, context, totals, vectors, out_full_weight, gathered, ids, cot_slots, cot_own, own_tokens = head(
+        tokens, norm_vectors, flat_qkv, qv_bias, segments, live_mask, int_rows, cotangent, out_weight, experts, capacity, stride, half, part_half, head_parts,
     )
     id_cols = ids.T
     own_residual, own_second, own_columns, gates, arrived, hidden, result, gate_col, cot_rows = forward(
@@ -1726,7 +1762,7 @@
     )
     gate_cols = gates.T
     own_result = lax.psum_scatter(result, "head", scatter_dimension=0, tiled=True)[0]
-    sums, grad_up, grad_up_bias, grad_down, grad_down_bias = backward(
+    sums, route_terms, grad_up, grad_up_bias, grad_down, grad_down_bias = backward(
         arrived, hidden, result, cot_rows, gate_col, id_cols, up, up_bias, down, half, head_parts,
         seqlen,
     )
@@ -1734,7 +1770,7 @@
         (*copies_of(grad_up, grad_down), own_result)
     )
     grad_tokens, block_out, qkv_grad, out_grad, bias_grad, small = tail(
-        sums, id_cols, gate_cols, own_residual, own_second, cot_own, own_columns,
+        sums, route_terms, id_cols, gate_cols, own_residual, own_second, cot_own, own_columns,
         router_wide, vectors, own_tokens, own_result, context, first, qkv, totals,
         flat_qkv, out_weight, segments, live_mask, stride, half, part_half, head_parts,
     )

time: 493 us -> 482 us (0.978)
  Pallas kernels: 425 us -> 419 us
  local copies, waits for them, and re-layouts: 23.8 us -> 18.5 us
    pallas_call x1, Pallas kernels: 173 us -> 167 us  [tail(): pl.pallas_call(partial(tail_kernel, experts, stride, half, part_half, seq...]
  transfers between devices with their start and end apart: 1 -> 1, of which waited for: 1 -> 1; matrix products, arithmetic and copies ran while one was open for 1% -> 1% of each run, Pallas kernels for 16% -> 17%
where the time goes in v6:
time: 482 us; the launch traced here: 475 us
  Pallas kernels  419 us (87%)
  local copies, waits for them, and re-layouts  18.5 us (4%)
  waiting for transfers between devices  16.8 us (3%)
  between operations  14.3 us (3%)
  other arithmetic  5.96 us (1%)
    pallas_call x1, Pallas kernels, tail(): pl.pallas_call(partial(tail_kernel, experts, stride, half, part_half, seq...  167 us
    pallas_call x1, Pallas kernels, forward(): pl.pallas_call(partial(forward_kernel, experts, stride, half, seq_count,...  104 us
    pallas_call x1, Pallas kernels, backward(): pl.pallas_call(partial(backward_kernel, experts, stride, half, head_parts...  74.3 us
    pallas_call x1, Pallas kernels, head(): pl.pallas_call(partial(head_kernel, experts, capacity, stride, half, part...  68.5 us
    reduce_scatter x1, waiting for transfers between devices, body(): lax.psum_scatter(result, 'head', scatter_dimension=0, tiled=True)[0]  16.8 us
  transfers between devices with their start and end apart: 1, of which 1 were waited for; matrix products, arithmetic and copies ran while one was open for 1% of the time, Pallas kernels for 17%

profile of v6, /device:TPU:0, one launch (start us, length us, event | category | flops | bytes accessed | tf_op | source)
XLA Modules:
  0.0 474.7 jit_solution(11579997706070787685)
XLA Ops:
  7.3 2.3 copy.41.weight_ref
  9.5 0.8 reshape.40
  10.4 1.2 copy.42.cot_ref
  11.8 0.7 pad.4.router_ref
  12.5 0.7 add_add_fusion.rows_ref
  13.2 68.5 %head.1 = (bf16[1728,768]{1,0:T(8,128)(2,1)}, bf16[1728,576]{1,0:T(8,128)(2,1)}, bf16[1728,192]{1,0:T(8,128)(2,1)}, f32[1728,128]{1,0:T(8,128)}, f32[8,768]{1,0:...) custom-call(bf16[1728,768]{1,0:T(8,128)(2,1)} %tokens_ref.3, ...), custom_call_target="tpu_custom_call" | custom-call | flops 60000002048 | bytes 10000000 | tf_op jit(solution)/shard_map/head/pallas_call | solution.py:434
  81.7 104.1 %forward.1 = (f32[3,144,768]{2,1,0:T(8,128)}, bf16[3,144,768]{2,1,0:T(8,128)(2,1)}, f32[1728,192]{1,0:T(8,128)}, f32[8,1728]{1,0:T(8,128)}, bf16[8,464,768]{2,1,...) custom-call(bf16[4,3,864,128]{3,2,1,0:T(8,128)(2,1)} %get-tuple-elem, ...), custom_call_target="tpu_custom_call" | custom-call | flops 80000000000 | bytes 100000000 | tf_op jit(solution)/shard_map/forward/pallas_call | solution.py:724
  185.8 0.8 copy-done.4
  186.6 1.2 copy.44
  187.8 1.3 copy.45
  189.1 74.3 %backward.1 = (bf16[1728,768]{1,0:T(8,128)(2,1)}, f32[4,3,8,144]{3,2,1,0:T(8,128)}, f32[768,768]{1,0:T(8,128)}, f32[8,768]{1,0:T(8,128)}, f32[768,768]{1,0:T(8,128)}, /*index=5*/f32[8,768]{1,0:T(8,128)}) custom-call(bf16[8,464,768]{2,1,0:T(8,128)(2,1)} %get-tuple-element.57.arrived_hbm, bf16[8,464,768]{2,1,0:T(8,128)(2,1)} %get-tuple-element.58.hidden_hbm, ...), custom_call_target="tpu_custom_call" | custom-call | flops 80000000000 | bytes 100000000 | tf_op jit(solution)/shard_map/backward/pallas_call | solution.py:932
  263.4 0.7 slice.39
  264.1 1.3 slice.38
  265.5 5.0 %copies.1 = (f32[768,768]{1,0:T(8,128)}, f32[768,768]{1,0:T(8,128)}) custom-call(f32[768,768]{1,0:T(8,128)} %get-tuple-element.70.first_ref, f32[768,768]{1,0:T(8,128)} %get-tuple-element.71.second_ref), custom_call_target="tpu_custom_call" | custom-call | bytes 10000000 | tf_op jit(solution)/shard_map/copies/pallas_call | solution.py:978
  270.4 0.6 constant_dynamic-slice_fusion
  271.1 16.8 %reduce-scatter.2.cloned.1.call-done = bf16[1,8,704,128]{3,2,1,0:T(8,128)(2,1)} async-done(((bf16[4,8,704,128]{3,2,1,0:T(8,128)(2,1)}), bf16[1,8,704,128]{3,2,1,0:T(8,128)(2,1)}) %reduce-scatter.2.cloned.1.call-update) | async-done | bytes 1441808 | tf_op jit(solution)/shard_map/reduce_scatter | solution.py:1764
  287.9 167.2 %tail.1 = (bf16[1728,768]{1,0:T(8,128)(2,1)}, bf16[1728,192]{1,0:T(8,128)(2,1)}, f32[768,576]{1,0:T(8,128)}, f32[192,768]{1,0:T(8,128)}, f32[8,576]{1,0:T(8,128)}, /*index=5*/f32[16,768]{1,0:T(8,128)}) custom-call(bf16[1728,768]{1,0:T(8,128)(2,1)} %get-tuple-element.62.sums_ref, f32[4,3,8,144]{3,2,1,0:T(8,128)} %get-tuple-element.63.route_hbm, ...), custom_call_target="tpu_custom_call" | custom-call | flops 99999997952 | bytes 100000000 | tf_op jit(solution)/shard_map/tail/pallas_call | solution.py:1633
  455.1 1.3 slice_bitcast_fusion
  456.4 1.6 slice_reduce_fusion
  458.0 0.7 fusion
  458.7 4.7 convert_element_type.5
  463.4 1.7 copy.47
  465.1 1.1 copy.48
  466.8 0.8 copy.50
  (23 shorter events, 0.9 us)
Async XLA Ops:
  7.2 3.2 copy-start.2
  7.2 4.4 copy-start.7
  7.2 5.3 %copy-start.6 = (s32[1728,2]{0,1:T(2,128)S(1)}, s32[1728,2]{0,1:T(2,128)}, u32[]{:S(2)}) copy-start(s32[1728,2]{0,1:T(2,128)} %param.22) | copy-start | bytes 41476
  7.2 5.3 %copy-start.8 = (s32[1,1728]{1,0:T(1,128)S(1)}, s32[1,1728]{1,0:T(1,128)}, u32[]{:S(2)}) copy-start(s32[1,1728]{1,0:T(1,128)} %param.23) | copy-start | bytes 20740
  7.2 280.7 %reduce-scatter.2.cloned.1.call-start = ((), (), s32[]{:S(2)}) async-start(), calls=%async_computation.1 | async-start | bytes 7208960 | tf_op jit(solution)/shard_map/reduce_scatter | solution.py:1764
  185.8 0.8 copy-start.4
  185.8 2.0 copy-start.5
  458.7 4.7 copy-start
  463.4 1.7 copy-start.1
  463.4 3.4 copy-start.3
Sparse Core Ops, SparseCore 0:
  186.0 101.8 reduce-scatter.1

commit v7 on v6

--- a/solution.py
+++ b/solution.py
@@ -134,9 +134,9 @@
 
 def head_kernel(
     experts, capacity, stride, half, part_half, seq_count, head_parts,
-    tokens_ref, gain1_ref, bias1_ref, out_bias_ref, gain2_ref, bias2_ref, weight_ref, bias_ref, seg_ref, live_ref, rows_ref, cot_ref, out_weight_ref,
-    first_hbm, qkv_hbm, context_hbm, total_hbm, norm_ref, out_full_ref, gathered_ref, ids_ref, cot_recv, own_send, own_tokens_ref,
-    cot_send, first_scr, qkv_scr, context_scr, total_scr,
+    tokens_ref, gain1_ref, bias1_ref, out_bias_ref, gain2_ref, bias2_ref, weight_ref, bias_ref, seg_ref, live_ref, routes_ref, prio_ref, cot_ref, out_weight_ref,
+    first_hbm, qkv_hbm, context_hbm, total_hbm, norm_ref, out_full_ref, gathered_ref, ids_ref, id_cols_ref, cot_recv, own_send, own_tokens_ref,
+    rows_scr, cot_send, first_scr, qkv_scr, context_scr, total_scr,
     gather_sem, gather_out, cot_send_sem, cot_recv_sem, store_sem,
     weight_sem, weight_out, pair_send_sem, pair_recv_sem,
 ):
@@ -150,18 +150,31 @@
     pl.semaphore_wait(barrier, experts - 1 + ends)
 
     def own_rows():
+        diagonal = diagonal_of(seqlen)
+        for start in range(0, tok_count, seqlen):
+            for pick in range(2):
+                row = ids_ref[pick : pick + 1, start : start + seqlen]
+                id_cols_ref[start : start + seqlen, pick : pick + 1] = as_column(
+                    row, diagonal
+                ).astype(jnp.int32)
         for seq in range(seq_count):
             own = pl.ds(pl.multiple_of(seq * seqlen + here * part, part), part)
             own_tokens_ref[seq] = tokens_ref[own]
             for z in range(head_parts):
                 start = seq * seqlen + z * part
-                wide, tail = pack_rows(cot_ref[start : start + part], part_half)
+                block = cot_ref[:, start : start + part].astype(F32).T.astype(BF16)
+                wide, tail = pack_rows(block, part_half)
                 own_send[z, seq, :part] = wide
                 own_send[z, seq, part:] = tail
 
     for row, vector in enumerate((gain1_ref, bias1_ref, out_bias_ref, gain2_ref, bias2_ref)):
         norm_ref[row : row + 1] = vector[...].astype(F32).reshape(1, -1)
     norm_ref[5:8] = jnp.zeros((3, norm_ref.shape[1]), F32)
+    rows_scr[0:2] = routes_ref[...]
+    rows_scr[3:4] = prio_ref[...]
+    rows_scr[4:8] = jnp.zeros((4, tok_count), jnp.int32)
+    for seq in range(seq_count):
+        rows_scr[2:3, seq * seqlen : (seq + 1) * seqlen] = live_ref[seq : seq + 1]
     core = lax.rem(me, 2)
     weight_rows = out_weight_ref.shape[0]
     half_rows = weight_rows // 2
@@ -306,16 +319,16 @@
         return first, second
 
     def tables():
-        rank_row = rows_ref[3:4].astype(F32)
+        rank_row = rows_scr[3:4].astype(F32)
         diagonal = diagonal_of(seqlen)
         counts = jnp.zeros((2 * experts, tok_count), F32)
         for start in range(0, tok_count, seqlen):
-            first, second = hot(rows_ref[:, start : start + seqlen])
+            first, second = hot(rows_scr[:, start : start + seqlen])
             rank_col = as_column(rank_row[:, start : start + seqlen], diagonal)
             earlier = jnp.where(rank_col < rank_row, 1.0, 0.0)
             both = jnp.concatenate([first, second], axis=0)
             counts = counts + dot(both.astype(BF16), earlier.astype(BF16))
-        first, second = hot(rows_ref[...])
+        first, second = hot(rows_scr[...])
         total = jnp.sum(first, axis=1, keepdims=True)
         places = [
             jnp.sum(first * counts[:experts], axis=0, keepdims=True),
@@ -323,9 +336,9 @@
         ]
         for pick in range(2):
             place = places[pick].astype(jnp.int32)
-            kept = (place < capacity) & (rows_ref[2:3] > 0)
+            kept = (place < capacity) & (rows_scr[2:3] > 0)
             ids_ref[pick : pick + 1] = jnp.where(
-                kept, rows_ref[pick : pick + 1] * stride + place, -1
+                kept, rows_scr[pick : pick + 1] * stride + place, -1
             )
         ids_ref[2:8] = jnp.full((6, tok_count), -1, jnp.int32)
 
@@ -342,7 +355,7 @@
     def fill(target):
         slots = target * stride + lax.broadcasted_iota(jnp.int32, (stride, 1), 0)
         hit = (ids_ref[0:1] == slots) | (ids_ref[1:2] == slots)
-        block = dot(jnp.where(hit, 1.0, 0.0).astype(BF16), cot_ref[...]).astype(BF16)
+        block = dot_last(jnp.where(hit, 1.0, 0.0).astype(BF16), cot_ref[...]).astype(BF16)
         return pack_rows(block, half)
 
     def dispatch():
@@ -420,7 +433,7 @@
 
 
 def head(
-    tokens, norm_vectors, flat_qkv, qv_bias, segments, live, rows, cotangent, out_weight,
+    tokens, norm_vectors, flat_qkv, qv_bias, segments, live, routes_t, priority, cotangent, out_weight,
     experts, capacity, stride, half, part_half, head_parts,
 ):
     tok_count, model_width = tokens.shape
@@ -433,8 +446,8 @@
     slots = (experts, stride + half, LANES)
     return pl.pallas_call(
         partial(head_kernel, experts, capacity, stride, half, part_half, seq_count, head_parts),
-        in_specs=[whole()] * 13,
-        out_specs=[anywhere()] * 4 + [whole()] * 7,
+        in_specs=[whole()] * 14,
+        out_specs=[anywhere()] * 4 + [whole()] * 8,
         out_shape=[
             shaped((tok_count, model_width), BF16),
             shaped((tok_count, wide), BF16),
@@ -444,11 +457,13 @@
             shaped((head_parts * out_weight.shape[0], model_width), BF16),
             shaped((head_parts, seq_count, seqlen + seqlen // 2, LANES), BF16),
             shaped((8, tok_count), jnp.int32),
+            shaped((tok_count, 8), jnp.int32),
             shaped(slots, BF16),
             shaped(own, BF16),
             shaped((seq_count, part, model_width), BF16),
         ],
         scratch_shapes=[
+            pltpu.VMEM((8, tok_count), jnp.int32),
             pltpu.VMEM(slots, BF16),
             pltpu.VMEM((2, seqlen, model_width), BF16),
             pltpu.VMEM((2, seqlen, wide), BF16),
@@ -467,7 +482,7 @@
         compiler_params=params(collective_id=3, has_side_effects=True),
         cost_estimate=cost(6e10, 1e7),
         name="head",
-    )(tokens, *norm_vectors, flat_qkv, qv_bias, segments, live, rows, cotangent, out_weight)
+    )(tokens, *norm_vectors, flat_qkv, qv_bias, segments, live, routes_t, priority, cotangent, out_weight)
 
 
 def gelu_parts(pre):
@@ -485,8 +500,8 @@
     experts, stride, half, seq_count, head_parts,
     gathered_ref, tokens_ref, vectors_ref, out_weight_ref, router_ref, rows_ref, ids_ref,
     up_ref, up_bias_ref, down_ref, down_bias_ref, cot_hbm,
-    own_residual_ref, own_second_ref, own_columns_ref, gates_ref, arrived_hbm, hidden_hbm, result_hbm,
-    gate_col_ref, cot_all, arrived_ref, hidden_scr, result_scr, residual_ref, context_scr, second_scr, logit_scr, send_scr, gate_send, gate_recv,
+    own_residual_ref, own_second_ref, own_columns_ref, gate_cols_ref, arrived_hbm, hidden_hbm, result_hbm,
+    gate_col_ref, cot_all, gates_ref, arrived_ref, hidden_scr, result_scr, residual_ref, context_scr, second_scr, logit_scr, send_scr, gate_send, gate_recv,
     send_sem, recv_sem, gate_send_sem, gate_recv_sem, cot_sem, cot_out, local_sem,
     arrived_sem, store_sem,
 ):
@@ -664,6 +679,12 @@
         for copy in stores(step):
             copy.start()
 
+    diagonal = diagonal_of(seqlen)
+    for start in range(0, tok_count, seqlen):
+        for pick in range(2):
+            gate_cols_ref[start : start + seqlen, pick : pick + 1] = as_column(
+                gates_ref[pick : pick + 1, start : start + seqlen], diagonal
+            )
     work(0)
     moves = [(hop, piece) for hop in range(1, ends) for piece in range(pieces)]
     early = len(moves) - min(experts - 2, len(moves))
@@ -729,7 +750,7 @@
             shaped((seq_count, part, model_width), F32),
             shaped((seq_count, part, model_width), BF16),
             shaped((tok_count, model_width // head_parts), F32),
-            shaped((8, tok_count), F32),
+            shaped((tok_count, 8), F32),
             shaped((experts, stride, model_width), BF16),
             shaped((experts, stride, up.shape[1]), BF16),
             shaped((head_parts, experts, stride + half, LANES), BF16),
@@ -737,6 +758,7 @@
             shaped((head_parts, experts, stride + half, LANES), BF16),
         ],
         scratch_shapes=[
+            pltpu.VMEM((8, tok_count), F32),
             pltpu.VMEM((experts, stride, model_width), BF16),
             pltpu.VMEM((2, stride, up.shape[1]), BF16),
             pltpu.VMEM((2, head_parts, stride + half, LANES), BF16),
@@ -985,6 +1007,24 @@
         cost_estimate=cost(0, 1e7),
         name="copies",
     )(first, second)
+
+
+def widen_kernel(rows_ref, out_ref):
+    out_ref[...] = rows_ref[...].astype(F32)
+
+
+def widened(rows):
+    spec = pl.BlockSpec((rows.shape[0] // 4, rows.shape[1]), lambda i: (i, 0))
+    return pl.pallas_call(
+        widen_kernel,
+        grid=(4,),
+        in_specs=[spec],
+        out_specs=spec,
+        out_shape=shaped(rows.shape, F32),
+        compiler_params=params(),
+        cost_estimate=cost(0, 8e6),
+        name="widen",
+    )(rows)
 
 
 def tail_kernel(
@@ -1742,25 +1782,15 @@
     router_wide = jnp.pad(router, ((0, 0), (0, LANES - experts)))
     up, down = up_weight[0], down_weight[0]
 
-    int_rows = jnp.concatenate(
-        [
-            routes.T,
-            live_mask.reshape(1, tok_count),
-            priority,
-            jnp.zeros((4, tok_count), jnp.int32),
-        ],
-        axis=0,
+    routes_t = routes.T
+    part_half = round_up(seqlen // head_parts // 2, 16)
+    first, qkv, context, totals, vectors, out_full_weight, gathered, ids, id_cols, cot_slots, cot_own, own_tokens = head(
+        tokens, norm_vectors, flat_qkv, qv_bias, segments, live_mask, routes_t, priority, cotangent.T, out_weight, experts, capacity, stride, half, part_half, head_parts,
     )
-    part_half = round_up(seqlen // head_parts // 2, 16)
-    first, qkv, context, totals, vectors, out_full_weight, gathered, ids, cot_slots, cot_own, own_tokens = head(
-        tokens, norm_vectors, flat_qkv, qv_bias, segments, live_mask, int_rows, cotangent, out_weight, experts, capacity, stride, half, part_half, head_parts,
-    )
-    id_cols = ids.T
-    own_residual, own_second, own_columns, gates, arrived, hidden, result, gate_col, cot_rows = forward(
-        gathered, tokens, vectors, out_full_weight, router_wide, int_rows, ids,
+    own_residual, own_second, own_columns, gate_cols, arrived, hidden, result, gate_col, cot_rows = forward(
+        gathered, tokens, vectors, out_full_weight, router_wide, routes_t, ids,
         up, up_bias, down, down_bias, cot_slots, experts, stride, half, seq_count, head_parts,
     )
-    gate_cols = gates.T
     own_result = lax.psum_scatter(result, "head", scatter_dimension=0, tiled=True)[0]
     sums, route_terms, grad_up, grad_up_bias, grad_down, grad_down_bias = backward(
         arrived, hidden, result, cot_rows, gate_col, id_cols, up, up_bias, down, half, head_parts,
@@ -1779,7 +1809,7 @@
     )
     return (
         block_out,
-        grad_tokens.astype(F32),
+        widened(grad_tokens),
         small[3],
         small[4],
         qkv_grad.reshape(model_width, 3, local_width),

time: 482 us -> 481 us (level)
  other arithmetic: 5.96 us -> 0.58 us
  Pallas kernels: 419 us -> 424 us
where the time goes in v7:
time: 481 us; the launch traced here: 473 us
  Pallas kernels  424 us (88%)
  waiting for transfers between devices  20.7 us (4%)
  between operations  14.3 us (3%)
  local copies, waits for them, and re-layouts  13.8 us (3%)
    pallas_call x1, Pallas kernels, tail(): pl.pallas_call(partial(tail_kernel, experts, stride, half, part_half, seq...  167 us
    pallas_call x1, Pallas kernels, forward(): pl.pallas_call(partial(forward_kernel, experts, stride, half, seq_count,...  104 us
    pallas_call x1, Pallas kernels, backward(): pl.pallas_call(partial(backward_kernel, experts, stride, half, head_parts...  73.7 us
    pallas_call x1, Pallas kernels, head(): pl.pallas_call(partial(head_kernel, experts, capacity, stride, half, part...  68.6 us
    reduce_scatter x1, waiting for transfers between devices, body(): lax.psum_scatter(result, 'head', scatter_dimension=0, tiled=True)[0]  20.7 us
  transfers between devices with their start and end apart: 1, of which 1 were waited for; matrix products, arithmetic and copies ran while one was open for 1% of the time, Pallas kernels for 17%

profile of v7, /device:TPU:0, one launch (start us, length us, event | category | flops | bytes accessed | tf_op | source)
XLA Modules:
  0.0 473.0 jit_solution(12739534094783282361)
XLA Ops:
  7.2 0.0 reduce-scatter.2.cloned.1.call-start
  7.2 2.2 copy.38.weight_ref
  9.4 0.9 copy.39
  10.3 0.7 pad.4.router_ref
  11.1 68.6 %head.1 = (bf16[1728,768]{1,0:T(8,128)(2,1)}, bf16[1728,576]{1,0:T(8,128)(2,1)}, bf16[1728,192]{1,0:T(8,128)(2,1)}, f32[1728,128]{1,0:T(8,128)}, f32[8,768]{1,0:...) custom-call(bf16[1728,768]{1,0:T(8,128)(2,1)} %tokens_ref.3, ...), custom_call_target="tpu_custom_call" | custom-call | flops 60000002048 | bytes 10000000 | tf_op jit(solution)/shard_map/head/pallas_call | solution.py:447
  79.7 104.3 %forward.1 = (f32[3,144,768]{2,1,0:T(8,128)}, bf16[3,144,768]{2,1,0:T(8,128)(2,1)}, f32[1728,192]{1,0:T(8,128)}, f32[1728,8]{1,0:T(8,128)}, bf16[8,464,768]{2,1,...) custom-call(bf16[4,3,864,128]{3,2,1,0:T(8,128)(2,1)} %get-tuple-elem, ...), custom_call_target="tpu_custom_call" | custom-call | flops 80000000000 | bytes 100000000 | tf_op jit(solution)/shard_map/forward/pallas_call | solution.py:745
  184.0 0.0 reduce-scatter.2.cloned.1.call-update
  184.1 73.7 %backward.1 = (bf16[1728,768]{1,0:T(8,128)(2,1)}, f32[4,3,8,144]{3,2,1,0:T(8,128)}, f32[768,768]{1,0:T(8,128)}, f32[8,768]{1,0:T(8,128)}, f32[768,768]{1,0:T(8,128)}, /*index=5*/f32[8,768]{1,0:T(8,128)}) custom-call(bf16[8,464,768]{2,1,0:T(8,128)(2,1)} %get-tuple-element.58.arrived_hbm, bf16[8,464,768]{2,1,0:T(8,128)(2,1)} %get-tuple-element.59.hidden_hbm, ...), custom_call_target="tpu_custom_call" | custom-call | flops 80000000000 | bytes 100000000 | tf_op jit(solution)/shard_map/backward/pallas_call | solution.py:954
  257.8 0.7 slice.39
  258.5 1.3 slice.38
  259.8 5.0 %copies.1 = (f32[768,768]{1,0:T(8,128)}, f32[768,768]{1,0:T(8,128)}) custom-call(f32[768,768]{1,0:T(8,128)} %get-tuple-element.72.first_ref, f32[768,768]{1,0:T(8,128)} %get-tuple-element.73.second_ref), custom_call_target="tpu_custom_call" | custom-call | bytes 10000000 | tf_op jit(solution)/shard_map/copies/pallas_call | solution.py:1000
  264.8 0.6 constant_dynamic-slice_fusion
  265.5 20.7 %reduce-scatter.2.cloned.1.call-done = bf16[1,8,704,128]{3,2,1,0:T(8,128)(2,1)} async-done(((bf16[4,8,704,128]{3,2,1,0:T(8,128)(2,1)}), bf16[1,8,704,128]{3,2,1,0:T(8,128)(2,1)}) %reduce-scatter.2.cloned.1.call-update) | async-done | bytes 1441808 | tf_op jit(solution)/shard_map/reduce_scatter | solution.py:1794
  286.2 167.2 %tail.1 = (bf16[1728,768]{1,0:T(8,128)(2,1)}, bf16[1728,192]{1,0:T(8,128)(2,1)}, f32[768,576]{1,0:T(8,128)}, f32[192,768]{1,0:T(8,128)}, f32[8,576]{1,0:T(8,128)}, /*index=5*/f32[16,768]{1,0:T(8,128)}) custom-call(bf16[1728,768]{1,0:T(8,128)(2,1)} %get-tuple-element.64.sums_ref, f32[4,3,8,144]{3,2,1,0:T(8,128)} %get-tuple-element.65.route_hbm, ...), custom_call_target="tpu_custom_call" | custom-call | flops 99999997952 | bytes 100000000 | tf_op jit(solution)/shard_map/tail/pallas_call | solution.py:1673
  453.3 1.3 slice_bitcast_fusion
  454.7 1.6 slice_reduce_fusion
  456.2 0.7 fusion
  457.0 4.7 %widen.1 = f32[1728,768]{1,0:T(8,128)} custom-call(bf16[1728,768]{1,0:T(8,128)(2,1)} %get-tuple-element.82.rows_ref), custom_call_target="tpu_custom_call" | custom-call | bytes 8000000 | tf_op jit(solution)/shard_map/widen/pallas_call | solution.py:1018
  461.7 0.0 copy-done
  461.7 1.7 copy.41
  463.4 0.0 copy-done.1
  463.4 1.1 copy.42
  464.6 0.6 pad_maximum_fusion
  465.1 0.8 copy.44
  (4 shorter events, 0.0 us)
Async XLA Ops:
  7.2 279.0 %reduce-scatter.2.cloned.1.call-start = ((), (), s32[]{:S(2)}) async-start(), calls=%async_computation.1 | async-start | bytes 7208960 | tf_op jit(solution)/shard_map/reduce_scatter | solution.py:1794
  457.0 4.7 %copy-start = (f32[768,576]{1,0:T(8,128)S(1)}, f32[768,576]{1,0:T(8,128)}, u32[]{:S(2)}) copy-start(f32[768,576]{1,0:T(8,128)} %get-tuple-element.84) | copy-start | bytes 5308420
  461.7 1.7 copy-start.1
  461.7 3.4 copy-start.2
Sparse Core Ops, SparseCore 0:
  184.2 101.9 reduce-scatter.1

commit v8 on v7

--- a/solution.py
+++ b/solution.py
@@ -1121,10 +1121,8 @@
         route_copy(other).start()
     route_local = pltpu.make_async_copy(route_hbm.at[here], route_recv.at[here], columns_sem.at[2])
     route_local.start()
-    route_local.wait()
-    own_local = pltpu.make_async_copy(cot_own_hbm.at[here], own_recv.at[here], columns_sem.at[1])
+    own_local = pltpu.make_async_copy(cot_own_hbm.at[here], own_recv.at[here], columns_sem.at[3])
     own_local.start()
-    own_local.wait()
 
     def down_copy(buffer, sems, outs, seq, shard):
         return pltpu.make_async_remote_copy(
@@ -1258,6 +1256,8 @@
         chances = powers / jnp.sum(powers, axis=1, keepdims=True)
         @pl.when(seq == 0)
         def routes():
+            route_local.wait()
+            own_local.wait()
             for other in range(1, head_parts):
                 route_copy(other).wait_recv()
 
@@ -1722,7 +1722,7 @@
             dma((head_parts,)),
             dma((seq_count, head_parts)),
             dma((seq_count, head_parts)),
-            dma((3,)),
+            dma((4,)),
             dma((4,)),
             dma((seq_count,)),
             dma((experts,)),

time: 481 us -> 480 us (level)
  no operation moved by 1% of the time
where the time goes in v8:
time: 480 us; the launch traced here: 473 us
  Pallas kernels  423 us (88%)
  waiting for transfers between devices  20.7 us (4%)
  between operations  14.3 us (3%)
  local copies, waits for them, and re-layouts  13.8 us (3%)
    pallas_call x1, Pallas kernels, tail(): pl.pallas_call(partial(tail_kernel, experts, stride, half, part_half, seq...  167 us
    pallas_call x1, Pallas kernels, forward(): pl.pallas_call(partial(forward_kernel, experts, stride, half, seq_count,...  104 us
    pallas_call x1, Pallas kernels, backward(): pl.pallas_call(partial(backward_kernel, experts, stride, half, head_parts...  73.7 us
    pallas_call x1, Pallas kernels, head(): pl.pallas_call(partial(head_kernel, experts, capacity, stride, half, part...  68.6 us
    reduce_scatter x1, waiting for transfers between devices, body(): lax.psum_scatter(result, 'head', scatter_dimension=0, tiled=True)[0]  20.7 us
  transfers between devices with their start and end apart: 1, of which 1 were waited for; matrix products, arithmetic and copies ran while one was open for 1% of the time, Pallas kernels for 17%

profile of v8, /device:TPU:0, one launch (start us, length us, event | category | flops | bytes accessed | tf_op | source)
XLA Modules:
  0.0 472.7 jit_solution(14744754309792204730)
XLA Ops:
  7.2 0.0 reduce-scatter.2.cloned.1.call-start
  7.2 2.2 copy.38.weight_ref
  9.4 0.9 copy.39
  10.3 0.7 pad.4.router_ref
  11.1 68.6 %head.1 = (bf16[1728,768]{1,0:T(8,128)(2,1)}, bf16[1728,576]{1,0:T(8,128)(2,1)}, bf16[1728,192]{1,0:T(8,128)(2,1)}, f32[1728,128]{1,0:T(8,128)}, f32[8,768]{1,0:...) custom-call(bf16[1728,768]{1,0:T(8,128)(2,1)} %tokens_ref.3, ...), custom_call_target="tpu_custom_call" | custom-call | flops 60000002048 | bytes 10000000 | tf_op jit(solution)/shard_map/head/pallas_call | solution.py:447
  79.7 104.3 %forward.1 = (f32[3,144,768]{2,1,0:T(8,128)}, bf16[3,144,768]{2,1,0:T(8,128)(2,1)}, f32[1728,192]{1,0:T(8,128)}, f32[1728,8]{1,0:T(8,128)}, bf16[8,464,768]{2,1,...) custom-call(bf16[4,3,864,128]{3,2,1,0:T(8,128)(2,1)} %get-tuple-elem, ...), custom_call_target="tpu_custom_call" | custom-call | flops 80000000000 | bytes 100000000 | tf_op jit(solution)/shard_map/forward/pallas_call | solution.py:745
  184.0 0.0 reduce-scatter.2.cloned.1.call-update
  184.1 73.7 %backward.1 = (bf16[1728,768]{1,0:T(8,128)(2,1)}, f32[4,3,8,144]{3,2,1,0:T(8,128)}, f32[768,768]{1,0:T(8,128)}, f32[8,768]{1,0:T(8,128)}, f32[768,768]{1,0:T(8,128)}, /*index=5*/f32[8,768]{1,0:T(8,128)}) custom-call(bf16[8,464,768]{2,1,0:T(8,128)(2,1)} %get-tuple-element.58.arrived_hbm, bf16[8,464,768]{2,1,0:T(8,128)(2,1)} %get-tuple-element.59.hidden_hbm, ...), custom_call_target="tpu_custom_call" | custom-call | flops 80000000000 | bytes 100000000 | tf_op jit(solution)/shard_map/backward/pallas_call | solution.py:954
  257.8 0.7 slice.39
  258.5 1.3 slice.38
  259.8 5.0 %copies.1 = (f32[768,768]{1,0:T(8,128)}, f32[768,768]{1,0:T(8,128)}) custom-call(f32[768,768]{1,0:T(8,128)} %get-tuple-element.72.first_ref, f32[768,768]{1,0:T(8,128)} %get-tuple-element.73.second_ref), custom_call_target="tpu_custom_call" | custom-call | bytes 10000000 | tf_op jit(solution)/shard_map/copies/pallas_call | solution.py:1000
  264.8 0.6 constant_dynamic-slice_fusion
  265.5 20.7 %reduce-scatter.2.cloned.1.call-done = bf16[1,8,704,128]{3,2,1,0:T(8,128)(2,1)} async-done(((bf16[4,8,704,128]{3,2,1,0:T(8,128)(2,1)}), bf16[1,8,704,128]{3,2,1,0:T(8,128)(2,1)}) %reduce-scatter.2.cloned.1.call-update) | async-done | bytes 1441808 | tf_op jit(solution)/shard_map/reduce_scatter | solution.py:1794
  286.2 166.9 %tail.1 = (bf16[1728,768]{1,0:T(8,128)(2,1)}, bf16[1728,192]{1,0:T(8,128)(2,1)}, f32[768,576]{1,0:T(8,128)}, f32[192,768]{1,0:T(8,128)}, f32[8,576]{1,0:T(8,128)}, /*index=5*/f32[16,768]{1,0:T(8,128)}) custom-call(bf16[1728,768]{1,0:T(8,128)(2,1)} %get-tuple-element.64.sums_ref, f32[4,3,8,144]{3,2,1,0:T(8,128)} %get-tuple-element.65.route_hbm, ...), custom_call_target="tpu_custom_call" | custom-call | flops 99999997952 | bytes 100000000 | tf_op jit(solution)/shard_map/tail/pallas_call | solution.py:1673
  453.1 1.3 slice_bitcast_fusion
  454.4 1.6 slice_reduce_fusion
  456.0 0.7 fusion
  456.7 4.7 %widen.1 = f32[1728,768]{1,0:T(8,128)} custom-call(bf16[1728,768]{1,0:T(8,128)(2,1)} %get-tuple-element.82.rows_ref), custom_call_target="tpu_custom_call" | custom-call | bytes 8000000 | tf_op jit(solution)/shard_map/widen/pallas_call | solution.py:1018
  461.4 0.0 copy-done
  461.4 1.7 copy.41
  463.2 1.1 copy.42
  464.3 0.6 pad_maximum_fusion
  464.9 0.0 copy-done.2
  464.9 0.8 copy.44
  (4 shorter events, 0.0 us)
Async XLA Ops:
  7.2 279.0 %reduce-scatter.2.cloned.1.call-start = ((), (), s32[]{:S(2)}) async-start(), calls=%async_computation.1 | async-start | bytes 7208960 | tf_op jit(solution)/shard_map/reduce_scatter | solution.py:1794
  456.7 4.7 %copy-start = (f32[768,576]{1,0:T(8,128)S(1)}, f32[768,576]{1,0:T(8,128)}, u32[]{:S(2)}) copy-start(f32[768,576]{1,0:T(8,128)} %get-tuple-element.84) | copy-start | bytes 5308420
  461.4 1.7 copy-start.1
  461.4 3.4 copy-start.2
Sparse Core Ops, SparseCore 0:
  184.2 101.9 reduce-scatter.1
